TPU v7x, 256 devices: a whole 4x4x8 slice. The times are simulated.
256 devices in a mesh: dp: 8 (over z), seq: 32 (over x, y, core).
Axes of the slice: x: 4, y: 4, z: 8, core: 2. Of those that a mesh axis runs over, the one named last changes fastest.
Arguments:
- queries: bfloat16 [8, 4096, 2048], P('dp', 'seq'), may hold values from -6 to 6
- keys: bfloat16 [8, 4096, 2048], P('dp', 'seq'), may hold values from -6 to 6
- values: bfloat16 [8, 4096, 2048], P('dp', 'seq'), may hold values from -6 to 6
- out_grad: bfloat16 [8, 4096, 2048], P('dp', 'seq'), may hold values from -6 to 6
- out_weight: bfloat16 [2048, 2048], P(('dp', 'seq')), may hold values from -0.125 to 0.125
Outputs:
- query_grad: bfloat16 [8, 4096, 2048], P('dp', 'seq')
- key_grad: bfloat16 [8, 4096, 2048], P('dp', 'seq')
- value_grad: bfloat16 [8, 4096, 2048], P('dp', 'seq')
- weight_grad: float32 [2048, 2048], P(('dp', 'seq'))
All inputs are finite; a program needn't handle non-finite values.
Results may differ from a plain program's by a relative error of at most 0.011.
Values may be sent and summed in bfloat16 or wider, within the bound.
No kernel may reach another device: no remote copies, remote signals or barrier semaphores. Data moves between devices by JAX's collectives and lax.ppermute only.
A program may use at most 192 MiB of HBM per device.

v0:
```python
import jax
import jax.numpy as jnp
from jax import lax
from jax.sharding import PartitionSpec as P

DH = 128


def carried_in(value, axis, join, neutral, backward):
    count, mine = (lax.axis_size(axis), lax.axis_index(axis))
    pieces = jax.tree.map(lambda part: lax.all_gather(part, axis), value)
    if backward:
        pieces = jax.tree.map(lambda part: part[::-1], pieces)
        mine = count - 1 - mine
    so_far = jax.tree.map(
        lambda part, zero: jnp.full_like(part, 0) + jnp.asarray(zero, part.dtype), value, neutral
    )

    def lap(position, so_far):
        longer = join(so_far, jax.tree.map(lambda part: part[position], pieces))
        return jax.tree.map(lambda new, old: jnp.where(position < mine, new, old), longer, so_far)

    return lax.fori_loop(0, count - 1, lap, so_far)


def feature(values_in):
    return jnp.where(values_in > 0, values_in + 1.0, jnp.exp(jnp.minimum(values_in, 0.0)))


def feature_slope(values_in):
    return jnp.where(values_in > 0, 1.0, jnp.exp(jnp.minimum(values_in, 0.0)))


def mix_sum(form, left, right):
    return jnp.einsum(form, left, right, precision=lax.Precision.HIGHEST)


def low_sum(form, left, right):
    return jnp.einsum(form, left, right, preferred_element_type=jnp.float32)


def add_pair(earlier, later):
    return jax.tree.map(jnp.add, earlier, later)


def on_device(queries, keys, values, out_grad, out_weight):
    seq_count, tok_rows, head_width = queries.shape
    head_count = head_width // DH
    block_shape = (seq_count, tok_rows, head_count, DH)
    q_raw = queries.astype(jnp.float32).reshape(block_shape)
    k_raw = keys.astype(jnp.float32).reshape(block_shape)
    q_feat = feature(q_raw).astype(jnp.bfloat16)
    k_feat = feature(k_raw).astype(jnp.bfloat16)
    q_wide = q_feat.astype(jnp.float32)
    k_wide = k_feat.astype(jnp.float32)
    v_full = values.reshape(block_shape)
    v_wide = v_full.astype(jnp.float32)
    positions = jnp.arange(tok_rows, dtype=jnp.int32)
    causal = (positions[:, None] >= positions[None, :]).astype(jnp.float32)
    scores = low_sum("bthd,bshd->bhts", q_feat, k_feat) * causal
    scores_low = scores.astype(jnp.bfloat16)
    zero_state = jnp.zeros((seq_count, head_count, DH, DH), jnp.float32)
    zero_norm = jnp.zeros((seq_count, head_count, DH), jnp.float32)
    state_local = low_sum("bshd,bshe->bhde", k_feat, v_full)
    norm_local = jnp.sum(k_wide, axis=1)
    attn_grad = jnp.einsum(
        "btd,rd->btr",
        out_grad,
        lax.all_gather(out_weight, ("dp", "seq"), axis=0, tiled=True),
        preferred_element_type=jnp.float32,
    ).reshape(block_shape)
    inner_sum = low_sum("bhts,bshe->bthe", scores_low, v_full)
    row_sums = jnp.transpose(jnp.sum(scores, axis=3), (0, 2, 1))
    state_in, norm_in = carried_in(
        (state_local, norm_local), "seq", add_pair, (zero_state, zero_norm), False
    )
    denoms = row_sums + mix_sum("bthd,bhd->bth", q_wide, norm_in)
    outputs = (inner_sum + mix_sum("bthd,bhde->bthe", q_wide, state_in)) / denoms[..., None]
    scaled = attn_grad / denoms[..., None]
    residue = -jnp.sum(scaled * outputs, axis=3)
    grad_local = mix_sum("bthd,bthe->bhde", q_wide, scaled)
    weight_local = mix_sum("bth,bthd->bhd", residue, q_wide)
    grad_state, grad_norm = carried_in(
        (grad_local, weight_local), "seq", add_pair, (zero_state, zero_norm), True
    )
    attended = outputs.reshape(seq_count, tok_rows, head_width).astype(jnp.bfloat16)
    weight_grad = lax.psum_scatter(
        jnp.einsum("btr,btd->rd", attended, out_grad, preferred_element_type=jnp.float32),
        ("dp", "seq"),
        scatter_dimension=0,
        tiled=True,
    )
    scaled_low = scaled.astype(jnp.bfloat16)
    mixed_w = (
        (
            low_sum("bthe,bshe->bhts", scaled_low, v_full)
            + jnp.transpose(residue, (0, 2, 1))[..., None]
        )
        * causal
    ).astype(jnp.bfloat16)
    q_grad = (
        low_sum("bhts,bshd->bthd", mixed_w, k_feat)
        + mix_sum("bthe,bhde->bthd", scaled, state_in)
        + residue[..., None] * norm_in[:, None]
    )
    k_grad = (
        low_sum("bhts,bthd->bshd", mixed_w, q_feat)
        + mix_sum("bhde,bshe->bshd", grad_state, v_wide)
        + grad_norm[:, None]
    )
    v_grad = low_sum("bhts,bthe->bshe", scores_low, scaled_low) + mix_sum(
        "bhde,bshd->bshe", grad_state, k_wide
    )
    query_grad = (
        (q_grad * feature_slope(q_raw))
        .reshape(seq_count, tok_rows, head_width)
        .astype(jnp.bfloat16)
    )
    key_grad = (
        (k_grad * feature_slope(k_raw))
        .reshape(seq_count, tok_rows, head_width)
        .astype(jnp.bfloat16)
    )
    value_grad = v_grad.reshape(seq_count, tok_rows, head_width).astype(jnp.bfloat16)
    return (query_grad, key_grad, value_grad, weight_grad)


def solution(mesh):
    return jax.shard_map(
        on_device,
        mesh=mesh,
        in_specs=(
            P("dp", "seq", None),
            P("dp", "seq", None),
            P("dp", "seq", None),
            P("dp", "seq", None),
            P(("dp", "seq"), None),
        ),
        out_specs=(
            P("dp", "seq", None),
            P("dp", "seq", None),
            P("dp", "seq", None),
            P(("dp", "seq"), None),
        ),
        check_vma=False,
    )
```

profile of v0, /device:TPU:1, one launch (start us, length us, event | category | flops | bytes accessed | tf_op | source)
XLA Modules:
  0.0 1679.0 jit_solution(3385762445193055043)
XLA Ops:
  7.2 2.4 fusion.17
  13.7 2.4 fusion.29
  16.7 26.5 %all_gather.31 = f32[32,1,16,128]{3,2,1,0:T(8,128)S(1)} all-gather(f32[1,1,16,128]{3,2,1,0:T(8,128)S(1)} %bitcast.180), channel_id=1, replica_groups=mesh['dp'=8,'seq'=32] {'seq'}, dimensions={0}, use_global_device_ids=true | all-gather | bytes 270336 | tf_op jit(solution)/shard_map/all_gather | solution.py:11
  44.5 92.1 %all-gather.9.cloned.1.call-done = f32[512,128,128]{2,1,0:T(8,128)} async-done(((f32[16,128,128]{2,1,0:T(8,128)}), f32[512,128,128]{2,1,0:T(8,128)}) %all-gather.9.cloned.1.call-update) | async-done | bytes 33554448 | tf_op jit(solution)/shard_map/all_gather | solution.py:11
  136.5 50.7 %while.32 = (s32[]{:T(128)}, f32[1,16,128,128]{3,2,1,0:T(8,128)S(1)}, f32[1,16,128]{2,1,0:T(8,128)S(1)}, s32[]{:T(128)}, f32[32,1,16,128,128]{4,3,2,1,0:T(8,128)...) while((s32[]{:T(128)}, f32[1,16,128,128]{3,2,1,0:T(8,128)S(1)}, ...), condition=%wide.region_3.4_spmd.clone, body=%wide.region_2.3_spmd.clone.sunk | while | flops 792580 | bytes 3170427 | solution.py:23
  151.2 1.6 add_select_fusion.8
  187.7 70.2 %all-gather.7.cloned.1.call-done = bf16[2048,2048]{1,0:T(8,128)(2,1)} async-done(((bf16[8,2048]{1,0:T(8,128)(2,1)}), bf16[2048,2048]{1,0:T(8,128)(2,1)}) %all-gather.7.cloned.1.call-update) | async-done | bytes 8388624 | tf_op jit(solution)/shard_map/all_gather | solution.py:69
  257.9 5.7 convolution_divide_fusion
  263.7 2.2 fusion.55
  266.1 2.0 fusion.25
  268.2 1.6 fusion.50
  269.8 8.9 fusion.31
  278.8 2.6 copy.53
  281.4 2.6 copy.60
  284.0 1.7 fusion.10
  287.9 3.8 fusion.11
  291.6 2.1 copy.64
  294.2 24.5 %all-gather.2 = f32[512,128]{1,0:T(8,128)S(1)} all-gather(f32[16,128]{1,0:T(8,128)S(1)} %bitcast.181), channel_id=4, replica_groups=mesh['dp'=8,'seq'=32] {'seq'}, dimensions={0}, use_global_device_ids=true | all-gather | bytes 270336 | tf_op jit(solution)/shard_map/all_gather | solution.py:11
  318.7 63.3 %all-gather.11.cloned.1.call-done = f32[512,128,128]{2,1,0:T(8,128)} async-done(((f32[16,128,128]{2,1,0:T(8,128)}), f32[512,128,128]{2,1,0:T(8,128)}) %all-gather.11.cloned.1.call-update) | async-done | bytes 33554448 | tf_op jit(solution)/shard_map/all_gather | solution.py:11
  382.0 23.1 %rev.6 = f32[32,1,16,128,128]{4,3,2,1,0:T(8,128)} reverse(f32[32,1,16,128,128]{4,3,2,1,0:T(8,128)} %bitcast.155), dimensions={0} | reverse | bytes 67108864 | tf_op jit(solution)/shard_map/rev | solution.py:13
  405.1 50.8 %while.33 = (s32[]{:T(128)}, f32[1,16,128,128]{3,2,1,0:T(8,128)S(1)}, f32[1,16,128]{2,1,0:T(8,128)S(1)}, s32[]{:T(128)}, f32[32,1,16,128,128]{4,3,2,1,0:T(8,128)...) while((s32[]{:T(128)}, f32[1,16,128,128]{3,2,1,0:T(8,128)S(1)}, ...), condition=%wide.region_6.7_spmd.clone, body=%wide.region_5.6_spmd.clone.sunk | while | flops 792580 | bytes 3170427 | solution.py:23
  405.1 1.7 add_select_fusion.10
  406.8 1.6 add_select_fusion.10
  415.0 1.6 add_select_fusion.10
  416.6 1.6 add_select_fusion.10
  424.8 1.6 add_select_fusion.10
  426.4 1.6 add_select_fusion.10
  455.9 2.3 convolution_bitcast_fusion.4
  458.1 2.7 fusion.13
  460.9 2.0 copy.65
  462.9 2.0 convolution_bitcast_fusion.3
  467.5 1205.0 %reduce-scatter.2.cloned.1.call-done = f32[8,2048]{1,0:T(8,128)} async-done(((f32[2048,2048]{1,0:T(8,128)}), f32[8,2048]{1,0:T(8,128)}) %reduce-scatter.2.cloned.1.call-update) | async-done | bytes 65552 | tf_op jit(solution)/shard_map/reduce_scatter | solution.py:87
  (165 shorter events, 100.1 us)
Async XLA Ops:
  7.2 250.8 %copy-start = (bf16[1,128,2048]{2,1,0:T(8,128)(2,1)S(1)}, bf16[1,128,2048]{2,1,0:T(8,128)(2,1)}, u32[]{:S(2)}) copy-start(bf16[1,128,2048]{2,1,0:T(8,128)(2,1)} %param.12) | copy-start | bytes 1572868
  7.2 129.3 %all-gather.9.cloned.1.call-start = ((), (), s32[]{:S(2)}) async-start(), calls=%async_computation.3 | async-start | bytes 34603008 | tf_op jit(solution)/shard_map/all_gather | solution.py:11
  9.8 248.2 %copy-start.7 = (bf16[16,8,16,128]{3,2,1,0:T(8,128)(2,1)}, bf16[16,8,16,128]{3,2,1,0:T(8,128)(2,1)S(1)}, u32[]{:S(2)}) copy-start(bf16[16,8,16,128]{3,2,1,0:T(8,128)(2,1)S(1)} %copy.81) | copy-start | bytes 1572868
  10.2 5.9 copy-start.9
  11.6 4.7 copy-start.6
  12.9 245.0 %all-gather.7.cloned.1.call-start = ((), (), s32[]{:S(2)}) async-start(), calls=%async_computation.1 | async-start | bytes 8421376 | tf_op jit(solution)/shard_map/all_gather | solution.py:69
  13.6 368.4 %all-gather.11.cloned.1.call-start = ((), (), s32[]{:S(2)}) async-start(), calls=%async_computation.4 | async-start | bytes 34603008 | tf_op jit(solution)/shard_map/all_gather | solution.py:11
  16.2 241.7 %copy-start.4 = (bf16[16,8,16,128]{3,2,1,0:T(8,128)(2,1)}, bf16[16,8,16,128]{3,2,1,0:T(8,128)(2,1)S(1)}, u32[]{:S(2)}) copy-start(bf16[16,8,16,128]{3,2,1,0:T(8,128)(2,1)S(1)} %copy.83) | copy-start | bytes 1572868
  263.7 15.1 copy-start.2
  265.9 1406.6 %reduce-scatter.2.cloned.1.call-start = ((), (), s32[]{:S(2)}) async-start(), calls=%async_computation.2 | async-start | bytes 16842752 | tf_op jit(solution)/shard_map/reduce_scatter | solution.py:87
  278.8 14.9 copy-start.5
  285.7 0.8 copy-start.8
  382.0 1290.5 %copy-start.1 = (bf16[1,128,2048]{2,1,0:T(8,128)(2,1)S(1)}, bf16[1,128,2048]{2,1,0:T(8,128)(2,1)}, u32[]{:S(2)}) copy-start(bf16[1,128,2048]{2,1,0:T(8,128)(2,1)} %param.12) | copy-start | bytes 1572868
  405.1 59.9 %copy-start.3 = (f32[128,16,128]{0,2,1:T(8,128)S(1)}, f32[128,16,128]{0,2,1:T(8,128)}, u32[]{:S(2)}) copy-start(f32[128,16,128]{0,2,1:T(8,128)} %copy-done.2) | copy-start | bytes 3145732
Sparse Core Ops, SparseCore 0:
  13.0 123.4 all-gather.8
  140.2 117.6 all-gather.6
  266.0 115.9 all-gather.10
  384.9 1287.5 reduce-scatter.1
where the time goes:
time: 1690 us; the launch traced here: 1680 us
  waiting for transfers between devices  1430 us (85%)
  other arithmetic  104 us (6%)
  blocking collectives  50.9 us (3%)
  matrix products  39.5 us (2%)
  local copies, waits for them, and re-layouts  36.7 us (2%)
    reduce_scatter x1, waiting for transfers between devices, on_device(): lax.psum_scatter(jnp.einsum('btr,btd->rd', attended, out_grad, preferred_...  1200 us
    all_gather x2, waiting for transfers between devices, carried_in(): pieces = jax.tree.map(lambda part: lax.all_gather(part, axis), value)  155 us
    select_n x124, other arithmetic, lap(): jnp.where(position < mine, new, old)  99.5 us
    all_gather x1, waiting for transfers between devices, on_device(): lax.all_gather(out_weight, ('dp', 'seq'), axis=0, tiled=True)  70.2 us
    all_gather x2, blocking collectives, carried_in(): pieces = jax.tree.map(lambda part: lax.all_gather(part, axis), value)  50.9 us
  transfers between devices with their start and end apart: 4, of which 4 were waited for; matrix products, arithmetic and copies ran while one was open for 10% of the time, Pallas kernels for 0%

commit v1 on v0

v1 whole, which is shorter than its diff:
```python
import functools

import jax
import jax.numpy as jnp
from jax import lax
from jax.experimental import pallas as pl
from jax.experimental.pallas import tpu as pltpu
from jax.sharding import Mesh, PartitionSpec as P

DH = 128
BLK = 128
BF = jnp.bfloat16
F32 = jnp.float32
NN = (((1,), (0,)), ((), ()))
NT = (((1,), (1,)), ((), ()))
TN = (((0,), (0,)), ((), ()))
HALF = DH // 2
ROWS = HALF + 8
PARAMS = pltpu.CompilerParams(vmem_limit_bytes=48 * 1024 * 1024)


def dot(left, right, dims):
    return lax.dot_general(left, right, dims, preferred_element_type=F32)


def split(wide):
    high = wide.astype(BF)
    return high, (wide - high.astype(F32)).astype(BF)


def feature(raw):
    return jnp.where(raw > 0, raw + 1.0, jnp.exp(jnp.minimum(raw, 0.0)))


def feature_slope(raw):
    return jnp.where(raw > 0, 1.0, jnp.exp(jnp.minimum(raw, 0.0)))


def features_of(raw):
    return feature(raw.astype(F32)).astype(BF)


def causal_mask():
    row = lax.broadcasted_iota(jnp.int32, (BLK, BLK), 0)
    col = lax.broadcasted_iota(jnp.int32, (BLK, BLK), 1)
    return row >= col


def state_of(ref):
    return jnp.concatenate([ref[0, :HALF], ref[1, :HALF]], axis=0), ref[0, HALF : HALF + 1]


def put_state(ref, matrix, vector):
    tail = jnp.broadcast_to(vector, (8, DH))
    for half in range(2):
        ref[half, :HALF] = matrix[half * HALF : (half + 1) * HALF]
        ref[half, HALF:] = tail


def call(body, grid, ins, outs, scratch=()):
    return pl.pallas_call(
        body,
        grid_spec=pltpu.PrefetchScalarGridSpec(
            num_scalar_prefetch=1,
            grid=grid,
            in_specs=[pl.BlockSpec(*spec) for spec in ins],
            out_specs=[pl.BlockSpec(spec[0], spec[1]) for spec in outs],
            scratch_shapes=list(scratch),
        ),
        out_shape=[jax.ShapeDtypeStruct(spec[2], spec[3]) for spec in outs],
        compiler_params=PARAMS,
    )


def pack_body(core, q_ref, k_ref, v_ref, out_ref):
    out_ref[0] = q_ref[...]
    out_ref[1] = k_ref[...]
    out_ref[2] = v_ref[...]


def grads_body(core, mine_ref, other_ref, out_ref):
    out_ref[core[0]] = mine_ref[...]
    out_ref[1 - core[0]] = other_ref[...]


def local_body(core, q_ref, k_ref, v_ref, other_ref, both_ref, sum_ref, first_ref):
    me = core[0]
    both_ref[0, me] = q_ref[...]
    both_ref[1, me] = k_ref[...]
    both_ref[2, me] = v_ref[...]
    for part in range(3):
        both_ref[part, 1 - me] = other_ref[part]
    total, total_norm = None, None
    for block in range(2):
        k_feat = features_of(both_ref[1, block])
        state = dot(k_feat, both_ref[2, block], TN)
        norm = jnp.sum(k_feat.astype(F32), axis=0, keepdims=True)
        if block == 0:
            put_state(first_ref, state, norm)
            total, total_norm = state, norm
        else:
            put_state(sum_ref, total + state, total_norm + norm)


def scan_body(backward, core, in_ref, out_ref):
    count = in_ref.shape[0]
    so_far = jnp.zeros(in_ref.shape[1:], F32)
    order = range(count - 1, -1, -1) if backward else range(count)
    for position in order:
        out_ref[position] = so_far
        so_far = so_far + in_ref[position]


def forward_body(core, both_ref, in_ref, first_ref, att_ref, o_ref, den_ref):
    causal = causal_mask()
    state, norm = state_of(in_ref)
    for block in range(2):
        if block == 1:
            extra, extra_norm = state_of(first_ref)
            state, norm = state + extra, norm + extra_norm
        q_feat = features_of(both_ref[0, block])
        k_feat = features_of(both_ref[1, block])
        scores = jnp.where(causal, dot(q_feat, k_feat, NT), 0.0)
        den = jnp.sum(scores, axis=1, keepdims=True) + jnp.sum(
            q_feat.astype(F32) * norm, axis=1, keepdims=True
        )
        high, low = split(state)
        out = (
            dot(scores.astype(BF), both_ref[2, block], NN)
            + dot(q_feat, high, NN)
            + dot(q_feat, low, NN)
        ) / den
        att_ref[0, block * BLK : (block + 1) * BLK] = out.astype(BF)
        o_ref[block] = out
        den_ref[block] = jnp.broadcast_to(den, (BLK, DH))


def scaled_body(
    core, w_ref, og_ref, ogr_ref, q_ref, o_ref, den_ref, g_ref, r_ref, sum_ref, last_ref
):
    me = core[0]
    g_ref[me] = dot(og_ref[...], w_ref[...], NT)
    g_ref[1 - me] = dot(ogr_ref[...], w_ref[...], NT)
    total, total_norm = None, None
    for block in range(2):
        scaled = g_ref[block] / den_ref[block]
        g_ref[block] = scaled
        residue = -jnp.sum(scaled * o_ref[block], axis=1, keepdims=True)
        r_ref[block] = jnp.broadcast_to(residue, (BLK, DH))
        q_feat = features_of(q_ref[0, block])
        high, low = split(scaled)
        state = dot(q_feat, high, TN) + dot(q_feat, low, TN)
        norm = jnp.sum(residue * q_feat.astype(F32), axis=0, keepdims=True)
        if block == 0:
            total, total_norm = state, norm
        else:
            put_state(last_ref, state, norm)
            put_state(sum_ref, total + state, total_norm + norm)


def backward_body(
    core,
    both_ref,
    in_ref,
    first_ref,
    g_ref,
    r_ref,
    later_ref,
    last_ref,
    keep_ref,
    send_ref,
    held,
):
    me = core[0]
    causal = causal_mask()
    state0, norm0 = state_of(in_ref)
    extra, extra_norm = state_of(first_ref)
    grad1, weight1 = state_of(later_ref)
    after, after_norm = state_of(last_ref)
    states = (state0, state0 + extra)
    norms = (norm0, norm0 + extra_norm)
    grads = (grad1 + after, grad1)
    weights = (weight1 + after_norm, weight1)
    for block in range(2):
        q_raw = both_ref[0, block].astype(F32)
        k_raw = both_ref[1, block].astype(F32)
        v_full = both_ref[2, block]
        q_feat, k_feat = feature(q_raw).astype(BF), feature(k_raw).astype(BF)
        scaled, residue = g_ref[block], r_ref[block]
        g_high, g_low = split(scaled)
        s_high, s_low = split(states[block])
        grad_high, grad_low = split(grads[block])
        scores = jnp.where(causal, dot(q_feat, k_feat, NT), 0.0).astype(BF)
        mixed = jnp.where(causal, dot(g_high, v_full, NT) + residue, 0.0).astype(BF)
        q_grad = (
            dot(mixed, k_feat, NN)
            + (dot(g_high, s_high, NT) + dot(g_high, s_low, NT) + dot(g_low, s_high, NT))
            + residue * norms[block]
        )
        k_grad = (
            dot(mixed, q_feat, TN)
            + (dot(v_full, grad_high, NT) + dot(v_full, grad_low, NT))
            + weights[block]
        )
        v_grad = dot(scores, g_high, TN) + (
            dot(k_feat, grad_high, NN) + dot(k_feat, grad_low, NN)
        )
        held[block, 0] = (q_grad * feature_slope(q_raw)).astype(BF)
        held[block, 1] = (k_grad * feature_slope(k_raw)).astype(BF)
        held[block, 2] = v_grad.astype(BF)
    keep_ref[...] = held[me]
    send_ref[...] = held[1 - me]


def merge_body(core, keep_ref, back_ref, q_ref, k_ref, v_ref):
    mine = pl.ds(pl.multiple_of(core[0] * DH, DH), DH)
    other = pl.ds(pl.multiple_of((1 - core[0]) * DH, DH), DH)
    for part, ref in enumerate((q_ref, k_ref, v_ref)):
        ref[:, mine] = keep_ref[part]
        ref[:, other] = back_ref[part]


def weight_body(core, mine_ref, other_ref, og_ref, out_ref):
    mine = pl.ds(pl.multiple_of(core[0] * DH, DH), DH)
    other = pl.ds(pl.multiple_of((1 - core[0]) * DH, DH), DH)
    out_ref[mine, :] = dot(mine_ref[...], og_ref[...], TN)
    out_ref[other, :] = dot(other_ref[...], og_ref[...], TN)


def total_body(core, in_ref, keep_ref, send_ref, held):
    held[...] = jnp.sum(in_ref[...], axis=0)
    keep_ref[...] = held[pl.ds(pl.multiple_of(core[0] * 8, 8), 8), :]
    send_ref[...] = held[pl.ds(pl.multiple_of((1 - core[0]) * 8, 8), 8), :]


def on_device(nx, ny, nz, queries, keys, values, out_grad, out_weight):
    chips = nx * ny
    tok, width = queries.shape[1:]
    pairs = width // (2 * DH)
    wide = width // 2
    model = out_grad.shape[2]
    half = model // 2
    me = lax.axis_index("c")
    core = jnp.reshape(me, (1,)).astype(jnp.int32)
    q_in, k_in, v_in, og = (
        part.reshape(tok, part.shape[2]) for part in (queries, keys, values, out_grad)
    )
    swap = functools.partial(lax.ppermute, axis_name="c", perm=[(0, 1), (1, 0)])
    plane = ("x", "y")

    sent = call(
        pack_body,
        (pairs,),
        [((tok, DH), lambda j, c: (0, 2 * j + 1 - c[0]))] * 3,
        [((3, tok, DH), lambda j, c: (0, 0, j), (3, tok, wide), BF)],
    )(core, q_in, k_in, v_in)[0]
    other_in = swap(sent)
    og_other = swap(og)

    moves = []
    for x in range(nx):
        for y in range(ny):
            for c in range(2):
                place = (x % (nx // 2)) * ny * 2 + y * 2 + c
                to = place * 2 + x // (nx // 2)
                moves.append((x * ny * 2 + y * 2 + c, to))
    rows = lax.ppermute(out_weight, ("x", "y", "c"), moves)
    weight = lax.all_gather(rows, ("z", "x", "y"), axis=0, tiled=True)

    col = lambda j, c: (0, 0, j)
    col4 = lambda j, c: (0, 0, 0, j)
    lead = lambda j, c: (j, 0, 0)
    state_spec = ((2, ROWS, DH), lead)
    state_out = (2, ROWS, DH), lead, (2 * pairs, ROWS, DH), F32
    pair_spec = ((2, tok, DH), col)
    pair_out = (2, tok, DH), col, (2, tok, wide), F32

    og_half = call(
        grads_body,
        (half // 512,),
        [((tok, 512), lambda j, c: (0, (half // 512) * c[0] + j))] * 2,
        [((2, tok, 512), col, (2, tok, half), BF)],
    )(core, og, og_other)[0]
    og_all = lax.all_gather(og_half.reshape(2 * tok, half), "z", axis=0, tiled=True)

    both, local_sum, first = call(
        local_body,
        (pairs,),
        [((tok, DH), lambda j, c: (0, 2 * j + c[0]))] * 3 + [((3, tok, DH), col)],
        [((3, 2, tok, DH), col4, (3, 2, tok, wide), BF), state_out, state_out],
    )(core, q_in, k_in, v_in, other_in)

    def carried_in(state, backward):
        parts = lax.all_to_all(state, plane, 0, 0, tiled=True)
        whole = ((chips, ROWS, DH), lambda j, c: (0, 0, 0))
        carried = call(
            functools.partial(scan_body, backward),
            (1,),
            [whole],
            [(*whole, (chips, ROWS, DH), F32)],
        )(core, parts)[0]
        return lax.all_to_all(carried, plane, 0, 0, tiled=True)

    earlier = carried_in(local_sum, False)
    attended, outputs, dens = call(
        forward_body,
        (pairs,),
        [((3, 2, tok, DH), col4), state_spec, state_spec],
        [((1, 2 * tok, DH), lead, (pairs, 2 * tok, DH), BF), pair_out, pair_out],
    )(core, both, earlier, first)

    att_mine = lax.all_to_all(attended, "z", 0, 0, tiled=True)
    att_other = swap(att_mine)
    tokens = nz * 2 * tok
    partial = call(
        weight_body,
        (half // 256,),
        [
            ((tokens, DH), lambda j, c: (0, 0)),
            ((tokens, DH), lambda j, c: (0, 0)),
            ((tokens, 256), lambda j, c: (0, j)),
        ],
        [((2 * DH, 256), lambda j, c: (0, j), (2 * DH, half), F32)],
    )(core, att_mine.reshape(tokens, DH), att_other.reshape(tokens, DH), og_all)[0]
    pieces = lax.all_to_all(
        partial.reshape(chips, 2 * DH // chips, half), plane, 0, 0, tiled=True
    )
    rows_each = 2 * DH // chips
    kept, moved = call(
        total_body,
        (1,),
        [((chips, rows_each, half), lambda j, c: (0, 0, 0))],
        [((rows_each // 2, half), lambda j, c: (0, 0), (rows_each // 2, half), F32)] * 2,
        [pltpu.VMEM((rows_each, half), F32)],
    )(core, pieces)
    got = swap(moved)
    weight_grad = jnp.where(
        me == 0, jnp.concatenate([kept, got], axis=1), jnp.concatenate([got, kept], axis=1)
    )

    scaled, residue, grad_sum, last = call(
        scaled_body,
        (pairs,),
        [
            ((DH, model), lambda j, c: (j, 0)),
            ((tok, model), lambda j, c: (0, 0)),
            ((tok, model), lambda j, c: (0, 0)),
            ((1, 2, tok, DH), col4),
            pair_spec,
            pair_spec,
        ],
        [pair_out, pair_out, state_out, state_out],
    )(core, weight, og, og_other, both, outputs, dens)
    later = carried_in(grad_sum, True)
    keep, send = call(
        backward_body,
        (pairs,),
        [
            ((3, 2, tok, DH), col4),
            state_spec,
            state_spec,
            pair_spec,
            pair_spec,
            state_spec,
            state_spec,
        ],
        [((3, tok, DH), col, (3, tok, wide), BF)] * 2,
        [pltpu.VMEM((2, 3, tok, DH), BF)],
    )(core, both, earlier, first, scaled, residue, later, last)
    back = swap(send)
    grads = call(
        merge_body,
        (pairs,),
        [((3, tok, DH), col)] * 2,
        [((tok, 2 * DH), lambda j, c: (0, j), (tok, width), BF)] * 3,
    )(core, keep, back)
    return (*(grad.reshape(1, tok, width) for grad in grads), weight_grad)


def solution(mesh):
    nz, nx, ny = mesh.shape["dp"], 4, mesh.shape["seq"] // 8
    grid = Mesh(mesh.devices.reshape(nz, nx, ny, 2), ("z", "x", "y", "c"))
    tokens = P("z", ("x", "y", "c"), None)
    weights = P(("z", "x", "y", "c"), None)
    return jax.shard_map(
        functools.partial(on_device, nx, ny, nz),
        mesh=grid,
        in_specs=(tokens, tokens, tokens, tokens, weights),
        out_specs=(tokens, tokens, tokens, weights),
        check_vma=False,
    )
```

time: 1690 us -> 247 us (0.15)
  waiting for transfers between devices: 1430 us -> 101 us
  other arithmetic: 104 us -> 0.64 us
  matrix products: 39.5 us -> 0 us
  Pallas kernels: 0 us -> 34.2 us
  starting transfers between devices: 0.34 us -> 29.3 us
  local copies, waits for them, and re-layouts: 36.7 us -> 18.6 us
    reduce_scatter x1 -> x0, waiting for transfers between devices: 1200 us -> none  [on_device(): lax.psum_scatter(jnp.einsum('btr,btd->rd', attended, out_grad, preferred_...]
    all_gather x3 -> x2, waiting for transfers between devices: 226 us -> 69 us  [the longest x1 64.2 us: on_device(): weight = lax.all_gather(rows, ('z', 'x', 'y'), axis=0, tiled=True)]
    select_n x125 -> x1, other arithmetic: 102 us -> 0.64 us  [on_device(): jnp.where(me == 0, jnp.concatenate([kept, got], axis=1), jnp.concatenate(...]
    all_gather x2 -> x0, blocking collectives: 50.9 us -> none  [carried_in(): pieces = jax.tree.map(lambda part: lax.all_gather(part, axis), value)]
    all_to_all x0 -> x3, blocking collectives: none -> 47.2 us  [the longest x2 33.7 us: carried_in(): parts = lax.all_to_all(state, plane, 0, 0, tiled=True)]
    dot_general x16 -> x0, matrix products: 39.5 us -> none  [the longest x7 13.3 us: mix_sum(): return jnp.einsum(form, left, right, precision=lax.Precision.HIGHEST)]
    pallas_call x0 -> x11, Pallas kernels: none -> 34.2 us  [the longest x1 8.13 us: on_device(): call(backward_body, (pairs,), [((3, 2, tok, DH), col4), state_spec, state...]
    rev x2 -> x0, local copies, waits for them, and re-layouts: 23.1 us -> none  [carried_in(): pieces = jax.tree.map(lambda part: part[::-1], pieces)]
  transfers between devices with their start and end apart: 4 -> 11, of which waited for: 4 -> 9; matrix products, arithmetic and copies ran while one was open for 10% -> 0% of each run, Pallas kernels for 0% -> 13%
where the time goes in v1:
time: 247 us; the launch traced here: 245 us
  waiting for transfers between devices  101 us (41%)
  blocking collectives  47.2 us (19%)
  Pallas kernels  34.2 us (14%)
  starting transfers between devices  29.3 us (12%)
  local copies, waits for them, and re-layouts  18.6 us (8%)
  between operations  14.2 us (6%)
    all_gather x1, waiting for transfers between devices, on_device(): weight = lax.all_gather(rows, ('z', 'x', 'y'), axis=0, tiled=True)  64.2 us
    all_to_all x2, blocking collectives, carried_in(): parts = lax.all_to_all(state, plane, 0, 0, tiled=True)  33.7 us
    all_to_all x1, waiting for transfers between devices, on_device(): att_mine = lax.all_to_all(attended, 'z', 0, 0, tiled=True)  20.2 us
    unnamed x40, local copies, waits for them, and re-layouts  18.6 us
    all_to_all x1, blocking collectives, carried_in(): return lax.all_to_all(carried, plane, 0, 0, tiled=True)  13.5 us
    pallas_call x1, Pallas kernels, on_device(): call(backward_body, (pairs,), [((3, 2, tok, DH), col4), state_spec, state...  8.13 us
    pallas_call x1, Pallas kernels, on_device(): call(scaled_body, (pairs,), [((DH, model), lambda j, c: (j, 0)), ((tok, m...  7.85 us
    all_to_all x1, starting transfers between devices, on_device(): lax.all_to_all(partial.reshape(chips, 2 * DH // chips, half), plane, 0, 0...  6.53 us
  transfers between devices with their start and end apart: 11, of which 9 were waited for; matrix products, arithmetic and copies ran while one was open for 0% of the time, Pallas kernels for 13%

profile of v1, /device:TPU:1, one launch (start us, length us, event | category | flops | bytes accessed | tf_op | source)
XLA Modules:
  0.0 245.3 jit_solution(13561205008443522053)
XLA Ops:
  7.2 4.6 %collective-permute-start.1 = (bf16[8,2048]{1,0:T(8,128)(2,1)}, bf16[8,2048]{1,0:T(8,128)(2,1)S(1)}, u32[]{:S(2)}, u32[]{:S(2)}) collective-permute-start(bf16[8,2048]{1,0:T(8,128)(2,1)} %param.9), channel_id=1, source_target_pairs={{0,0},{1,2},{2,4},{3,6},{4,8},{5,10},{6,12},{7,14},{8,16},{9,18},{... | collective-permute-start | bytes 98312 | tf_op jit(solution)/shard_map/ppermute | solution.py:267
  11.8 3.2 %collective-permute-done.1 = bf16[8,2048]{1,0:T(8,128)(2,1)S(1)} collective-permute-done((bf16[8,2048]{1,0:T(8,128)(2,1)}, bf16[8,2048]{1,0:T(8,128)(2,1)S(1)}, u32[]{:S(2)}, u32[]{:S(2)}) %collective-permute-start.1) | collective-permute-done | bytes 32800 | tf_op jit(solution)/shard_map/ppermute | solution.py:267
  15.8 2.1 collective-permute-done.2.ogr_ref.other_ref
  18.0 1.2 copy-done.4
  21.1 1.0 copy-done.2
  22.2 1.0 copy-done.3
  24.2 2.1 collective-permute-done.other_ref
  26.3 2.8 %shard_map.85 = (bf16[3,2,128,1024]{3,2,1,0:T(8,128)(2,1)S(1)}, f32[16,72,128]{2,1,0:T(8,128)S(1)}, f32[16,72,128]{2,1,0:T(8,128)S(1)}) custom-call(s32[1]{0:T(128)} %bitcast.core, bf16[128,2048]{1,0:T(8,128)(2,1)S(1)} %bitcast.13, bf16[128,2048]{1,0:T(8,128)(2,1)S(1)} %bitcast.15, bf16[128,2048]{1,0:T(8,128)(2,1)S(1)} %bitcast.17, ...), custom_call_target="tpu_custom_call" | custom-call | tf_op jit(solution)/shard_map/pallas_call | solution.py:286
  29.2 19.6 %all_to_all.30.in_ref = f32[16,72,128]{2,1,0:T(8,128)S(1)} all-to-all(f32[16,72,128]{2,1,0:T(8,128)S(1)} %get-tuple-element.22), channel_id=1, replica_groups=mesh['z'=8,'x'=4,'y'=4,'c'=2] {'x','y'}, dimensions={0} | all-to-all | bytes 1179648 | tf_op jit(solution)/shard_map/all_to_all | solution.py:294
  48.9 13.5 %all_to_all.31.in_ref = f32[16,72,128]{2,1,0:T(8,128)S(1)} all-to-all(f32[16,72,128]{2,1,0:T(8,128)S(1)} %shard_map.86), channel_id=1, replica_groups=mesh['z'=8,'x'=4,'y'=4,'c'=2] {'x','y'}, dimensions={0} | all-to-all | bytes 1179648 | tf_op jit(solution)/shard_map/all_to_all | solution.py:302
  62.4 4.7 %shard_map.87 = (bf16[8,256,128]{2,1,0:T(8,128)(2,1)}, f32[2,128,1024]{2,1,0:T(8,128)S(1)}, f32[2,128,1024]{2,1,0:T(8,128)S(1)}) custom-call(s32[1]{0:T(128)} %bitcast.core, bf16[3,2,128,1024]{3,2,1,0:T(8,128)(2,1)S(1)} %get-tuple-element.21.both_ref.q_ref, f32[16,72,128]{2,1,0:T(8,128)S(1)} %all_to_all.31.in_ref, f32[16,72,128]{2,1,0:T(8,128)S(1)} %get-tuple-element.23.first_ref), custom_call_target="tpu_custom_call" | custom-call | tf_op jit(solution)/shard_map/pallas_call | solution.py:305
  69.0 64.2 %all-gather.3.cloned.1.call-done.w_ref = bf16[1024,2048]{1,0:T(8,128)(2,1)} async-done(((bf16[8,2048]{1,0:T(8,128)(2,1)}), bf16[1024,2048]{1,0:T(8,128)(2,1)}) %all-gather.3.cloned.1.call-update) | async-done | bytes 4194320 | tf_op jit(solution)/shard_map/all_gather | solution.py:268
  133.2 1.0 copy-done.5
  135.3 1.2 copy-done.9
  136.6 7.8 %shard_map.88 = (f32[2,128,1024]{2,1,0:T(8,128)S(1)}, f32[2,128,1024]{2,1,0:T(8,128)S(1)}, f32[16,72,128]{2,1,0:T(8,128)S(1)}, f32[16,72,128]{2,1,0:T(8,128)S(1)}) custom-call(s32[1]{0:T(128)} %bitcast.core, bf16[1024,2048]{1,0:T(8,128)(2,1)} %all-gather.3.cloned.1.call-done.w_ref, bf16[128,2048]{1,0:T(8,128)(2,1)S(1)} %bitcast.20, ...), custom_call_target="tpu_custom_call" | custom-call | tf_op jit(solution)/shard_map/pallas_call | solution.py:341
  147.3 14.1 %all_to_all.32.in_ref = f32[16,72,128]{2,1,0:T(8,128)S(1)} all-to-all(f32[16,72,128]{2,1,0:T(8,128)S(1)} %get-tuple-element.28), channel_id=1, replica_groups=mesh['z'=8,'x'=4,'y'=4,'c'=2] {'x','y'}, dimensions={0} | all-to-all | bytes 1179648 | tf_op jit(solution)/shard_map/all_to_all | solution.py:294
  161.3 4.0 %all-to-all-start.4 = ((bf16[8,256,128]{2,1,0:T(8,128)(2,1)}), bf16[8,256,128]{2,1,0:T(8,128)(2,1)S(1)}, u32[]{:S(2)}, u32[]{:S(2)}) async-start(bf16[8,256,128]{2,1,0:T(8,128)(2,1)} %get-tuple-element.35), calls=%async_computation.4 | async-start | bytes 1048576 | tf_op jit(solution)/shard_map/all_to_all | solution.py:312
  166.2 20.2 %all-to-all-done.4 = bf16[8,256,128]{2,1,0:T(8,128)(2,1)S(1)} async-done(((bf16[8,256,128]{2,1,0:T(8,128)(2,1)}), bf16[8,256,128]{2,1,0:T(8,128)(2,1)S(1)}, u32[]{:S(2)}, u32[]{:S(2)}) %all-to-all-start.4) | async-done | bytes 524320 | tf_op jit(solution)/shard_map/all_to_all | solution.py:312
  186.4 3.7 %all-to-all-start.3 = ((f32[16,72,128]{2,1,0:T(8,128)}), f32[16,72,128]{2,1,0:T(8,128)S(1)}, u32[]{:S(2)}, u32[]{:S(2)}) async-start(f32[16,72,128]{2,1,0:T(8,128)} %shard_map.89), calls=%async_computation.3 | async-start | bytes 1179648 | tf_op jit(solution)/shard_map/all_to_all | solution.py:302
  190.1 5.9 %collective-permute-start.4 = (bf16[8,256,128]{2,1,0:T(8,128)(2,1)S(1)}, bf16[8,256,128]{2,1,0:T(8,128)(2,1)S(1)}, u32[]{:S(2)}, u32[]{:S(2)}) collective-permute-start(bf16[8,256,128]{2,1,0:T(8,128)(2,1)S(1)} %all-to-all-done.4), channel_id=1, source_target_pairs={{0,1},{1,0},{2,3},{3,2},{4,5},{5,4},{6,7},{7,6},{8,9},{9,8},{10,11... | collective-permute-start | bytes 1572872 | tf_op jit(solution)/shard_map/ppermute | solution.py:313
  196.0 1.5 collective-permute-done.4
  197.6 4.8 %all-gather.5.cloned.1.call-done.og_ref = bf16[2048,1024]{1,0:T(8,128)(2,1)} async-done(((bf16[256,1024]{1,0:T(8,128)(2,1)}), bf16[2048,1024]{1,0:T(8,128)(2,1)}) %all-gather.5.cloned.1.call-update) | async-done | bytes 4194320 | tf_op jit(solution)/shard_map/all_gather | solution.py:284
  202.4 4.9 %shard_map.93 = f32[256,1024]{1,0:T(8,128)} custom-call(s32[1]{0:T(128)} %bitcast.core, bf16[2048,128]{1,0:T(8,128)(2,1)S(1)} %bitcast.21, bf16[2048,128]{1,0:T(8,128)(2,1)S(1)} %bitcast.22, bf16[2048,1024]{1,0:T(8,128)(2,1)} %all-gather.5.cloned.1.call-done.og_ref), custom_call_target="tpu_custom_call" | custom-call | tf_op jit(solution)/shard_map/pallas_call | solution.py:315
  207.3 6.5 %all-to-all-start.5 = ((f32[16,16,1024]{2,1,0:T(8,128)}), f32[16,16,1024]{2,1,0:T(8,128)S(1)}, u32[]{:S(2)}, u32[]{:S(2)}) async-start(f32[16,16,1024]{2,1,0:T(8,128)} %bitcast.11), calls=%async_computation.5 | async-start | bytes 2097152 | tf_op jit(solution)/shard_map/all_to_all | solution.py:325
  213.9 1.2 copy-done.12
  215.1 1.2 copy-done.14
  216.3 1.1 copy-done.18
  217.4 8.1 %shard_map.90 = (bf16[3,128,1024]{2,1,0:T(8,128)(2,1)S(1)}, bf16[3,128,1024]{2,1,0:T(8,128)(2,1)}) custom-call(s32[1]{0:T(128)} %bitcast.core, bf16[3,2,128,1024]{3,2,1,0:T(8,128)(2,1)} %copy-done, f32[16,72,128]{2,1,0:T(8,128)S(1)} %all_to_all.31.in_ref, f32[16,72,128]{2,1,0:T(8,128)S(1)} %get-tuple-element.23.first_ref, f32[2,128,1024]{2,1,0:T(8,128)S(1)} %copy-done.12, ...), custom_call_target="tpu_custom_call" | custom-call | tf_op jit(solution)/shard_map/pallas_call | solution.py:355
  227.3 2.0 all-to-all-done.5.in_ref
  229.4 3.2 %collective-permute-start.5 = (f32[8,1024]{1,0:T(8,128)S(1)}, f32[8,1024]{1,0:T(8,128)S(1)}, u32[]{:S(2)}, u32[]{:S(2)}) collective-permute-start(f32[8,1024]{1,0:T(8,128)S(1)} %get-tuple-element.37), channel_id=1, source_target_pairs={{0,1},{1,0},{2,3},{3,2},{4,5},{5,4},{6,7},{7,6},{8,9},{9,8},{10,11... | collective-permute-start | bytes 98312 | tf_op jit(solution)/shard_map/ppermute | solution.py:336
  234.2 1.1 copy-done.16
  235.3 3.2 %shard_map.91 = (bf16[128,2048]{1,0:T(8,128)(2,1)}, bf16[128,2048]{1,0:T(8,128)(2,1)}, bf16[128,2048]{1,0:T(8,128)(2,1)}) custom-call(s32[1]{0:T(128)} %bitcast.core, bf16[3,128,1024]{2,1,0:T(8,128)(2,1)S(1)} %copy-done.16, bf16[3,128,1024]{2,1,0:T(8,128)(2,1)S(1)} %collective-permute-done.3.back_ref), custom_call_target="tpu_custom_call" | custom-call | tf_op jit(solution)/shard_map/pallas_call | solution.py:371
  (47 shorter events, 13.9 us)
Async XLA Ops:
  7.2 126.1 %all-gather.3.cloned.1.call-start = ((), (), s32[]{:S(2)}) async-start(), calls=%async_computation.6 | async-start | bytes 4227072 | tf_op jit(solution)/shard_map/all_gather | solution.py:268
  7.2 7.8 %collective-permute-start.1 = (bf16[8,2048]{1,0:T(8,128)(2,1)}, bf16[8,2048]{1,0:T(8,128)(2,1)S(1)}, u32[]{:S(2)}, u32[]{:S(2)}) collective-permute-start(bf16[8,2048]{1,0:T(8,128)(2,1)} %param.9), channel_id=1, source_target_pairs={{0,0},{1,2},{2,4},{3,6},{4,8},{5,10},{6,12},{7,14},{8,16},{9,18},{... | collective-permute-start | bytes 98312 | tf_op jit(solution)/shard_map/ppermute | solution.py:267
  15.1 0.6 copy-start.19
  15.7 186.7 %all-gather.5.cloned.1.call-start = ((), (), s32[]{:S(2)}) async-start(), calls=%async_computation.7 | async-start | bytes 4718592 | tf_op jit(solution)/shard_map/all_gather | solution.py:284
  15.7 2.2 collective-permute-start.2
  18.0 6.2 %copy-start.6 = (bf16[128,2048]{1,0:T(8,128)(2,1)}, bf16[128,2048]{1,0:T(8,128)(2,1)S(1)}, u32[]{:S(2)}) copy-start(bf16[128,2048]{1,0:T(8,128)(2,1)S(1)} %collective-permute-done.2.ogr_ref.other_ref) | copy-start | bytes 1572868
  18.0 1.2 copy-start.4
  20.1 1.0 copy-start.1
  21.1 1.0 copy-start.2
  22.2 1.0 copy-start.3
  24.0 2.4 collective-permute-start
  29.2 104.1 %copy-start = (bf16[3,2,128,1024]{3,2,1,0:T(8,128)(2,1)}, bf16[3,2,128,1024]{3,2,1,0:T(8,128)(2,1)S(1)}, u32[]{:S(2)}) copy-start(bf16[3,2,128,1024]{3,2,1,0:T(8,128)(2,1)S(1)} %get-tuple-element.21.both_ref.q_ref) | copy-start | bytes 4718596
  67.1 1.0 copy-start.8
  68.0 1.0 copy-start.10
  133.2 1.0 copy-start.5
  134.3 1.0 copy-start.7
  135.3 1.2 copy-start.9
  144.4 1.0 copy-start.11
  145.4 1.0 copy-start.13
  146.4 0.9 copy-start.17
  161.3 25.1 %all-to-all-start.4 = ((bf16[8,256,128]{2,1,0:T(8,128)(2,1)}), bf16[8,256,128]{2,1,0:T(8,128)(2,1)S(1)}, u32[]{:S(2)}, u32[]{:S(2)}) async-start(bf16[8,256,128]{2,1,0:T(8,128)(2,1)} %get-tuple-element.35), calls=%async_computation.4 | async-start | bytes 1048576 | tf_op jit(solution)/shard_map/all_to_all | solution.py:312
  186.4 20.9 %all-to-all-start.3 = ((f32[16,72,128]{2,1,0:T(8,128)}), f32[16,72,128]{2,1,0:T(8,128)S(1)}, u32[]{:S(2)}, u32[]{:S(2)}) async-start(f32[16,72,128]{2,1,0:T(8,128)} %shard_map.89), calls=%async_computation.3 | async-start | bytes 1179648 | tf_op jit(solution)/shard_map/all_to_all | solution.py:302
  190.1 7.4 %collective-permute-start.4 = (bf16[8,256,128]{2,1,0:T(8,128)(2,1)S(1)}, bf16[8,256,128]{2,1,0:T(8,128)(2,1)S(1)}, u32[]{:S(2)}, u32[]{:S(2)}) collective-permute-start(bf16[8,256,128]{2,1,0:T(8,128)(2,1)S(1)} %all-to-all-done.4), channel_id=1, source_target_pairs={{0,1},{1,0},{2,3},{3,2},{4,5},{5,4},{6,7},{7,6},{8,9},{9,8},{10,11... | collective-permute-start | bytes 1572872 | tf_op jit(solution)/shard_map/ppermute | solution.py:313
  207.3 22.1 %all-to-all-start.5 = ((f32[16,16,1024]{2,1,0:T(8,128)}), f32[16,16,1024]{2,1,0:T(8,128)S(1)}, u32[]{:S(2)}, u32[]{:S(2)}) async-start(f32[16,16,1024]{2,1,0:T(8,128)} %bitcast.11), calls=%async_computation.5 | async-start | bytes 2097152 | tf_op jit(solution)/shard_map/all_to_all | solution.py:325
  213.8 1.2 copy-start.12
  215.1 1.2 copy-start.14
  216.3 1.1 copy-start.18
  225.5 0.9 copy-start.15
  226.4 7.8 %collective-permute-start.3 = (bf16[3,128,1024]{2,1,0:T(8,128)(2,1)}, bf16[3,128,1024]{2,1,0:T(8,128)(2,1)S(1)}, u32[]{:S(2)}, u32[]{:S(2)}) collective-permute-start(bf16[3,128,1024]{2,1,0:T(8,128)(2,1)} %get-tuple-element.31), channel_id=1, source_target_pairs={{0,1},{1,0},{2,3},{3,2},{4,5},{5,4},{6,7},{7,6},{8,9},{9,8},{10,11... | collective-permute-start | bytes 2359304 | tf_op jit(solution)/shard_map/ppermute | solution.py:370
  229.4 4.1 %collective-permute-start.5 = (f32[8,1024]{1,0:T(8,128)S(1)}, f32[8,1024]{1,0:T(8,128)S(1)}, u32[]{:S(2)}, u32[]{:S(2)}) collective-permute-start(f32[8,1024]{1,0:T(8,128)S(1)} %get-tuple-element.37), channel_id=1, source_target_pairs={{0,1},{1,0},{2,3},{3,2},{4,5},{5,4},{6,7},{7,6},{8,9},{9,8},{10,11... | collective-permute-start | bytes 98312 | tf_op jit(solution)/shard_map/ppermute | solution.py:336
  234.2 1.1 copy-start.16
Sparse Core Ops, SparseCore 0:
  15.8 117.3 all-gather.2
  135.6 66.7 all-gather.4

commit v2 on v1

v2 whole, which is shorter than its diff:
```python
import functools

import jax
import jax.numpy as jnp
from jax import lax
from jax.experimental import pallas as pl
from jax.experimental.pallas import tpu as pltpu
from jax.sharding import Mesh, PartitionSpec as P

DH = 128
BLK = 128
BF = jnp.bfloat16
F32 = jnp.float32
NN = (((1,), (0,)), ((), ()))
NT = (((1,), (1,)), ((), ()))
TN = (((0,), (0,)), ((), ()))
HALF = DH // 2
ROWS = HALF + 8
PARAMS = pltpu.CompilerParams(vmem_limit_bytes=16 * 1024 * 1024)


def dot(left, right, dims):
    return lax.dot_general(left, right, dims, preferred_element_type=F32)


def split(wide):
    high = wide.astype(BF)
    return high, (wide - high.astype(F32)).astype(BF)


def feature(raw):
    return jnp.where(raw > 0, raw + 1.0, jnp.exp(jnp.minimum(raw, 0.0)))


def feature_slope(raw):
    return jnp.where(raw > 0, 1.0, jnp.exp(jnp.minimum(raw, 0.0)))


def features_of(raw):
    return feature(raw.astype(F32)).astype(BF)


def causal_mask():
    row = lax.broadcasted_iota(jnp.int32, (BLK, BLK), 0)
    col = lax.broadcasted_iota(jnp.int32, (BLK, BLK), 1)
    return row >= col


def state_of(ref):
    return jnp.concatenate([ref[0, :HALF], ref[1, :HALF]], axis=0), ref[0, HALF : HALF + 1]


def put_state(ref, matrix, vector):
    tail = jnp.broadcast_to(vector, (8, DH))
    for half in range(2):
        ref[half, :HALF] = matrix[half * HALF : (half + 1) * HALF]
        ref[half, HALF:] = tail


def call(body, grid, ins, outs, scratch=()):
    run = pl.pallas_call(
        body,
        grid_spec=pltpu.PrefetchScalarGridSpec(
            num_scalar_prefetch=1,
            grid=grid,
            in_specs=[pl.BlockSpec(*spec) for spec in ins],
            out_specs=[pl.BlockSpec(spec[0], spec[1]) for spec in outs],
            scratch_shapes=list(scratch),
        ),
        out_shape=[pltpu.HBM(spec[2], spec[3]) for spec in outs],
        compiler_params=PARAMS,
    )

    return run


def kept_out(*arrays):
    return [pltpu.with_memory_space_constraint(array, pltpu.HBM) for array in arrays]


def put_pair(ref, core, mine, other):
    ref[core] = mine[...]
    ref[1 - core] = other[...]


def local_body(place, k_ref, v_ref, k_other, v_other, keys, values, sum_ref, first_ref):
    put_pair(keys, place[0], k_ref, k_other)
    put_pair(values, place[0], v_ref, v_other)
    total, total_norm = None, None
    for block in range(2):
        k_feat = features_of(keys[block])
        state = dot(k_feat, values[block], TN)
        norm = jnp.sum(k_feat.astype(F32), axis=0, keepdims=True)
        if block == 0:
            put_state(first_ref, state, norm)
            total, total_norm = state, norm
        else:
            put_state(sum_ref, total + state, total_norm + norm)


def scan_body(backward, place, in_ref, out_ref):
    count = in_ref.shape[0]
    so_far = jnp.zeros(in_ref.shape[1:], F32)
    order = range(count - 1, -1, -1) if backward else range(count)
    for position in order:
        out_ref[position] = so_far
        so_far = so_far + in_ref[position]


def attn_grad_body(place, og_ref, w_ref, out_ref):
    out_ref[0] = dot(og_ref[...], w_ref[...], NT).astype(BF)


def forward_body(
    place,
    q_ref,
    q_other,
    keys,
    values,
    in_ref,
    first_ref,
    queries,
    copy_ref,
    att_ref,
    o_ref,
    den_ref,
):
    put_pair(queries, place[0], q_ref, q_other)
    copy_ref[...] = in_ref[...]
    causal = causal_mask()
    state, norm = state_of(in_ref)
    for block in range(2):
        if block == 1:
            extra, extra_norm = state_of(first_ref)
            state, norm = state + extra, norm + extra_norm
        q_feat = features_of(queries[block])
        k_feat = features_of(keys[block])
        scores = jnp.where(causal, dot(q_feat, k_feat, NT), 0.0)
        den = jnp.sum(scores, axis=1, keepdims=True) + jnp.sum(
            q_feat.astype(F32) * norm, axis=1, keepdims=True
        )
        high, low = split(state)
        out = (
            dot(scores.astype(BF), values[block], NN)
            + dot(q_feat, high, NN)
            + dot(q_feat, low, NN)
        ) / den
        att_ref[0, block * BLK : (block + 1) * BLK] = out.astype(BF)
        o_ref[block] = out
        den_ref[block] = jnp.broadcast_to(den, (BLK, DH))


def scaled_body(
    place,
    queries,
    o_ref,
    den_ref,
    grad_ref,
    grad_other,
    g_ref,
    r_ref,
    sum_ref,
    last_ref,
    grads,
):
    me = place[0]
    grads[me] = grad_ref[0]
    grads[1 - me] = grad_other[0]
    total, total_norm = None, None
    for block in range(2):
        q_feat = features_of(queries[block])
        scaled = grads[block].astype(F32) / den_ref[block]
        g_ref[block] = scaled
        residue = -jnp.sum(scaled * o_ref[block], axis=1, keepdims=True)
        r_ref[block] = jnp.broadcast_to(residue, (BLK, DH))
        high, low = split(scaled)
        grad = dot(q_feat, high, TN) + dot(q_feat, low, TN)
        grad_norm = jnp.sum(residue * q_feat.astype(F32), axis=0, keepdims=True)
        if block == 0:
            total, total_norm = grad, grad_norm
        else:
            put_state(last_ref, grad, grad_norm)
            put_state(sum_ref, total + grad, total_norm + grad_norm)


def backward_body(
    place,
    queries,
    keys,
    values,
    in_ref,
    first_ref,
    g_ref,
    r_ref,
    later_ref,
    last_ref,
    keep_ref,
    send_ref,
    held,
):
    me = place[0]
    causal = causal_mask()
    state0, norm0 = state_of(in_ref)
    extra, extra_norm = state_of(first_ref)
    grad1, weight1 = state_of(later_ref)
    after, after_norm = state_of(last_ref)
    states = (state0, state0 + extra)
    norms = (norm0, norm0 + extra_norm)
    grads = (grad1 + after, grad1)
    weights = (weight1 + after_norm, weight1)
    for block in range(2):
        q_raw = queries[block].astype(F32)
        k_raw = keys[block].astype(F32)
        v_full = values[block]
        q_feat, k_feat = feature(q_raw).astype(BF), feature(k_raw).astype(BF)
        scaled, residue = g_ref[block], r_ref[block]
        g_high, g_low = split(scaled)
        s_high, s_low = split(states[block])
        grad_high, grad_low = split(grads[block])
        scores = jnp.where(causal, dot(q_feat, k_feat, NT), 0.0).astype(BF)
        mixed = jnp.where(causal, dot(g_high, v_full, NT) + residue, 0.0).astype(BF)
        q_grad = (
            dot(mixed, k_feat, NN)
            + (dot(g_high, s_high, NT) + dot(g_high, s_low, NT) + dot(g_low, s_high, NT))
            + residue * norms[block]
        )
        k_grad = (
            dot(mixed, q_feat, TN)
            + (dot(v_full, grad_high, NT) + dot(v_full, grad_low, NT))
            + weights[block]
        )
        v_grad = dot(scores, g_high, TN) + (
            dot(k_feat, grad_high, NN) + dot(k_feat, grad_low, NN)
        )
        held[block, 0] = (q_grad * feature_slope(q_raw)).astype(BF)
        held[block, 1] = (k_grad * feature_slope(k_raw)).astype(BF)
        held[block, 2] = v_grad.astype(BF)
    keep_ref[...] = held[me]
    send_ref[...] = held[1 - me]


def merge_body(place, keep_ref, back_ref, q_ref, k_ref, v_ref):
    mine = pl.ds(pl.multiple_of(place[0] * DH, DH), DH)
    other = pl.ds(pl.multiple_of((1 - place[0]) * DH, DH), DH)
    for part, ref in enumerate((q_ref, k_ref, v_ref)):
        ref[:, mine] = keep_ref[part]
        ref[:, other] = back_ref[part]


def weight_body(steps, place, mine_ref, other_ref, og_ref, send_ref, keep_ref, heads):
    left = pl.ds(pl.multiple_of(place[0] * DH, DH), DH)
    right = pl.ds(pl.multiple_of((1 - place[0]) * DH, DH), DH)

    @pl.when(pl.program_id(0) == 0)
    def _():
        heads[:, left] = mine_ref[...].reshape(-1, DH)
        heads[:, right] = other_ref[...].reshape(-1, DH)

    part = dot(heads[...], og_ref[...], TN)

    @pl.when(pl.program_id(0) < steps)
    def _():
        send_ref[...] = part

    @pl.when(pl.program_id(0) >= steps)
    def _():
        keep_ref[...] = part


def total_body(place, in_ref, keep_ref, send_ref, held):
    held[...] = jnp.sum(in_ref[...], axis=0)
    keep_ref[...] = held[pl.ds(pl.multiple_of(place[0] * 8, 8), 8), :]
    send_ref[...] = held[pl.ds(pl.multiple_of((1 - place[0]) * 8, 8), 8), :]


def on_device(nx, ny, nz, queries, keys, values, out_grad, out_weight):
    chips = nx * ny
    tok, width = queries.shape[1:]
    pairs = width // (2 * DH)
    wide = width // 2
    model = out_grad.shape[2]
    half = model // 2
    me = lax.axis_index("c")
    place = jnp.stack([lax.axis_index(name) for name in ("c", "x", "y", "z")]).astype(jnp.int32)
    q_in, k_in, v_in, og = (
        part.reshape(tok, part.shape[2]) for part in (queries, keys, values, out_grad)
    )
    swap = functools.partial(lax.ppermute, axis_name="c", perm=[(0, 1), (1, 0)])
    plane = ("x", "y")

    k_other, v_other, q_other = swap(k_in), swap(v_in), swap(q_in)
    og_all = lax.all_gather(og, "z", axis=0, tiled=True)

    col = lambda j, p: (0, 0, j)
    lead = lambda j, p: (j, 0, 0)
    state_spec = ((2, ROWS, DH), lead)
    state_out = (2, ROWS, DH), lead, (2 * pairs, ROWS, DH), F32
    pair_spec = ((2, tok, DH), col)
    pair_out = (2, tok, DH), col, (2, tok, wide), F32
    head_spec = ((tok, DH), lambda j, p: (0, 2 * j + p[0]))
    pair_hold = pltpu.VMEM((2, tok, DH), BF)

    both_out = (2, tok, DH), col, (2, tok, wide), BF
    keys_all, values_all, local_sum, first = call(
        local_body,
        (pairs,),
        [head_spec] * 4,
        [both_out, both_out, state_out, state_out],
    )(place, *kept_out(k_in, v_in), k_other, v_other)
    keys_all, values_all, first = kept_out(keys_all, values_all, first)

    spread = jnp.broadcast_to(out_weight[None], (chips, *out_weight.shape))
    rows_mine = lax.all_to_all(spread, plane, 0, 0, tiled=True)
    rows_mine, local_sum = lax.optimization_barrier((rows_mine, local_sum))

    def carried_in(state, backward):
        parts = lax.all_to_all(state, plane, 0, 0, tiled=True)
        whole = ((chips, ROWS, DH), lambda j, p: (0, 0, 0))
        carried = call(
            functools.partial(scan_body, backward),
            (1,),
            [whole],
            [(*whole, (chips, ROWS, DH), F32)],
        )(place, parts)[0]
        return lax.all_to_all(carried, plane, 0, 0, tiled=True)

    earlier = carried_in(local_sum, False)
    queries_all, earlier, attended, outputs, dens = call(
        forward_body,
        (pairs,),
        [head_spec] * 2 + [pair_spec] * 2 + [state_spec] * 2,
        [both_out, state_out]
        + [((1, 2 * tok, DH), lead, (pairs, 2 * tok, DH), BF), pair_out, pair_out],
    )(place, *kept_out(q_in), q_other, keys_all, values_all, earlier, first)

    og_all = lax.optimization_barrier((og_all, attended))[0]
    og_all = kept_out(og_all)[0]
    rows_other = swap(rows_mine)
    rows = jnp.where(
        me == 0,
        jnp.stack([rows_mine, rows_other], axis=1),
        jnp.stack([rows_other, rows_mine], axis=1),
    ).reshape(2 * DH, model)
    attn_grad = call(
        attn_grad_body,
        (nz,),
        [((tok, model), lambda k, p: (k, 0)), ((2 * DH, model), lambda k, p: (0, 0))],
        [((1, tok, 2 * DH), lead, (nz, tok, 2 * DH), BF)],
    )(place, og_all, rows)[0]
    att_mine = lax.all_to_all(attended, "z", 0, 0, tiled=True)
    attn_grad, att_mine = lax.optimization_barrier((attn_grad, att_mine))
    grad_mine = lax.all_to_all(attn_grad, "z", 0, 0, tiled=True)
    grad_other = swap(grad_mine)
    grad_spec = ((1, tok, DH), lambda j, p: (j, 0, p[0]))
    scaled, residue, grad_sum, last = call(
        scaled_body,
        (pairs,),
        [pair_spec] * 3 + [grad_spec] * 2,
        [pair_out, pair_out, state_out, state_out],
        [pair_hold],
    )(place, *kept_out(queries_all, outputs, dens), grad_mine, grad_other)

    att_other = swap(att_mine)
    steps = half // 256
    att_spec = ((nz, tok, DH), lambda j, p: (0, p[0], 0))
    moved, kept = call(
        functools.partial(weight_body, steps),
        (2 * steps,),
        [
            att_spec,
            att_spec,
            (
                (nz * tok, 256),
                lambda j, p: (0, jnp.where(j < steps, 1 - p[0], p[0]) * steps + lax.rem(j, steps)),
            ),
        ],
        [
            ((2 * DH, 256), lambda j, p: (0, jnp.minimum(j, steps - 1)), (2 * DH, half), F32),
            ((2 * DH, 256), lambda j, p: (0, jnp.maximum(j - steps, 0)), (2 * DH, half), F32),
        ],
        [pltpu.VMEM((nz * tok, 2 * DH), BF)],
    )(place, att_mine, att_other, og_all)
    partial = kept + swap(moved)
    rows_each = 2 * DH // chips
    pieces = lax.all_to_all(
        partial.reshape(chips, rows_each, half), plane, 0, 0, tiled=True
    )
    kept, moved = call(
        total_body,
        (1,),
        [((chips, rows_each, half), lambda j, p: (0, 0, 0))],
        [((rows_each // 2, half), lambda j, p: (0, 0), (rows_each // 2, half), F32)] * 2,
        [pltpu.VMEM((rows_each, half), F32)],
    )(place, pieces)
    got = swap(moved)
    weight_grad = jnp.where(
        me == 0, jnp.concatenate([kept, got], axis=1), jnp.concatenate([got, kept], axis=1)
    )

    later = carried_in(grad_sum, True)
    keep, send = call(
        backward_body,
        (pairs,),
        [pair_spec] * 3
        + [state_spec, state_spec, pair_spec, pair_spec, state_spec, state_spec],
        [((3, tok, DH), col, (3, tok, wide), BF)] * 2,
        [pltpu.VMEM((2, 3, tok, DH), BF)],
    )(
        place,
        *kept_out(queries_all, keys_all, values_all, earlier, first, scaled, residue),
        later,
        *kept_out(last),
    )
    back = swap(send)
    grads = call(
        merge_body,
        (pairs,),
        [((3, tok, DH), col)] * 2,
        [((tok, 2 * DH), lambda j, p: (0, j), (tok, width), BF)] * 3,
    )(place, *kept_out(keep), back)
    return (*(grad.reshape(1, tok, width) for grad in grads), weight_grad)


def solution(mesh):
    nz, nx, ny = mesh.shape["dp"], 4, mesh.shape["seq"] // 8
    grid = Mesh(mesh.devices.reshape(nz, nx, ny, 2), ("z", "x", "y", "c"))
    tokens = P("z", ("x", "y", "c"), None)
    weights = P(("z", "x", "y", "c"), None)
    return jax.shard_map(
        functools.partial(on_device, nx, ny, nz),
        mesh=grid,
        in_specs=(tokens, tokens, tokens, tokens, weights),
        out_specs=(tokens, tokens, tokens, weights),
        check_vma=False,
    )
```

time: 247 us -> 193 us (0.78)
  waiting for transfers between devices: 101 us -> 28.8 us
  Pallas kernels: 34.2 us -> 56.9 us
  starting transfers between devices: 29.3 us -> 48.3 us
  local copies, waits for them, and re-layouts: 18.6 us -> 1.61 us
  blocking collectives: 47.2 us -> 36.6 us
  other arithmetic: 0.64 us -> 4.06 us
    all_gather x2 -> x1, waiting for transfers between devices: 69 us -> 0.02 us  [on_device(): og_all = lax.all_gather(og, 'z', axis=0, tiled=True)]
    all_to_all x1, waiting for transfers between devices: 20.2 us -> 0.01 us  [on_device(): att_mine = lax.all_to_all(attended, 'z', 0, 0, tiled=True)]
    all_to_all x2 -> x1, blocking collectives: 33.7 us -> 13.8 us  [carried_in(): parts = lax.all_to_all(state, plane, 0, 0, tiled=True)]
    unnamed x40 -> x2, local copies, waits for them, and re-layouts: 18.6 us -> 0.01 us
    pallas_call x8 -> x7, Pallas kernels: 30.1 us -> 48.2 us  [the longest x1 9.74 us: on_device(): call(backward_body, (pairs,), [pair_spec] * 3 + [state_spec, state_spec,...]
    all_to_all x1 -> x2, waiting for transfers between devices: 0.01 us -> 13.3 us  [carried_in(): return lax.all_to_all(carried, plane, 0, 0, tiled=True)]
    all_to_all x1, blocking collectives: 13.5 us -> 22.7 us  [on_device(): grad_mine = lax.all_to_all(attn_grad, 'z', 0, 0, tiled=True)]
    ppermute x3 -> x6, starting transfers between devices: 4.91 us -> 13.6 us  [the longest x3 6.56 us: on_device(): k_other, v_other, q_other = (swap(k_in), swap(v_in), swap(q_in))]
  transfers between devices with their start and end apart: 11 -> 16, of which waited for: 9 -> 9; matrix products, arithmetic and copies ran while one was open for 0% -> 3% of each run, Pallas kernels for 13% -> 27%
where the time goes in v2:
time: 193 us; the launch traced here: 190 us
  Pallas kernels  56.9 us (29%)
  starting transfers between devices  48.3 us (25%)
  blocking collectives  36.6 us (19%)
  waiting for transfers between devices  28.8 us (15%)
  between operations  14.1 us (7%)
  other arithmetic  4.06 us (2%)
    all_to_all x1, blocking collectives, on_device(): grad_mine = lax.all_to_all(attn_grad, 'z', 0, 0, tiled=True)  22.7 us
    all_to_all x1, blocking collectives, carried_in(): parts = lax.all_to_all(state, plane, 0, 0, tiled=True)  13.8 us
    all_to_all x2, waiting for transfers between devices, carried_in(): return lax.all_to_all(carried, plane, 0, 0, tiled=True)  13.3 us
    pallas_call x1, Pallas kernels, on_device(): call(backward_body, (pairs,), [pair_spec] * 3 + [state_spec, state_spec,...  9.74 us
    all_to_all x1, starting transfers between devices, on_device(): att_mine = lax.all_to_all(attended, 'z', 0, 0, tiled=True)  8.54 us
    all_to_all x2, starting transfers between devices, carried_in(): return lax.all_to_all(carried, plane, 0, 0, tiled=True)  8.31 us
    pallas_call x1, Pallas kernels, on_device(): call(functools.partial(weight_body, steps), (2 * steps,), [att_spec, att_...  8.16 us
    pallas_call x1, Pallas kernels, on_device(): call(attn_grad_body, (nz,), [((tok, model), lambda k, p: (k, 0)), ((2 * D...  8.12 us
  transfers between devices with their start and end apart: 16, of which 9 were waited for; matrix products, arithmetic and copies ran while one was open for 3% of the time, Pallas kernels for 27%

profile of v2, /device:TPU:1, one launch (start us, length us, event | category | flops | bytes accessed | tf_op | source)
XLA Modules:
  0.0 190.3 jit_solution(17421192834486271197)
XLA Ops:
  7.9 3.3 %collective-permute-start.1 = (bf16[128,2048]{1,0:T(8,128)(2,1)}, bf16[128,2048]{1,0:T(8,128)(2,1)S(1)}, u32[]{:S(2)}, u32[]{:S(2)}) collective-permute-start(bf16[128,2048]{1,0:T(8,128)(2,1)} %bitcast.19), channel_id=1, source_target_pairs={{0,1},{1,0},{2,3},{3,2},{4,5},{5,4},{6,7},{7,6},{8,9},{9,8},{10,11... | collective-permute-start | bytes 1572872 | tf_op jit(solution)/shard_map/ppermute | solution.py:291
  11.3 1.6 broadcast_in_dim.2
  12.9 5.0 %all-to-all-start = ((bf16[16,8,2048]{2,1,0:T(8,128)(2,1)}), bf16[16,8,2048]{2,1,0:T(8,128)(2,1)S(1)}, u32[]{:S(2)}, u32[]{:S(2)}) async-start(bf16[16,8,2048]{2,1,0:T(8,128)(2,1)} %broadcast_in_dim.2), calls=%async_computation | async-start | bytes 1048576 | tf_op jit(solution)/shard_map/all_to_all | solution.py:313
  18.1 6.1 %shard_map.84 = (bf16[2,128,1024]{2,1,0:T(8,128)(2,1)}, bf16[2,128,1024]{2,1,0:T(8,128)(2,1)}, f32[16,72,128]{2,1,0:T(8,128)}, f32[16,72,128]{2,1,0:T(8,128)}) custom-call(s32[4]{0:T(128)S(1)} %pad_add_fusion.place, bf16[128,2048]{1,0:T(8,128)(2,1)} %bitcast.20, bf16[128,2048]{1,0:T(8,128)(2,1)} %bitcast.22, ...), custom_call_target="tpu_custom_call" | custom-call | tf_op jit(solution)/shard_map/pallas_call | solution.py:304
  24.1 4.2 %all-to-all-done = bf16[16,8,2048]{2,1,0:T(8,128)(2,1)S(1)} async-done(((bf16[16,8,2048]{2,1,0:T(8,128)(2,1)}), bf16[16,8,2048]{2,1,0:T(8,128)(2,1)S(1)}, u32[]{:S(2)}, u32[]{:S(2)}) %all-to-all-start) | async-done | bytes 524320 | tf_op jit(solution)/shard_map/all_to_all | solution.py:313
  28.3 13.8 %all_to_all.40.in_ref = f32[16,72,128]{2,1,0:T(8,128)S(1)} all-to-all(f32[16,72,128]{2,1,0:T(8,128)} %get-tuple-element.34), channel_id=1, replica_groups=mesh['z'=8,'x'=4,'y'=4,'c'=2] {'x','y'}, dimensions={0} | all-to-all | bytes 1179648 | tf_op jit(solution)/shard_map/all_to_all | solution.py:317
  43.6 3.6 %all-to-all-start.2 = ((f32[16,72,128]{2,1,0:T(8,128)}), f32[16,72,128]{2,1,0:T(8,128)S(1)}, u32[]{:S(2)}, u32[]{:S(2)}) async-start(f32[16,72,128]{2,1,0:T(8,128)} %shard_map.85), calls=%async_computation.2 | async-start | bytes 1179648 | tf_op jit(solution)/shard_map/all_to_all | solution.py:325
  47.2 3.1 %collective-permute-start = (bf16[128,2048]{1,0:T(8,128)(2,1)S(1)}, bf16[128,2048]{1,0:T(8,128)(2,1)S(1)}, u32[]{:S(2)}, u32[]{:S(2)}) collective-permute-start(bf16[128,2048]{1,0:T(8,128)(2,1)S(1)} %bitcast.25), channel_id=1, source_target_pairs={{0,1},{1,0},{2,3},{3,2},{4,5},{5,4},{6,7},{7,6},{8,9},{9,8},{10,11... | collective-permute-start | bytes 1572872 | tf_op jit(solution)/shard_map/ppermute | solution.py:291
  50.3 1.5 collective-permute-done.q_other
  51.8 4.7 %all-to-all-done.2.in_ref = f32[16,72,128]{2,1,0:T(8,128)S(1)} async-done(((f32[16,72,128]{2,1,0:T(8,128)}), f32[16,72,128]{2,1,0:T(8,128)S(1)}, u32[]{:S(2)}, u32[]{:S(2)}) %all-to-all-start.2) | async-done | bytes 589856 | tf_op jit(solution)/shard_map/all_to_all | solution.py:325
  56.6 7.7 %shard_map.86 = (bf16[2,128,1024]{2,1,0:T(8,128)(2,1)}, f32[16,72,128]{2,1,0:T(8,128)}, bf16[8,256,128]{2,1,0:T(8,128)(2,1)}, f32[2,128,1024]{2,1,0:T(8,128)}, f32[2,128,1024]{2,1,0:T(8,128)}) custom-call(s32[4]{0:T(128)S(1)} %pad_add_fusion.place, bf16[128,2048]{1,0:T(8,128)(2,1)} %bitcast.24, bf16[128,2048]{1,0:T(8,128)(2,1)S(1)} %collective-permute-done.q_other, ...), custom_call_target="tpu_custom_call" | custom-call | tf_op jit(solution)/shard_map/pallas_call | solution.py:328
  64.3 8.5 %all-to-all-start.3 = ((bf16[8,256,128]{2,1,0:T(8,128)(2,1)}), bf16[8,256,128]{2,1,0:T(8,128)(2,1)S(1)}, u32[]{:S(2)}, u32[]{:S(2)}) async-start(bf16[8,256,128]{2,1,0:T(8,128)(2,1)} %get-tuple-element.40), calls=%async_computation.3 | async-start | bytes 1048576 | tf_op jit(solution)/shard_map/all_to_all | solution.py:350
  72.8 4.1 %collective-permute-start.3 = (bf16[16,8,2048]{2,1,0:T(8,128)(2,1)S(1)}, bf16[16,8,2048]{2,1,0:T(8,128)(2,1)S(1)}, u32[]{:S(2)}, u32[]{:S(2)}) collective-permute-start(bf16[16,8,2048]{2,1,0:T(8,128)(2,1)S(1)} %all-to-all-done), channel_id=1, source_target_pairs={{0,1},{1,0},{2,3},{3,2},{4,5},{5,4},{6,7},{7,6},{8,9},{9,8},{10,11... | collective-permute-start | bytes 1572872 | tf_op jit(solution)/shard_map/ppermute | solution.py:338
  76.9 1.5 collective-permute-done.3
  78.6 8.1 %shard_map.87 = bf16[8,128,256]{2,1,0:T(8,128)(2,1)} custom-call(s32[4]{0:T(128)S(1)} %pad_add_fusion.place, bf16[1024,2048]{1,0:T(8,128)(2,1)} %bitcast.16, bf16[256,2048]{1,0:T(8,128)(2,1)S(1)} %bitcast.15), custom_call_target="tpu_custom_call" | custom-call | tf_op jit(solution)/shard_map/pallas_call | solution.py:344
  86.7 22.7 %all_to_all.41.grad_ref = bf16[8,128,256]{2,1,0:T(8,128)(2,1)S(1)} all-to-all(bf16[8,128,256]{2,1,0:T(8,128)(2,1)} %shard_map.87), channel_id=1, replica_groups=mesh['z'=8,'x'=4,'y'=4,'c'=2] {'z'}, dimensions={0} | all-to-all | bytes 1048576 | tf_op jit(solution)/shard_map/all_to_all | solution.py:352
  109.4 2.6 %collective-permute-start.4 = (bf16[8,128,256]{2,1,0:T(8,128)(2,1)S(1)}, bf16[8,128,256]{2,1,0:T(8,128)(2,1)S(1)}, u32[]{:S(2)}, u32[]{:S(2)}) collective-permute-start(bf16[8,128,256]{2,1,0:T(8,128)(2,1)S(1)} %all_to_all.41.grad_ref), channel_id=1, source_target_pairs={{0,1},{1,0},{2,3},{3,2},{4,5},{5,4},{6,7},{7,6},{8,9},{9,8},{10,11... | collective-permute-start | bytes 1572872 | tf_op jit(solution)/shard_map/ppermute | solution.py:353
  112.1 1.5 collective-permute-done.4.grad_other
  113.6 7.2 %shard_map.88 = (f32[2,128,1024]{2,1,0:T(8,128)}, f32[2,128,1024]{2,1,0:T(8,128)}, f32[16,72,128]{2,1,0:T(8,128)}, f32[16,72,128]{2,1,0:T(8,128)}) custom-call(s32[4]{0:T(128)S(1)} %pad_add_fusion.place, bf16[2,128,1024]{2,1,0:T(8,128)(2,1)} %get-tuple-element.36.queries, f32[2,128,1024]{2,1,0:T(8,128)} %get-tuple-element.38.o_ref, ...), custom_call_target="tpu_custom_call" | custom-call | tf_op jit(solution)/shard_map/pallas_call | solution.py:355
  120.8 3.6 %all-to-all-start.5 = ((f32[16,72,128]{2,1,0:T(8,128)}), f32[16,72,128]{2,1,0:T(8,128)S(1)}, u32[]{:S(2)}, u32[]{:S(2)}) async-start(f32[16,72,128]{2,1,0:T(8,128)} %get-tuple-element.46), calls=%async_computation.5 | async-start | bytes 1179648 | tf_op jit(solution)/shard_map/all_to_all | solution.py:317
  124.4 8.2 %shard_map.92 = (f32[256,1024]{1,0:T(8,128)}, f32[256,1024]{1,0:T(8,128)}) custom-call(s32[4]{0:T(128)S(1)} %pad_add_fusion.place, bf16[8,256,128]{2,1,0:T(8,128)(2,1)S(1)} %all-to-all-done.3.mine_ref, bf16[8,256,128]{2,1,0:T(8,128)(2,1)S(1)} %collective-permute-done.6.other_ref, bf16[1024,2048]{1,0:T(8,128)(2,1)} %bitcast.17), custom_call_target="tpu_custom_call" | custom-call | tf_op jit(solution)/shard_map/pallas_call | solution.py:366
  132.9 2.1 %all-to-all-done.5.in_ref = f32[16,72,128]{2,1,0:T(8,128)S(1)} async-done(((f32[16,72,128]{2,1,0:T(8,128)}), f32[16,72,128]{2,1,0:T(8,128)S(1)}, u32[]{:S(2)}, u32[]{:S(2)}) %all-to-all-start.5) | async-done | bytes 589856 | tf_op jit(solution)/shard_map/all_to_all | solution.py:317
  136.5 4.7 %all-to-all-start.6 = ((f32[16,72,128]{2,1,0:T(8,128)}), f32[16,72,128]{2,1,0:T(8,128)S(1)}, u32[]{:S(2)}, u32[]{:S(2)}) async-start(f32[16,72,128]{2,1,0:T(8,128)} %shard_map.89), calls=%async_computation.6 | async-start | bytes 1179648 | tf_op jit(solution)/shard_map/all_to_all | solution.py:325
  141.2 2.4 %add.3 = f32[256,1024]{1,0:T(8,128)} add(f32[256,1024]{1,0:T(8,128)} %get-tuple-element.54, f32[256,1024]{1,0:T(8,128)S(1)} %collective-permute-done.7) | non-fusion elementwise | flops 262144 | bytes 3145728 | tf_op jit(solution)/shard_map/add | solution.py:383
  143.6 8.6 %all-to-all-done.6.later_ref = f32[16,72,128]{2,1,0:T(8,128)S(1)} async-done(((f32[16,72,128]{2,1,0:T(8,128)}), f32[16,72,128]{2,1,0:T(8,128)S(1)}, u32[]{:S(2)}, u32[]{:S(2)}) %all-to-all-start.6) | async-done | bytes 589856 | tf_op jit(solution)/shard_map/all_to_all | solution.py:325
  152.2 3.7 %all-to-all-start.7 = ((f32[16,16,1024]{2,1,0:T(8,128)}), f32[16,16,1024]{2,1,0:T(8,128)S(1)}, u32[]{:S(2)}, u32[]{:S(2)}) async-start(f32[16,16,1024]{2,1,0:T(8,128)} %bitcast.14), calls=%async_computation.7 | async-start | bytes 2097152 | tf_op jit(solution)/shard_map/all_to_all | solution.py:385
  155.8 9.7 %shard_map.90 = (bf16[3,128,1024]{2,1,0:T(8,128)(2,1)}, bf16[3,128,1024]{2,1,0:T(8,128)(2,1)}) custom-call(s32[4]{0:T(128)S(1)} %pad_add_fusion.place, bf16[2,128,1024]{2,1,0:T(8,128)(2,1)} %get-tuple-element.36.queries, bf16[2,128,1024]{2,1,0:T(8,128)(2,1)} %get-tuple-element.31.keys, bf16[2,128,1024]{2,1,0:T(8,128)(2,1)} %get-tuple-element.32.values, ...), custom_call_target="tpu_custom_call" | custom-call | tf_op jit(solution)/shard_map/pallas_call | solution.py:401
  165.6 2.2 %collective-permute-start.5 = (bf16[3,128,1024]{2,1,0:T(8,128)(2,1)}, bf16[3,128,1024]{2,1,0:T(8,128)(2,1)S(1)}, u32[]{:S(2)}, u32[]{:S(2)}) collective-permute-start(bf16[3,128,1024]{2,1,0:T(8,128)(2,1)} %get-tuple-element.49), channel_id=1, source_target_pairs={{0,1},{1,0},{2,3},{3,2},{4,5},{5,4},{6,7},{7,6},{8,9},{9,8},{10,11... | collective-permute-start | bytes 2359304 | tf_op jit(solution)/shard_map/ppermute | solution.py:414
  167.8 2.8 %all-to-all-done.7.in_ref = f32[16,16,1024]{2,1,0:T(8,128)S(1)} async-done(((f32[16,16,1024]{2,1,0:T(8,128)}), f32[16,16,1024]{2,1,0:T(8,128)S(1)}, u32[]{:S(2)}, u32[]{:S(2)}) %all-to-all-start.7) | async-done | bytes 1048608 | tf_op jit(solution)/shard_map/all_to_all | solution.py:385
  171.8 3.3 %collective-permute-start.8 = (f32[8,1024]{1,0:T(8,128)}, f32[8,1024]{1,0:T(8,128)S(1)}, u32[]{:S(2)}, u32[]{:S(2)}) collective-permute-start(f32[8,1024]{1,0:T(8,128)} %get-tuple-element.57), channel_id=1, source_target_pairs={{0,1},{1,0},{2,3},{3,2},{4,5},{5,4},{6,7},{7,6},{8,9},{9,8},{10,11... | collective-permute-start | bytes 98312 | tf_op jit(solution)/shard_map/ppermute | solution.py:395
  176.2 1.5 maximum_select_fusion.1
  177.6 5.9 %shard_map.91 = (bf16[128,2048]{1,0:T(8,128)(2,1)}, bf16[128,2048]{1,0:T(8,128)(2,1)}, bf16[128,2048]{1,0:T(8,128)(2,1)}) custom-call(s32[4]{0:T(128)S(1)} %pad_add_fusion.place, bf16[3,128,1024]{2,1,0:T(8,128)(2,1)} %get-tuple-element.48.keep_ref, bf16[3,128,1024]{2,1,0:T(8,128)(2,1)S(1)} %collective-permute-done.5.back_ref), custom_call_target="tpu_custom_call" | custom-call | tf_op jit(solution)/shard_map/pallas_call | solution.py:415
  (20 shorter events, 6.5 us)
Async XLA Ops:
  7.2 40.0 %copy-start = (bf16[1,128,2048]{2,1,0:T(8,128)(2,1)S(1)}, bf16[1,128,2048]{2,1,0:T(8,128)(2,1)}, u32[]{:S(2)}) copy-start(bf16[1,128,2048]{2,1,0:T(8,128)(2,1)} %param.5) | copy-start | bytes 1572868
  7.2 71.4 %all-gather.3.cloned.1.call-start = ((), (), s32[]{:S(2)}) async-start(), calls=%async_computation.8 | async-start | bytes 4718592 | tf_op jit(solution)/shard_map/all_gather | solution.py:292
  7.9 10.1 %collective-permute-start.1 = (bf16[128,2048]{1,0:T(8,128)(2,1)}, bf16[128,2048]{1,0:T(8,128)(2,1)S(1)}, u32[]{:S(2)}, u32[]{:S(2)}) collective-permute-start(bf16[128,2048]{1,0:T(8,128)(2,1)} %bitcast.19), channel_id=1, source_target_pairs={{0,1},{1,0},{2,3},{3,2},{4,5},{5,4},{6,7},{7,6},{8,9},{9,8},{10,11... | collective-permute-start | bytes 1572872 | tf_op jit(solution)/shard_map/ppermute | solution.py:291
  11.2 6.8 %collective-permute-start.2 = (bf16[128,2048]{1,0:T(8,128)(2,1)}, bf16[128,2048]{1,0:T(8,128)(2,1)S(1)}, u32[]{:S(2)}, u32[]{:S(2)}) collective-permute-start(bf16[128,2048]{1,0:T(8,128)(2,1)} %bitcast.21), channel_id=1, source_target_pairs={{0,1},{1,0},{2,3},{3,2},{4,5},{5,4},{6,7},{7,6},{8,9},{9,8},{10,11... | collective-permute-start | bytes 1572872 | tf_op jit(solution)/shard_map/ppermute | solution.py:291
  12.9 15.4 %all-to-all-start = ((bf16[16,8,2048]{2,1,0:T(8,128)(2,1)}), bf16[16,8,2048]{2,1,0:T(8,128)(2,1)S(1)}, u32[]{:S(2)}, u32[]{:S(2)}) async-start(bf16[16,8,2048]{2,1,0:T(8,128)(2,1)} %broadcast_in_dim.2), calls=%async_computation | async-start | bytes 1048576 | tf_op jit(solution)/shard_map/all_to_all | solution.py:313
  43.6 13.0 %all-to-all-start.2 = ((f32[16,72,128]{2,1,0:T(8,128)}), f32[16,72,128]{2,1,0:T(8,128)S(1)}, u32[]{:S(2)}, u32[]{:S(2)}) async-start(f32[16,72,128]{2,1,0:T(8,128)} %shard_map.85), calls=%async_computation.2 | async-start | bytes 1179648 | tf_op jit(solution)/shard_map/all_to_all | solution.py:325
  47.2 4.7 %collective-permute-start = (bf16[128,2048]{1,0:T(8,128)(2,1)S(1)}, bf16[128,2048]{1,0:T(8,128)(2,1)S(1)}, u32[]{:S(2)}, u32[]{:S(2)}) collective-permute-start(bf16[128,2048]{1,0:T(8,128)(2,1)S(1)} %bitcast.25), channel_id=1, source_target_pairs={{0,1},{1,0},{2,3},{3,2},{4,5},{5,4},{6,7},{7,6},{8,9},{9,8},{10,11... | collective-permute-start | bytes 1572872 | tf_op jit(solution)/shard_map/ppermute | solution.py:291
  64.3 22.4 %all-to-all-start.3 = ((bf16[8,256,128]{2,1,0:T(8,128)(2,1)}), bf16[8,256,128]{2,1,0:T(8,128)(2,1)S(1)}, u32[]{:S(2)}, u32[]{:S(2)}) async-start(bf16[8,256,128]{2,1,0:T(8,128)(2,1)} %get-tuple-element.40), calls=%async_computation.3 | async-start | bytes 1048576 | tf_op jit(solution)/shard_map/all_to_all | solution.py:350
  72.8 5.6 %collective-permute-start.3 = (bf16[16,8,2048]{2,1,0:T(8,128)(2,1)S(1)}, bf16[16,8,2048]{2,1,0:T(8,128)(2,1)S(1)}, u32[]{:S(2)}, u32[]{:S(2)}) collective-permute-start(bf16[16,8,2048]{2,1,0:T(8,128)(2,1)S(1)} %all-to-all-done), channel_id=1, source_target_pairs={{0,1},{1,0},{2,3},{3,2},{4,5},{5,4},{6,7},{7,6},{8,9},{9,8},{10,11... | collective-permute-start | bytes 1572872 | tf_op jit(solution)/shard_map/ppermute | solution.py:338
  109.4 4.2 %collective-permute-start.4 = (bf16[8,128,256]{2,1,0:T(8,128)(2,1)S(1)}, bf16[8,128,256]{2,1,0:T(8,128)(2,1)S(1)}, u32[]{:S(2)}, u32[]{:S(2)}) collective-permute-start(bf16[8,128,256]{2,1,0:T(8,128)(2,1)S(1)} %all_to_all.41.grad_ref), channel_id=1, source_target_pairs={{0,1},{1,0},{2,3},{3,2},{4,5},{5,4},{6,7},{7,6},{8,9},{9,8},{10,11... | collective-permute-start | bytes 1572872 | tf_op jit(solution)/shard_map/ppermute | solution.py:353
  112.1 12.3 %collective-permute-start.6 = (bf16[8,256,128]{2,1,0:T(8,128)(2,1)S(1)}, bf16[8,256,128]{2,1,0:T(8,128)(2,1)S(1)}, u32[]{:S(2)}, u32[]{:S(2)}) collective-permute-start(bf16[8,256,128]{2,1,0:T(8,128)(2,1)S(1)} %all-to-all-done.3.mine_ref), channel_id=1, source_target_pairs={{0,1},{1,0},{2,3},{3,2},{4,5},{5,4},{6,7},{7,6},{8,9},{9,8},{10,11... | collective-permute-start | bytes 1572872 | tf_op jit(solution)/shard_map/ppermute | solution.py:363
  120.8 14.3 %all-to-all-start.5 = ((f32[16,72,128]{2,1,0:T(8,128)}), f32[16,72,128]{2,1,0:T(8,128)S(1)}, u32[]{:S(2)}, u32[]{:S(2)}) async-start(f32[16,72,128]{2,1,0:T(8,128)} %get-tuple-element.46), calls=%async_computation.5 | async-start | bytes 1179648 | tf_op jit(solution)/shard_map/all_to_all | solution.py:317
  132.5 8.6 %collective-permute-start.7 = (f32[256,1024]{1,0:T(8,128)}, f32[256,1024]{1,0:T(8,128)S(1)}, u32[]{:S(2)}, u32[]{:S(2)}) collective-permute-start(f32[256,1024]{1,0:T(8,128)} %get-tuple-element.55), channel_id=1, source_target_pairs={{0,1},{1,0},{2,3},{3,2},{4,5},{5,4},{6,7},{7,6},{8,9},{9,8},{10,11... | collective-permute-start | bytes 3145736 | tf_op jit(solution)/shard_map/ppermute | solution.py:383
  136.5 15.7 %all-to-all-start.6 = ((f32[16,72,128]{2,1,0:T(8,128)}), f32[16,72,128]{2,1,0:T(8,128)S(1)}, u32[]{:S(2)}, u32[]{:S(2)}) async-start(f32[16,72,128]{2,1,0:T(8,128)} %shard_map.89), calls=%async_computation.6 | async-start | bytes 1179648 | tf_op jit(solution)/shard_map/all_to_all | solution.py:325
  152.2 18.4 %all-to-all-start.7 = ((f32[16,16,1024]{2,1,0:T(8,128)}), f32[16,16,1024]{2,1,0:T(8,128)S(1)}, u32[]{:S(2)}, u32[]{:S(2)}) async-start(f32[16,16,1024]{2,1,0:T(8,128)} %bitcast.14), calls=%async_computation.7 | async-start | bytes 2097152 | tf_op jit(solution)/shard_map/all_to_all | solution.py:385
  165.6 12.0 %collective-permute-start.5 = (bf16[3,128,1024]{2,1,0:T(8,128)(2,1)}, bf16[3,128,1024]{2,1,0:T(8,128)(2,1)S(1)}, u32[]{:S(2)}, u32[]{:S(2)}) collective-permute-start(bf16[3,128,1024]{2,1,0:T(8,128)(2,1)} %get-tuple-element.49), channel_id=1, source_target_pairs={{0,1},{1,0},{2,3},{3,2},{4,5},{5,4},{6,7},{7,6},{8,9},{9,8},{10,11... | collective-permute-start | bytes 2359304 | tf_op jit(solution)/shard_map/ppermute | solution.py:414
  171.8 4.4 %collective-permute-start.8 = (f32[8,1024]{1,0:T(8,128)}, f32[8,1024]{1,0:T(8,128)S(1)}, u32[]{:S(2)}, u32[]{:S(2)}) collective-permute-start(f32[8,1024]{1,0:T(8,128)} %get-tuple-element.57), channel_id=1, source_target_pairs={{0,1},{1,0},{2,3},{3,2},{4,5},{5,4},{6,7},{7,6},{8,9},{9,8},{10,11... | collective-permute-start | bytes 98312 | tf_op jit(solution)/shard_map/ppermute | solution.py:395
Sparse Core Ops, SparseCore 0:
  9.8 58.6 all-gather.2

commit v3 on v2

v3 whole, which is shorter than its diff:
```python
import functools

import jax
import jax.numpy as jnp
from jax import lax
from jax.experimental import pallas as pl
from jax.experimental.pallas import tpu as pltpu
from jax.sharding import Mesh, PartitionSpec as P

DH = 128
BLK = 128
BF = jnp.bfloat16
F32 = jnp.float32
NN = (((1,), (0,)), ((), ()))
NT = (((1,), (1,)), ((), ()))
TN = (((0,), (0,)), ((), ()))
HALF = DH // 2
ROWS = HALF + 8
PARAMS = pltpu.CompilerParams(vmem_limit_bytes=24 * 1024 * 1024)


def dot(left, right, dims):
    return lax.dot_general(left, right, dims, preferred_element_type=F32)


def split(wide):
    high = wide.astype(BF)
    return high, (wide - high.astype(F32)).astype(BF)


def feature(raw):
    return jnp.where(raw > 0, raw + 1.0, jnp.exp(jnp.minimum(raw, 0.0)))


def feature_slope(raw):
    return jnp.where(raw > 0, 1.0, jnp.exp(jnp.minimum(raw, 0.0)))


def features_of(raw):
    return feature(raw.astype(F32)).astype(BF)


def causal_mask():
    row = lax.broadcasted_iota(jnp.int32, (BLK, BLK), 0)
    col = lax.broadcasted_iota(jnp.int32, (BLK, BLK), 1)
    return row >= col


def state_of(ref, head):
    low, high = 2 * head, 2 * head + 1
    matrix = jnp.concatenate([ref[low, :HALF], ref[high, :HALF]], axis=0)
    return matrix, ref[low, HALF : HALF + 1]


def put_state(ref, head, matrix, vector):
    tail = jnp.broadcast_to(vector, (8, DH))
    for half in range(2):
        ref[2 * head + half, :HALF] = matrix[half * HALF : (half + 1) * HALF]
        ref[2 * head + half, HALF:ROWS] = tail


def call(body, grid, ins, outs, scratch=()):
    run = pl.pallas_call(
        body,
        grid_spec=pltpu.PrefetchScalarGridSpec(
            num_scalar_prefetch=1,
            grid=grid,
            in_specs=[pl.BlockSpec(*spec[:2], memory_space=(spec[2:] or (None,))[0]) for spec in ins],
            out_specs=[pl.BlockSpec(spec[0], spec[1]) for spec in outs],
            scratch_shapes=list(scratch),
        ),
        out_shape=[pltpu.HBM(spec[2], spec[3]) for spec in outs],
        compiler_params=PARAMS,
    )

    return run


def kept_out(*arrays):
    return [pltpu.with_memory_space_constraint(array, pltpu.HBM) for array in arrays]


def put_pair(ref, head, core, mine, other):
    cols = pl.ds(pl.multiple_of((2 * head + core) * DH, DH), DH)
    ref[head, core] = mine[:, cols]
    ref[head, 1 - core] = other[:, cols]


def local_body(place, k_ref, v_ref, k_other, v_other, keys, values, sum_ref, first_ref):
    for head in range(keys.shape[0]):
        put_pair(keys, head, place[0], k_ref, k_other)
        put_pair(values, head, place[0], v_ref, v_other)
    for head in range(keys.shape[0]):
        feats = [features_of(keys[head, block]) for block in range(2)]
        states = [dot(feats[block], values[head, block], TN) for block in range(2)]
        norms = [jnp.sum(feat.astype(F32), axis=0, keepdims=True) for feat in feats]
        put_state(first_ref, head, states[0], norms[0])
        put_state(sum_ref, head, states[0] + states[1], norms[0] + norms[1])


def scan_body(place, in_ref, out_ref):
    count = in_ref.shape[0]
    so_far = jnp.zeros(in_ref.shape[1:], F32)
    for position in range(count):
        out_ref[position] = so_far
        so_far = so_far + in_ref[position]


def back_scan_body(place, in_ref, out_ref):
    count = in_ref.shape[0]
    so_far = jnp.zeros(in_ref.shape[1:], F32)
    for position in range(count - 1, -1, -1):
        out_ref[position] = so_far
        so_far = so_far + in_ref[position]


def total_body(place, in_ref, keep_ref, send_ref):
    total = in_ref[0].astype(F32)
    for position in range(1, in_ref.shape[0]):
        total = total + in_ref[position].astype(F32)
    low, high = total[:8], total[8:]
    keep_ref[...] = jnp.where(place[0] == 0, low, high)
    send_ref[...] = jnp.where(place[0] == 0, high, low)


def attn_grad_body(count, place, *refs):
    *og_refs, w_ref, out_ref, tokens, arrived = refs
    copies, start = [], 0
    for position, ref in enumerate(og_refs):
        here = tokens.at[pl.ds(start, ref.shape[0])]
        copies.append(pltpu.make_async_copy(ref, here, arrived.at[position]))
        copies[-1].start()
        start += ref.shape[0]
    batch = count // 2
    for first, waits in ((0, copies[:batch]), (batch, copies[batch:])):
        for copy in waits:
            copy.wait()
        part = dot(tokens[first * BLK : (first + batch) * BLK], w_ref[...], NT).astype(BF)
        for more in range(batch):
            out_ref[lax.rem(place[3] + first + more, count)] = part[more * BLK : (more + 1) * BLK]


def forward_body(
    place,
    q_ref,
    q_other,
    keys,
    values,
    in_ref,
    first_ref,
    queries,
    copy_ref,
    att_ref,
    o_ref,
    den_ref,
):
    copy_ref[...] = in_ref[...]
    causal = causal_mask()
    for head in range(keys.shape[0]):
        put_pair(queries, head, place[0], q_ref, q_other)
    for head in range(keys.shape[0]):
        state, norm = state_of(in_ref, head)
        extra, extra_norm = state_of(first_ref, head)
        for block in range(2):
            if block == 1:
                state, norm = state + extra, norm + extra_norm
            q_feat = features_of(queries[head, block])
            k_feat = features_of(keys[head, block])
            scores = jnp.where(causal, dot(q_feat, k_feat, NT), 0.0)
            den = jnp.sum(scores, axis=1, keepdims=True) + jnp.sum(
                q_feat.astype(F32) * norm, axis=1, keepdims=True
            )
            high, low = split(state)
            out = (
                dot(scores.astype(BF), values[head, block], NN)
                + dot(q_feat, high, NN)
                + dot(q_feat, low, NN)
            ) / den
            att_ref[head, block * BLK : (block + 1) * BLK] = out.astype(BF)
            o_ref[head, block] = out
            den_ref[head, block] = jnp.broadcast_to(den, (BLK, DH))


def scaled_body(
    place,
    queries,
    o_ref,
    den_ref,
    grad_ref,
    grad_other,
    g_ref,
    r_ref,
    sum_ref,
    last_ref,
    grads,
):
    me = place[0]
    cols = pl.ds(pl.multiple_of(me * DH, DH), DH)
    for head in range(queries.shape[0]):
        grads[head, me] = grad_ref[head, :, cols]
        grads[head, 1 - me] = grad_other[head, :, cols]
    for head in range(queries.shape[0]):
        sums, norms = [], []
        for block in range(2):
            q_feat = features_of(queries[head, block])
            scaled = grads[head, block].astype(F32) / den_ref[head, block]
            g_ref[head, block] = scaled
            residue = -jnp.sum(scaled * o_ref[head, block], axis=1, keepdims=True)
            r_ref[head, block] = jnp.broadcast_to(residue, (BLK, DH))
            high, low = split(scaled)
            sums.append(dot(q_feat, high, TN) + dot(q_feat, low, TN))
            norms.append(jnp.sum(residue * q_feat.astype(F32), axis=0, keepdims=True))
        put_state(last_ref, head, sums[1], norms[1])
        put_state(sum_ref, head, sums[0] + sums[1], norms[0] + norms[1])


def backward_body(
    place,
    queries,
    keys,
    values,
    in_ref,
    first_ref,
    g_ref,
    r_ref,
    later_ref,
    last_ref,
    keep_ref,
    send_ref,
    held,
):
    me = place[0]
    causal = causal_mask()
    for head in range(keys.shape[0]):
        state0, norm0 = state_of(in_ref, head)
        extra, extra_norm = state_of(first_ref, head)
        grad1, weight1 = state_of(later_ref, head)
        after, after_norm = state_of(last_ref, head)
        states = (state0, state0 + extra)
        norms = (norm0, norm0 + extra_norm)
        grads = (grad1 + after, grad1)
        weights = (weight1 + after_norm, weight1)
        for block in range(2):
            q_raw = queries[head, block].astype(F32)
            k_raw = keys[head, block].astype(F32)
            v_full = values[head, block]
            q_feat, k_feat = feature(q_raw).astype(BF), feature(k_raw).astype(BF)
            scaled, residue = g_ref[head, block], r_ref[head, block]
            g_high, g_low = split(scaled)
            s_high, s_low = split(states[block])
            grad_high, grad_low = split(grads[block])
            scores = jnp.where(causal, dot(q_feat, k_feat, NT), 0.0).astype(BF)
            mixed = jnp.where(causal, dot(g_high, v_full, NT) + residue, 0.0).astype(BF)
            q_grad = (
                dot(mixed, k_feat, NN)
                + (dot(g_high, s_high, NT) + dot(g_high, s_low, NT) + dot(g_low, s_high, NT))
                + residue * norms[block]
            )
            k_grad = (
                dot(mixed, q_feat, TN)
                + (dot(v_full, grad_high, NT) + dot(v_full, grad_low, NT))
                + weights[block]
            )
            v_grad = dot(scores, g_high, TN) + (
                dot(k_feat, grad_high, NN) + dot(k_feat, grad_low, NN)
            )
            held[block, head, 0] = (q_grad * feature_slope(q_raw)).astype(BF)
            held[block, head, 1] = (k_grad * feature_slope(k_raw)).astype(BF)
            held[block, head, 2] = v_grad.astype(BF)
    keep_ref[...] = held[me]
    send_ref[...] = held[1 - me]


def merge_body(place, keep_ref, back_ref, q_ref, k_ref, v_ref):
    for head in range(keep_ref.shape[0]):
        mine = pl.ds(pl.multiple_of((2 * head + place[0]) * DH, DH), DH)
        other = pl.ds(pl.multiple_of((2 * head + 1 - place[0]) * DH, DH), DH)
        for part, ref in enumerate((q_ref, k_ref, v_ref)):
            ref[:, mine] = keep_ref[head, part]
            ref[:, other] = back_ref[head, part]


def weight_body(steps, count, place, mine_ref, other_ref, *refs):
    *og_refs, send_ref, keep_ref, heads = refs
    left = pl.ds(pl.multiple_of(place[0] * DH, DH), DH)
    right = pl.ds(pl.multiple_of((1 - place[0]) * DH, DH), DH)

    @pl.when(pl.program_id(0) == 0)
    def _():
        for ahead in range(count):
            source = lax.rem(place[3] + ahead, count)
            heads[ahead * BLK : (ahead + 1) * BLK, left] = mine_ref[source]
            heads[ahead * BLK : (ahead + 1) * BLK, right] = other_ref[source]

    right_side = jnp.concatenate([ref[...] for ref in og_refs], axis=0)
    part = dot(heads[...], right_side, TN)

    @pl.when(pl.program_id(0) < steps)
    def _():
        send_ref[...] = part

    @pl.when(pl.program_id(0) >= steps)
    def _():
        keep_ref[...] = part


def on_device(nx, ny, nz, queries, keys, values, out_grad, out_weight):
    chips = nx * ny
    tok, width = queries.shape[1:]
    pairs = width // (2 * DH)
    model = out_grad.shape[2]
    half = model // 2
    me = lax.axis_index("c")
    place = jnp.stack([lax.axis_index(name) for name in ("c", "x", "y", "z")]).astype(jnp.int32)
    q_in, k_in, v_in, og = (
        part.reshape(tok, part.shape[2]) for part in (queries, keys, values, out_grad)
    )
    swap = functools.partial(lax.ppermute, axis_name="c", perm=[(0, 1), (1, 0)])
    plane = ("x", "y")

    def from_ahead(piece, axis, size, ahead):
        return lax.ppermute(piece, axis, [((i + ahead) % size, i) for i in range(size)])

    k_other, v_other, q_other = swap(k_in), swap(v_in), swap(q_in)

    def both_ways(up, down):
        return from_ahead(up, "z", nz, 1), from_ahead(down, "z", nz, -1)

    og_1, og_7 = both_ways(og, og)
    og_2, og_6 = both_ways(og_1, og_7)
    og_3, og_5 = both_ways(og_2, og_6)
    low, high = both_ways(og_3[: tok // 2], og_5[tok // 2 :])
    og_all = kept_out(og, og_1, og_2, og_3, low, high, og_5, og_6, og_7)

    heads = 2
    grid = (pairs // heads,)
    lead = lambda j, p: (j, 0, 0)
    lead4 = lambda j, p: (j, 0, 0, 0)
    state_spec = ((2 * heads, ROWS, DH), lead)
    state_out = (*state_spec, (2 * pairs, ROWS, DH), F32)
    pair_spec = ((heads, 2, tok, DH), lead4)
    pair_out = (*pair_spec, (pairs, 2, tok, DH), F32)
    both_out = (*pair_spec, (pairs, 2, tok, DH), BF)
    head_spec = ((tok, 2 * heads * DH), lambda j, p: (0, j))
    whole = lambda *shape: (shape, lambda j, p: (0,) * len(shape))

    keys_all, values_all, local_sum, first = call(
        local_body, grid, [head_spec] * 4, [both_out, both_out, state_out, state_out]
    )(place, *kept_out(k_in, v_in), k_other, v_other)
    keys_all, values_all, first = kept_out(keys_all, values_all, first)

    out_weight = lax.optimization_barrier((out_weight, local_sum))[0]

    def fetched(piece, axis, size):
        return [from_ahead(piece, axis, size, ahead) for ahead in range(1, size)]

    def gathered(piece, fetched_parts, start):
        size = len(fetched_parts) + 1
        whole = jnp.broadcast_to(piece[None], (size, *piece.shape))
        for ahead, part in enumerate(fetched_parts, start=1):
            place = lax.rem(start + ahead, size)
            whole = lax.dynamic_update_index_in_dim(whole, part, place, 0)
        return whole

    row_group = gathered(out_weight, fetched(out_weight, "y", ny), lax.axis_index("y"))
    row_groups = fetched(row_group, "x", nx)

    parts = lax.all_to_all(local_sum, plane, 0, 0, tiled=True)
    earlier = call(
        scan_body,
        (1,),
        [whole(chips, ROWS, DH)],
        [(*whole(chips, ROWS, DH), (chips, ROWS, DH), F32)],
    )(place, parts)[0]
    earlier = lax.all_to_all(earlier, plane, 0, 0, tiled=True)
    queries_all, earlier, attended, outputs, dens = call(
        forward_body,
        grid,
        [head_spec] * 2 + [pair_spec] * 2 + [state_spec] * 2,
        [both_out, state_out]
        + [((heads, 2 * tok, DH), lead, (pairs, 2 * tok, DH), BF), pair_out, pair_out],
    )(place, *kept_out(q_in), q_other, keys_all, values_all, earlier, first)
    row_groups = lax.optimization_barrier((row_groups, attended))[0]
    rows_mine = gathered(row_group, row_groups, lax.axis_index("x")).reshape(chips, 8, model)
    rows_other = swap(rows_mine)
    rows = jnp.where(
        me == 0,
        jnp.stack([rows_mine, rows_other], axis=1),
        jnp.stack([rows_other, rows_mine], axis=1),
    ).reshape(2 * DH, model)
    att_mine = lax.all_to_all(attended, "z", 0, 0, tiled=True)
    att_other = swap(att_mine)

    attn_grad = call(
        functools.partial(attn_grad_body, nz),
        (1,),
        [(None, None, pl.ANY)] * len(og_all) + [whole(2 * DH, model)],
        [(*whole(nz, tok, 2 * DH), (nz, tok, 2 * DH), BF)],
        [pltpu.VMEM((nz * tok, model), BF), pltpu.SemaphoreType.DMA((len(og_all),))],
    )(place, *og_all, rows)[0]
    attn_grad, att_mine = lax.optimization_barrier((attn_grad, att_mine))
    grad_mine = lax.all_to_all(attn_grad, "z", 0, 0, tiled=True)

    steps = 2
    cols = half // steps
    att_spec = ((nz, tok, DH), lambda j, p: (0, p[0], 0))
    og_col = lambda j, p: (0, jnp.where(j < steps, 1 - p[0], p[0]) * steps + lax.rem(j, steps))
    moved, kept = call(
        functools.partial(weight_body, steps, nz),
        (2 * steps,),
        [att_spec] * 2 + [((part.shape[0], cols), og_col) for part in og_all],
        [
            ((2 * DH, cols), lambda j, p: (0, jnp.minimum(j, steps - 1)), (2 * DH, half), F32),
            ((2 * DH, cols), lambda j, p: (0, jnp.maximum(j - steps, 0)), (2 * DH, half), F32),
        ],
        [pltpu.VMEM((nz * tok, 2 * DH), BF)],
    )(place, att_mine, att_other, *og_all)
    grad_mine, moved, kept = lax.optimization_barrier((grad_mine, moved, kept))
    grad_other = swap(grad_mine)
    got = swap(moved)

    grad_spec = ((heads, tok, 2 * DH), lead)
    scaled, residue, grad_sum, last = call(
        scaled_body,
        grid,
        [pair_spec] * 3 + [grad_spec] * 2,
        [pair_out, pair_out, state_out, state_out],
        [pltpu.VMEM((heads, 2, tok, DH), BF)],
    )(
        place,
        *kept_out(queries_all, outputs, dens),
        *(grad_mine, grad_other),
    )
    parts = lax.all_to_all(grad_sum, plane, 0, 0, tiled=True)
    later = call(
        back_scan_body,
        (1,),
        [whole(chips, ROWS, DH)],
        [(*whole(chips, ROWS, DH), (chips, ROWS, DH), F32)],
    )(place, parts)[0]
    later = lax.all_to_all(later, plane, 0, 0, tiled=True)
    shares = (kept + got).astype(BF).reshape(chips, 2 * DH // chips, half)
    later, shares = lax.optimization_barrier((later, shares))
    shares = lax.all_to_all(shares, plane, 0, 0, tiled=True)
    grad_out = ((heads, 3, tok, DH), lead4, (pairs, 3, tok, DH), BF)
    keep, send = call(
        backward_body,
        grid,
        [pair_spec] * 3
        + [state_spec, state_spec, pair_spec, pair_spec, state_spec, state_spec],
        [grad_out] * 2,
        [pltpu.VMEM((2, heads, 3, tok, DH), BF)],
    )(
        place,
        *kept_out(queries_all, keys_all, values_all, earlier, first, scaled, residue),
        later,
        *kept_out(last),
    )
    send, shares = lax.optimization_barrier((send, shares))
    back = swap(send)
    weight_kept, weight_moved = call(
        total_body,
        (1,),
        [whole(*shares.shape)],
        [(*whole(8, half), (8, half), F32)] * 2,
    )(place, shares)
    weight_got = swap(weight_moved)
    weight_grad = jnp.where(
        me == 0,
        jnp.concatenate([weight_kept, weight_got], axis=1),
        jnp.concatenate([weight_got, weight_kept], axis=1),
    )
    grads = call(
        merge_body,
        grid,
        [grad_out[:2]] * 2,
        [(*head_spec, (tok, width), BF)] * 3,
    )(place, *kept_out(keep), back)
    return (*(grad.reshape(1, tok, width) for grad in grads), weight_grad)


def solution(mesh):
    nz, nx, ny = mesh.shape["dp"], 4, mesh.shape["seq"] // 8
    grid = Mesh(mesh.devices.reshape(nz, nx, ny, 2), ("z", "x", "y", "c"))
    tokens = P("z", ("x", "y", "c"), None)
    weights = P(("z", "x", "y", "c"), None)
    return jax.shard_map(
        functools.partial(on_device, nx, ny, nz),
        mesh=grid,
        in_specs=(tokens, tokens, tokens, tokens, weights),
        out_specs=(tokens, tokens, tokens, weights),
        check_vma=False,
    )
```

time: 193 us -> 172 us (0.89)
  blocking collectives: 36.6 us -> 15.3 us
  waiting for transfers between devices: 28.8 us -> 44.6 us
  Pallas kernels: 56.9 us -> 42.6 us
  starting transfers between devices: 48.3 us -> 62.5 us
  between operations: 14.1 us -> 0.85 us
    ppermute x1 -> x15, starting transfers between devices: 0.37 us -> 22.6 us  [the longest x14 22.6 us: from_ahead(): lax.ppermute(piece, axis, [((i + ahead) % size, i) for i in range(size)])]
    all_to_all x2 -> x1, blocking collectives: 36.6 us -> 15.3 us  [on_device(): parts = lax.all_to_all(grad_sum, plane, 0, 0, tiled=True)]
    pallas_call x10, Pallas kernels: 56.9 us -> 42.6 us  [the longest x1 7.62 us: on_device(): call(backward_body, grid, [pair_spec] * 3 + [state_spec, state_spec, pair...]
    ppermute x1 -> x15, waiting for transfers between devices: 0.01 us -> 12.1 us  [the longest x14 10.7 us: from_ahead(): lax.ppermute(piece, axis, [((i + ahead) % size, i) for i in range(size)])]
    all_to_all x5, waiting for transfers between devices: 22.4 us -> 28.8 us  [the longest x1 9.56 us: on_device(): later = lax.all_to_all(later, plane, 0, 0, tiled=True)]
    all_to_all x1, starting transfers between devices: 8.54 us -> 4.59 us  [on_device(): att_mine = lax.all_to_all(attended, 'z', 0, 0, tiled=True)]
    ppermute x1, starting transfers between devices: 3.3 us -> 0.02 us  [on_device(): got = swap(moved)]
    add x1 -> x0, other arithmetic: 2.41 us -> none  [on_device(): partial = kept + swap(moved)]
  transfers between devices with their start and end apart: 16 -> 29, of which waited for: 9 -> 10; matrix products, arithmetic and copies ran while one was open for 3% -> 3% of each run, Pallas kernels for 27% -> 23%
where the time goes in v3:
time: 172 us; the launch traced here: 171 us
  starting transfers between devices  62.5 us (36%)
  waiting for transfers between devices  44.6 us (26%)
  Pallas kernels  42.6 us (25%)
  blocking collectives  15.3 us (9%)
  local copies, waits for them, and re-layouts  2.64 us (2%)
  other arithmetic  2.58 us (2%)
    ppermute x14, starting transfers between devices, from_ahead(): lax.ppermute(piece, axis, [((i + ahead) % size, i) for i in range(size)])  22.6 us
    all_to_all x1, blocking collectives, on_device(): parts = lax.all_to_all(grad_sum, plane, 0, 0, tiled=True)  15.3 us
    ppermute x14, waiting for transfers between devices, from_ahead(): lax.ppermute(piece, axis, [((i + ahead) % size, i) for i in range(size)])  10.7 us
    all_to_all x1, waiting for transfers between devices, on_device(): later = lax.all_to_all(later, plane, 0, 0, tiled=True)  9.56 us
    all_to_all x1, waiting for transfers between devices, on_device(): grad_mine = lax.all_to_all(attn_grad, 'z', 0, 0, tiled=True)  9.18 us
    pallas_call x1, Pallas kernels, on_device(): call(backward_body, grid, [pair_spec] * 3 + [state_spec, state_spec, pair...  7.62 us
    pallas_call x1, Pallas kernels, on_device(): call(functools.partial(weight_body, steps, nz), (2 * steps,), [att_spec]...  6.23 us
    ppermute x1, starting transfers between devices, on_device(): rows_other = swap(rows_mine)  5.79 us
  transfers between devices with their start and end apart: 29, of which 10 were waited for; matrix products, arithmetic and copies ran while one was open for 3% of the time, Pallas kernels for 23%

profile of v3, /device:TPU:1, one launch (start us, length us, event | category | flops | bytes accessed | tf_op | source)
XLA Modules:
  0.0 171.0 jit_solution(7214313180246609276)
XLA Ops:
  0.6 3.3 %collective-permute-start.1 = (bf16[128,2048]{1,0:T(8,128)(2,1)}, bf16[128,2048]{1,0:T(8,128)(2,1)S(1)}, u32[]{:S(2)}, u32[]{:S(2)}) collective-permute-start(bf16[128,2048]{1,0:T(8,128)(2,1)} %bitcast.35), channel_id=1, source_target_pairs={{0,1},{1,0},{2,3},{3,2},{4,5},{5,4},{6,7},{7,6},{8,9},{9,8},{10,11... | collective-permute-start | bytes 1572872 | tf_op jit(solution)/shard_map/ppermute | solution.py:324
  4.1 3.8 %collective-permute-start.3 = (bf16[128,2048]{1,0:T(8,128)(2,1)}, bf16[128,2048]{1,0:T(8,128)(2,1)S(1)}, u32[]{:S(2)}, u32[]{:S(2)}) collective-permute-start(bf16[128,2048]{1,0:T(8,128)(2,1)} %bitcast.31), channel_id=1, source_target_pairs={{32,0},{64,32},{96,64},{128,96},{160,128},{192,160},{224,192},{0,2... | collective-permute-start | bytes 1572872 | tf_op jit(solution)/shard_map/ppermute | solution.py:322
  8.0 4.5 %shard_map.84 = (bf16[8,2,128,128]{3,2,1,0:T(8,128)(2,1)}, bf16[8,2,128,128]{3,2,1,0:T(8,128)(2,1)}, f32[16,72,128]{2,1,0:T(8,128)}, f32[16,72,128]{2,1,0:T(8,128)}) custom-call(s32[4]{0:T(128)S(1)} %pad_add_fusion.place, bf16[128,2048]{1,0:T(8,128)(2,1)} %bitcast.36, bf16[128,2048]{1,0:T(8,128)(2,1)} %bitcast.38, ...), custom_call_target="tpu_custom_call" | custom-call | tf_op jit(solution)/shard_map/pallas_call | solution.py:347
  12.5 2.8 %collective-permute-start.11 = (bf16[8,2048]{1,0:T(8,128)(2,1)S(1)}, bf16[8,2048]{1,0:T(8,128)(2,1)S(1)}, u32[]{:S(2)}, u32[]{:S(2)}) collective-permute-start(bf16[8,2048]{1,0:T(8,128)(2,1)S(1)} %copy-done.8), channel_id=1, source_target_pairs={{2,0},{4,2},{6,4},{0,6},{3,1},{5,3},{7,5},{1,7},{10,8},{12,10},{14... | collective-permute-start | bytes 98312 | tf_op jit(solution)/shard_map/ppermute | solution.py:322
  16.3 4.3 %all-to-all-start = ((f32[16,72,128]{2,1,0:T(8,128)}), f32[16,72,128]{2,1,0:T(8,128)S(1)}, u32[]{:S(2)}, u32[]{:S(2)}) async-start(f32[16,72,128]{2,1,0:T(8,128)} %get-tuple-element.41), calls=%async_computation | async-start | bytes 1179648 | tf_op jit(solution)/shard_map/all_to_all | solution.py:368
  20.6 2.9 %collective-permute-start.12 = (bf16[8,2048]{1,0:T(8,128)(2,1)S(1)}, bf16[8,2048]{1,0:T(8,128)(2,1)S(1)}, u32[]{:S(2)}, u32[]{:S(2)}) collective-permute-start(bf16[8,2048]{1,0:T(8,128)(2,1)S(1)} %copy-done.8), channel_id=1, source_target_pairs={{4,0},{6,2},{0,4},{2,6},{5,1},{7,3},{1,5},{3,7},{12,8},{14,10},{8,... | collective-permute-start | bytes 98312 | tf_op jit(solution)/shard_map/ppermute | solution.py:322
  23.8 3.0 %collective-permute-start.4 = (bf16[128,2048]{1,0:T(8,128)(2,1)S(1)}, bf16[128,2048]{1,0:T(8,128)(2,1)}, u32[]{:S(2)}, u32[]{:S(2)}) collective-permute-start(bf16[128,2048]{1,0:T(8,128)(2,1)S(1)} %collective-permute-done.3.refs_1_), channel_id=1, source_target_pairs={{32,0},{64,32},{96,64},{128,96},{160,128},{192,160},{224,192},{0,2... | collective-permute-start | bytes 1572872 | tf_op jit(solution)/shard_map/ppermute | solution.py:322
  26.8 4.6 %all-to-all-done.in_ref = f32[16,72,128]{2,1,0:T(8,128)S(1)} async-done(((f32[16,72,128]{2,1,0:T(8,128)}), f32[16,72,128]{2,1,0:T(8,128)S(1)}, u32[]{:S(2)}, u32[]{:S(2)}) %all-to-all-start) | async-done | bytes 589856 | tf_op jit(solution)/shard_map/all_to_all | solution.py:368
  32.8 5.0 %all-to-all-start.1 = ((f32[16,72,128]{2,1,0:T(8,128)}), f32[16,72,128]{2,1,0:T(8,128)S(1)}, u32[]{:S(2)}, u32[]{:S(2)}) async-start(f32[16,72,128]{2,1,0:T(8,128)} %shard_map.85), calls=%async_computation.1 | async-start | bytes 1179648 | tf_op jit(solution)/shard_map/all_to_all | solution.py:375
  37.8 2.7 %collective-permute-start.14 = (bf16[4,8,2048]{2,1,0:T(8,128)(2,1)S(1)}, bf16[4,8,2048]{2,1,0:T(8,128)(2,1)S(1)}, u32[]{:S(2)}, u32[]{:S(2)}) collective-permute-start(bf16[4,8,2048]{2,1,0:T(8,128)(2,1)S(1)} %bitcast_dynamic-update-slice_fusion.3), channel_id=1, source_target_pairs={{8,0},{16,8},{24,16},{0,24},{9,1},{17,9},{25,17},{1,25},{10,2},{18... | collective-permute-start | bytes 393224 | tf_op jit(solution)/shard_map/ppermute | solution.py:322
  41.6 3.0 %collective-permute-start.5 = (bf16[128,2048]{1,0:T(8,128)(2,1)}, bf16[128,2048]{1,0:T(8,128)(2,1)S(1)}, u32[]{:S(2)}, u32[]{:S(2)}) collective-permute-start(bf16[128,2048]{1,0:T(8,128)(2,1)} %collective-permute-done.4.refs_2_), channel_id=1, source_target_pairs={{32,0},{64,32},{96,64},{128,96},{160,128},{192,160},{224,192},{0,2... | collective-permute-start | bytes 1572872 | tf_op jit(solution)/shard_map/ppermute | solution.py:322
  44.6 3.8 %all-to-all-done.1.in_ref = f32[16,72,128]{2,1,0:T(8,128)S(1)} async-done(((f32[16,72,128]{2,1,0:T(8,128)}), f32[16,72,128]{2,1,0:T(8,128)S(1)}, u32[]{:S(2)}, u32[]{:S(2)}) %all-to-all-start.1) | async-done | bytes 589856 | tf_op jit(solution)/shard_map/all_to_all | solution.py:375
  48.4 5.6 %shard_map.86 = (bf16[8,2,128,128]{3,2,1,0:T(8,128)(2,1)}, f32[16,72,128]{2,1,0:T(8,128)}, bf16[8,256,128]{2,1,0:T(8,128)(2,1)}, f32[8,2,128,128]{3,2,1,0:T(8,128)}, f32[8,2,128,128]{3,2,1,0:T(8,128)}) custom-call(s32[4]{0:T(128)S(1)} %pad_add_fusion.place, bf16[128,2048]{1,0:T(8,128)(2,1)} %bitcast.40, bf16[128,2048]{1,0:T(8,128)(2,1)S(1)} %collective-permute-done.q_other, ...), custom_call_target="tpu_custom_call" | custom-call | tf_op jit(solution)/shard_map/pallas_call | solution.py:376
  54.1 4.6 %all-to-all-start.2 = ((bf16[8,256,128]{2,1,0:T(8,128)(2,1)}), bf16[8,256,128]{2,1,0:T(8,128)(2,1)S(1)}, u32[]{:S(2)}, u32[]{:S(2)}) async-start(bf16[8,256,128]{2,1,0:T(8,128)(2,1)} %get-tuple-element.48), calls=%async_computation.2 | async-start | bytes 1048576 | tf_op jit(solution)/shard_map/all_to_all | solution.py:391
  59.7 5.8 %collective-permute-start.17 = (bf16[16,8,2048]{2,1,0:T(8,128)(2,1)S(1)}, bf16[16,8,2048]{2,1,0:T(8,128)(2,1)S(1)}, u32[]{:S(2)}, u32[]{:S(2)}) collective-permute-start(bf16[16,8,2048]{2,1,0:T(8,128)(2,1)S(1)} %bitcast.29), channel_id=1, source_target_pairs={{0,1},{1,0},{2,3},{3,2},{4,5},{5,4},{6,7},{7,6},{8,9},{9,8},{10,11... | collective-permute-start | bytes 1572872 | tf_op jit(solution)/shard_map/ppermute | solution.py:385
  65.5 3.0 %collective-permute-start.6 = (bf16[64,2048]{1,0:T(8,128)(2,1)S(1)}, bf16[64,2048]{1,0:T(8,128)(2,1)S(1)}, u32[]{:S(2)}, u32[]{:S(2)}) collective-permute-start(bf16[64,2048]{1,0:T(8,128)(2,1)S(1)} %slice.8), channel_id=1, source_target_pairs={{32,0},{64,32},{96,64},{128,96},{160,128},{192,160},{224,192},{0,2... | collective-permute-start | bytes 786440 | tf_op jit(solution)/shard_map/ppermute | solution.py:322
  69.5 7.5 %collective-permute-done.6.refs_4_ = bf16[64,2048]{1,0:T(8,128)(2,1)S(1)} collective-permute-done((bf16[64,2048]{1,0:T(8,128)(2,1)S(1)}, bf16[64,2048]{1,0:T(8,128)(2,1)S(1)}, u32[]{:S(2)}, u32[]{:S(2)}) %collective-permute-start.6) | collective-permute-done | bytes 262176 | tf_op jit(solution)/shard_map/ppermute | solution.py:322
  77.0 3.2 %collective-permute-done.10.refs_5_ = bf16[64,2048]{1,0:T(8,128)(2,1)S(1)} collective-permute-done((bf16[64,2048]{1,0:T(8,128)(2,1)}, bf16[64,2048]{1,0:T(8,128)(2,1)S(1)}, u32[]{:S(2)}, u32[]{:S(2)}) %collective-permute-start.10) | collective-permute-done | bytes 262176 | tf_op jit(solution)/shard_map/ppermute | solution.py:322
  80.9 5.5 %shard_map.87 = bf16[8,128,256]{2,1,0:T(8,128)(2,1)} custom-call(s32[4]{0:T(128)S(1)} %pad_add_fusion.place, bf16[128,2048]{1,0:T(8,128)(2,1)} %bitcast.33, bf16[128,2048]{1,0:T(8,128)(2,1)} %copy-done.2, bf16[128,2048]{1,0:T(8,128)(2,1)} %collective-permute-done.4.refs_2_, bf16[128,2048]{1,0:T(8,128)(2,1)} %copy-done, bf16[64,2048]{1,0:T(8,128)(2,1)} %copy-done.5, ...), custom_call_target="tpu_custom_call" | custom-call | tf_op jit(solution)/shard_map/pallas_call | solution.py:394
  86.4 3.8 %all-to-all-start.3 = ((bf16[8,128,256]{2,1,0:T(8,128)(2,1)}), bf16[8,128,256]{2,1,0:T(8,128)(2,1)S(1)}, u32[]{:S(2)}, u32[]{:S(2)}) async-start(bf16[8,128,256]{2,1,0:T(8,128)(2,1)} %shard_map.87), calls=%async_computation.3 | async-start | bytes 1048576 | tf_op jit(solution)/shard_map/all_to_all | solution.py:402
  92.8 6.2 %shard_map.88 = (f32[256,1024]{1,0:T(8,128)}, f32[256,1024]{1,0:T(8,128)}) custom-call(s32[4]{0:T(128)S(1)} %pad_add_fusion.place, bf16[8,256,128]{2,1,0:T(8,128)(2,1)S(1)} %all-to-all-done.2.mine_ref, bf16[8,256,128]{2,1,0:T(8,128)(2,1)S(1)} %collective-permute-done.18.other_ref, bf16[128,2048]{1,0:T(8,128)(2,1)} %bitcast.34, bf16[128,2048]{1,0:T(8,128)(2,1)} %copy-done.2, ...), custom_call_target="tpu_custom_call" | custom-call | tf_op jit(solution)/shard_map/pallas_call | solution.py:408
  99.0 9.2 %all-to-all-done.3.grad_ref = bf16[8,128,256]{2,1,0:T(8,128)(2,1)S(1)} async-done(((bf16[8,128,256]{2,1,0:T(8,128)(2,1)}), bf16[8,128,256]{2,1,0:T(8,128)(2,1)S(1)}, u32[]{:S(2)}, u32[]{:S(2)}) %all-to-all-start.3) | async-done | bytes 524320 | tf_op jit(solution)/shard_map/all_to_all | solution.py:402
  108.7 2.1 %collective-permute-done.19.grad_other = bf16[8,128,256]{2,1,0:T(8,128)(2,1)S(1)} collective-permute-done((bf16[8,128,256]{2,1,0:T(8,128)(2,1)S(1)}, bf16[8,128,256]{2,1,0:T(8,128)(2,1)S(1)}, u32[]{:S(2)}, u32[]{:S(2)}) %collective-permute-start.19) | collective-permute-done | bytes 524320 | tf_op jit(solution)/shard_map/ppermute | solution.py:419
  110.8 5.0 %shard_map.89 = (f32[8,2,128,128]{3,2,1,0:T(8,128)}, f32[8,2,128,128]{3,2,1,0:T(8,128)}, f32[16,72,128]{2,1,0:T(8,128)}, f32[16,72,128]{2,1,0:T(8,128)}) custom-call(s32[4]{0:T(128)S(1)} %pad_add_fusion.place, bf16[8,2,128,128]{3,2,1,0:T(8,128)(2,1)} %get-tuple-element.43.queries, f32[8,2,128,128]{3,2,1,0:T(8,128)} %get-tuple-element.45.o_ref, ...), custom_call_target="tpu_custom_call" | custom-call | tf_op jit(solution)/shard_map/pallas_call | solution.py:423
  115.8 15.3 %all_to_all.35.in_ref = f32[16,72,128]{2,1,0:T(8,128)S(1)} all-to-all(f32[16,72,128]{2,1,0:T(8,128)} %get-tuple-element.59), channel_id=1, replica_groups=mesh['z'=8,'x'=4,'y'=4,'c'=2] {'x','y'}, dimensions={0} | all-to-all | bytes 1179648 | tf_op jit(solution)/shard_map/all_to_all | solution.py:434
  132.5 3.6 %all-to-all-start.5 = ((f32[16,72,128]{2,1,0:T(8,128)}), f32[16,72,128]{2,1,0:T(8,128)S(1)}, u32[]{:S(2)}, u32[]{:S(2)}) async-start(f32[16,72,128]{2,1,0:T(8,128)} %shard_map.90), calls=%async_computation.5 | async-start | bytes 1179648 | tf_op jit(solution)/shard_map/all_to_all | solution.py:441
  137.1 9.6 %all-to-all-done.5.later_ref = f32[16,72,128]{2,1,0:T(8,128)S(1)} async-done(((f32[16,72,128]{2,1,0:T(8,128)}), f32[16,72,128]{2,1,0:T(8,128)S(1)}, u32[]{:S(2)}, u32[]{:S(2)}) %all-to-all-start.5) | async-done | bytes 589856 | tf_op jit(solution)/shard_map/all_to_all | solution.py:441
  146.6 3.7 %all-to-all-start.6 = ((bf16[16,16,1024]{2,1,0:T(8,128)(2,1)}), bf16[16,16,1024]{2,1,0:T(8,128)(2,1)S(1)}, u32[]{:S(2)}, u32[]{:S(2)}) async-start(bf16[16,16,1024]{2,1,0:T(8,128)(2,1)} %bitcast.18), calls=%async_computation.6 | async-start | bytes 1048576 | tf_op jit(solution)/shard_map/all_to_all | solution.py:444
  150.3 7.6 %shard_map.91 = (bf16[8,3,128,128]{3,2,1,0:T(8,128)(2,1)}, bf16[8,3,128,128]{3,2,1,0:T(8,128)(2,1)}) custom-call(s32[4]{0:T(128)S(1)} %pad_add_fusion.place, bf16[8,2,128,128]{3,2,1,0:T(8,128)(2,1)} %get-tuple-element.43.queries, bf16[8,2,128,128]{3,2,1,0:T(8,128)(2,1)} %get-tuple-element.39.keys, bf16[8,2,128,128]{3,2,1,0:T(8,128)(2,1)} %get-tuple-element.40.values, ...), custom_call_target="tpu_custom_call" | custom-call | tf_op jit(solution)/shard_map/pallas_call | solution.py:446
  158.0 1.6 all-to-all-done.6.in_ref
  159.6 3.3 %collective-permute-start.21 = (bf16[8,3,128,128]{3,2,1,0:T(8,128)(2,1)}, bf16[8,3,128,128]{3,2,1,0:T(8,128)(2,1)S(1)}, u32[]{:S(2)}, u32[]{:S(2)}) collective-permute-start(bf16[8,3,128,128]{3,2,1,0:T(8,128)(2,1)} %get-tuple-element.67), channel_id=1, source_target_pairs={{0,1},{1,0},{2,3},{3,2},{4,5},{5,4},{6,7},{7,6},{8,9},{9,8},{10,11... | collective-permute-start | bytes 2359304 | tf_op jit(solution)/shard_map/ppermute | solution.py:460
  167.0 4.0 %shard_map.92 = (bf16[128,2048]{1,0:T(8,128)(2,1)}, bf16[128,2048]{1,0:T(8,128)(2,1)}, bf16[128,2048]{1,0:T(8,128)(2,1)}) custom-call(s32[4]{0:T(128)S(1)} %pad_add_fusion.place, bf16[8,3,128,128]{3,2,1,0:T(8,128)(2,1)} %get-tuple-element.64.keep_ref, bf16[8,3,128,128]{3,2,1,0:T(8,128)(2,1)S(1)} %collective-permute-done.21.back_ref), custom_call_target="tpu_custom_call" | custom-call | tf_op jit(solution)/shard_map/pallas_call | solution.py:473
  (69 shorter events, 16.3 us)
Async XLA Ops:
  0.6 7.4 %collective-permute-start.1 = (bf16[128,2048]{1,0:T(8,128)(2,1)}, bf16[128,2048]{1,0:T(8,128)(2,1)S(1)}, u32[]{:S(2)}, u32[]{:S(2)}) collective-permute-start(bf16[128,2048]{1,0:T(8,128)(2,1)} %bitcast.35), channel_id=1, source_target_pairs={{0,1},{1,0},{2,3},{3,2},{4,5},{5,4},{6,7},{7,6},{8,9},{9,8},{10,11... | collective-permute-start | bytes 1572872 | tf_op jit(solution)/shard_map/ppermute | solution.py:324
  4.0 4.0 %collective-permute-start.2 = (bf16[128,2048]{1,0:T(8,128)(2,1)}, bf16[128,2048]{1,0:T(8,128)(2,1)S(1)}, u32[]{:S(2)}, u32[]{:S(2)}) collective-permute-start(bf16[128,2048]{1,0:T(8,128)(2,1)} %bitcast.37), channel_id=1, source_target_pairs={{0,1},{1,0},{2,3},{3,2},{4,5},{5,4},{6,7},{7,6},{8,9},{9,8},{10,11... | collective-permute-start | bytes 1572872 | tf_op jit(solution)/shard_map/ppermute | solution.py:324
  4.1 19.4 %collective-permute-start.3 = (bf16[128,2048]{1,0:T(8,128)(2,1)}, bf16[128,2048]{1,0:T(8,128)(2,1)S(1)}, u32[]{:S(2)}, u32[]{:S(2)}) collective-permute-start(bf16[128,2048]{1,0:T(8,128)(2,1)} %bitcast.31), channel_id=1, source_target_pairs={{32,0},{64,32},{96,64},{128,96},{160,128},{192,160},{224,192},{0,2... | collective-permute-start | bytes 1572872 | tf_op jit(solution)/shard_map/ppermute | solution.py:322
  7.9 15.9 %collective-permute-start.7 = (bf16[128,2048]{1,0:T(8,128)(2,1)}, bf16[128,2048]{1,0:T(8,128)(2,1)S(1)}, u32[]{:S(2)}, u32[]{:S(2)}) collective-permute-start(bf16[128,2048]{1,0:T(8,128)(2,1)} %bitcast.32), channel_id=1, source_target_pairs={{224,0},{0,32},{32,64},{64,96},{96,128},{128,160},{160,192},{192,2... | collective-permute-start | bytes 1572872 | tf_op jit(solution)/shard_map/ppermute | solution.py:322
  8.0 7.4 %copy-start.7 = (bf16[1,128,2048]{2,1,0:T(8,128)(2,1)S(1)}, bf16[1,128,2048]{2,1,0:T(8,128)(2,1)}, u32[]{:S(2)}) copy-start(bf16[1,128,2048]{2,1,0:T(8,128)(2,1)} %param.5) | copy-start | bytes 1572868
  12.5 14.2 %collective-permute-start.11 = (bf16[8,2048]{1,0:T(8,128)(2,1)S(1)}, bf16[8,2048]{1,0:T(8,128)(2,1)S(1)}, u32[]{:S(2)}, u32[]{:S(2)}) collective-permute-start(bf16[8,2048]{1,0:T(8,128)(2,1)S(1)} %copy-done.8), channel_id=1, source_target_pairs={{2,0},{4,2},{6,4},{0,6},{3,1},{5,3},{7,5},{1,7},{10,8},{12,10},{14... | collective-permute-start | bytes 98312 | tf_op jit(solution)/shard_map/ppermute | solution.py:322
  15.3 25.7 %collective-permute-start = (bf16[128,2048]{1,0:T(8,128)(2,1)S(1)}, bf16[128,2048]{1,0:T(8,128)(2,1)S(1)}, u32[]{:S(2)}, u32[]{:S(2)}) collective-permute-start(bf16[128,2048]{1,0:T(8,128)(2,1)S(1)} %bitcast.41), channel_id=1, source_target_pairs={{0,1},{1,0},{2,3},{3,2},{4,5},{5,4},{6,7},{7,6},{8,9},{9,8},{10,11... | collective-permute-start | bytes 1572872 | tf_op jit(solution)/shard_map/ppermute | solution.py:324
  16.3 15.1 %all-to-all-start = ((f32[16,72,128]{2,1,0:T(8,128)}), f32[16,72,128]{2,1,0:T(8,128)S(1)}, u32[]{:S(2)}, u32[]{:S(2)}) async-start(f32[16,72,128]{2,1,0:T(8,128)} %get-tuple-element.41), calls=%async_computation | async-start | bytes 1179648 | tf_op jit(solution)/shard_map/all_to_all | solution.py:368
  20.6 6.2 %collective-permute-start.12 = (bf16[8,2048]{1,0:T(8,128)(2,1)S(1)}, bf16[8,2048]{1,0:T(8,128)(2,1)S(1)}, u32[]{:S(2)}, u32[]{:S(2)}) collective-permute-start(bf16[8,2048]{1,0:T(8,128)(2,1)S(1)} %copy-done.8), channel_id=1, source_target_pairs={{4,0},{6,2},{0,4},{2,6},{5,1},{7,3},{1,5},{3,7},{12,8},{14,10},{8,... | collective-permute-start | bytes 98312 | tf_op jit(solution)/shard_map/ppermute | solution.py:322
  23.5 9.3 %copy-start.2 = (bf16[128,2048]{1,0:T(8,128)(2,1)}, bf16[128,2048]{1,0:T(8,128)(2,1)S(1)}, u32[]{:S(2)}) copy-start(bf16[128,2048]{1,0:T(8,128)(2,1)S(1)} %collective-permute-done.3.refs_1_) | copy-start | bytes 1572868
  23.5 14.3 %collective-permute-start.13 = (bf16[8,2048]{1,0:T(8,128)(2,1)S(1)}, bf16[8,2048]{1,0:T(8,128)(2,1)S(1)}, u32[]{:S(2)}, u32[]{:S(2)}) collective-permute-start(bf16[8,2048]{1,0:T(8,128)(2,1)S(1)} %copy-done.8), channel_id=1, source_target_pairs={{6,0},{0,2},{2,4},{4,6},{7,1},{1,3},{3,5},{5,7},{14,8},{8,10},{10,... | collective-permute-start | bytes 98312 | tf_op jit(solution)/shard_map/ppermute | solution.py:322
  23.8 9.0 %copy-start.3 = (bf16[128,2048]{1,0:T(8,128)(2,1)}, bf16[128,2048]{1,0:T(8,128)(2,1)S(1)}, u32[]{:S(2)}) copy-start(bf16[128,2048]{1,0:T(8,128)(2,1)S(1)} %collective-permute-done.7.refs_8_) | copy-start | bytes 1572868
  23.8 17.9 %collective-permute-start.4 = (bf16[128,2048]{1,0:T(8,128)(2,1)S(1)}, bf16[128,2048]{1,0:T(8,128)(2,1)}, u32[]{:S(2)}, u32[]{:S(2)}) collective-permute-start(bf16[128,2048]{1,0:T(8,128)(2,1)S(1)} %collective-permute-done.3.refs_1_), channel_id=1, source_target_pairs={{32,0},{64,32},{96,64},{128,96},{160,128},{192,160},{224,192},{0,2... | collective-permute-start | bytes 1572872 | tf_op jit(solution)/shard_map/ppermute | solution.py:322
  26.7 17.9 %collective-permute-start.8 = (bf16[128,2048]{1,0:T(8,128)(2,1)S(1)}, bf16[128,2048]{1,0:T(8,128)(2,1)}, u32[]{:S(2)}, u32[]{:S(2)}) collective-permute-start(bf16[128,2048]{1,0:T(8,128)(2,1)S(1)} %collective-permute-done.7.refs_8_), channel_id=1, source_target_pairs={{224,0},{0,32},{32,64},{64,96},{96,128},{128,160},{160,192},{192,2... | collective-permute-start | bytes 1572872 | tf_op jit(solution)/shard_map/ppermute | solution.py:322
  32.8 15.6 %all-to-all-start.1 = ((f32[16,72,128]{2,1,0:T(8,128)}), f32[16,72,128]{2,1,0:T(8,128)S(1)}, u32[]{:S(2)}, u32[]{:S(2)}) async-start(f32[16,72,128]{2,1,0:T(8,128)} %shard_map.85), calls=%async_computation.1 | async-start | bytes 1179648 | tf_op jit(solution)/shard_map/all_to_all | solution.py:375
  37.8 20.9 %collective-permute-start.14 = (bf16[4,8,2048]{2,1,0:T(8,128)(2,1)S(1)}, bf16[4,8,2048]{2,1,0:T(8,128)(2,1)S(1)}, u32[]{:S(2)}, u32[]{:S(2)}) collective-permute-start(bf16[4,8,2048]{2,1,0:T(8,128)(2,1)S(1)} %bitcast_dynamic-update-slice_fusion.3), channel_id=1, source_target_pairs={{8,0},{16,8},{24,16},{0,24},{9,1},{17,9},{25,17},{1,25},{10,2},{18... | collective-permute-start | bytes 393224 | tf_op jit(solution)/shard_map/ppermute | solution.py:322
  40.5 18.2 %collective-permute-start.15 = (bf16[4,8,2048]{2,1,0:T(8,128)(2,1)S(1)}, bf16[4,8,2048]{2,1,0:T(8,128)(2,1)}, u32[]{:S(2)}, u32[]{:S(2)}) collective-permute-start(bf16[4,8,2048]{2,1,0:T(8,128)(2,1)S(1)} %bitcast_dynamic-update-slice_fusion.3), channel_id=1, source_target_pairs={{16,0},{24,8},{0,16},{8,24},{17,1},{25,9},{1,17},{9,25},{18,2},{26... | collective-permute-start | bytes 393224 | tf_op jit(solution)/shard_map/ppermute | solution.py:322
  41.1 17.6 %collective-permute-start.16 = (bf16[4,8,2048]{2,1,0:T(8,128)(2,1)S(1)}, bf16[4,8,2048]{2,1,0:T(8,128)(2,1)S(1)}, u32[]{:S(2)}, u32[]{:S(2)}) collective-permute-start(bf16[4,8,2048]{2,1,0:T(8,128)(2,1)S(1)} %bitcast_dynamic-update-slice_fusion.3), channel_id=1, source_target_pairs={{24,0},{0,8},{8,16},{16,24},{25,1},{1,9},{9,17},{17,25},{26,2},{2,... | collective-permute-start | bytes 393224 | tf_op jit(solution)/shard_map/ppermute | solution.py:322
  41.6 23.9 %collective-permute-start.5 = (bf16[128,2048]{1,0:T(8,128)(2,1)}, bf16[128,2048]{1,0:T(8,128)(2,1)S(1)}, u32[]{:S(2)}, u32[]{:S(2)}) collective-permute-start(bf16[128,2048]{1,0:T(8,128)(2,1)} %collective-permute-done.4.refs_2_), channel_id=1, source_target_pairs={{32,0},{64,32},{96,64},{128,96},{160,128},{192,160},{224,192},{0,2... | collective-permute-start | bytes 1572872 | tf_op jit(solution)/shard_map/ppermute | solution.py:322
  44.6 24.0 %collective-permute-start.9 = (bf16[128,2048]{1,0:T(8,128)(2,1)}, bf16[128,2048]{1,0:T(8,128)(2,1)S(1)}, u32[]{:S(2)}, u32[]{:S(2)}) collective-permute-start(bf16[128,2048]{1,0:T(8,128)(2,1)} %collective-permute-done.8.refs_7_), channel_id=1, source_target_pairs={{224,0},{0,32},{32,64},{64,96},{96,128},{128,160},{160,192},{192,2... | collective-permute-start | bytes 1572872 | tf_op jit(solution)/shard_map/ppermute | solution.py:322
  54.1 32.3 %all-to-all-start.2 = ((bf16[8,256,128]{2,1,0:T(8,128)(2,1)}), bf16[8,256,128]{2,1,0:T(8,128)(2,1)S(1)}, u32[]{:S(2)}, u32[]{:S(2)}) async-start(bf16[8,256,128]{2,1,0:T(8,128)(2,1)} %get-tuple-element.48), calls=%async_computation.2 | async-start | bytes 1048576 | tf_op jit(solution)/shard_map/all_to_all | solution.py:391
  59.7 9.7 %collective-permute-start.17 = (bf16[16,8,2048]{2,1,0:T(8,128)(2,1)S(1)}, bf16[16,8,2048]{2,1,0:T(8,128)(2,1)S(1)}, u32[]{:S(2)}, u32[]{:S(2)}) collective-permute-start(bf16[16,8,2048]{2,1,0:T(8,128)(2,1)S(1)} %bitcast.29), channel_id=1, source_target_pairs={{0,1},{1,0},{2,3},{3,2},{4,5},{5,4},{6,7},{7,6},{8,9},{9,8},{10,11... | collective-permute-start | bytes 1572872 | tf_op jit(solution)/shard_map/ppermute | solution.py:385
  65.5 11.5 %collective-permute-start.6 = (bf16[64,2048]{1,0:T(8,128)(2,1)S(1)}, bf16[64,2048]{1,0:T(8,128)(2,1)S(1)}, u32[]{:S(2)}, u32[]{:S(2)}) collective-permute-start(bf16[64,2048]{1,0:T(8,128)(2,1)S(1)} %slice.8), channel_id=1, source_target_pairs={{32,0},{64,32},{96,64},{128,96},{160,128},{192,160},{224,192},{0,2... | collective-permute-start | bytes 786440 | tf_op jit(solution)/shard_map/ppermute | solution.py:322
  69.4 10.8 %collective-permute-start.10 = (bf16[64,2048]{1,0:T(8,128)(2,1)}, bf16[64,2048]{1,0:T(8,128)(2,1)S(1)}, u32[]{:S(2)}, u32[]{:S(2)}) collective-permute-start(bf16[64,2048]{1,0:T(8,128)(2,1)} %slice.9), channel_id=1, source_target_pairs={{224,0},{0,32},{32,64},{64,96},{96,128},{128,160},{160,192},{192,2... | collective-permute-start | bytes 786440 | tf_op jit(solution)/shard_map/ppermute | solution.py:322
  86.4 21.8 %all-to-all-start.3 = ((bf16[8,128,256]{2,1,0:T(8,128)(2,1)}), bf16[8,128,256]{2,1,0:T(8,128)(2,1)S(1)}, u32[]{:S(2)}, u32[]{:S(2)}) async-start(bf16[8,128,256]{2,1,0:T(8,128)(2,1)} %shard_map.87), calls=%async_computation.3 | async-start | bytes 1048576 | tf_op jit(solution)/shard_map/all_to_all | solution.py:402
  90.2 2.5 %collective-permute-start.18 = (bf16[8,256,128]{2,1,0:T(8,128)(2,1)S(1)}, bf16[8,256,128]{2,1,0:T(8,128)(2,1)S(1)}, u32[]{:S(2)}, u32[]{:S(2)}) collective-permute-start(bf16[8,256,128]{2,1,0:T(8,128)(2,1)S(1)} %all-to-all-done.2.mine_ref), channel_id=1, source_target_pairs={{0,1},{1,0},{2,3},{3,2},{4,5},{5,4},{6,7},{7,6},{8,9},{9,8},{10,11... | collective-permute-start | bytes 1572872 | tf_op jit(solution)/shard_map/ppermute | solution.py:392
  108.2 2.6 %collective-permute-start.19 = (bf16[8,128,256]{2,1,0:T(8,128)(2,1)S(1)}, bf16[8,128,256]{2,1,0:T(8,128)(2,1)S(1)}, u32[]{:S(2)}, u32[]{:S(2)}) collective-permute-start(bf16[8,128,256]{2,1,0:T(8,128)(2,1)S(1)} %all-to-all-done.3.grad_ref), channel_id=1, source_target_pairs={{0,1},{1,0},{2,3},{3,2},{4,5},{5,4},{6,7},{7,6},{8,9},{9,8},{10,11... | collective-permute-start | bytes 1572872 | tf_op jit(solution)/shard_map/ppermute | solution.py:419
  108.7 27.4 %collective-permute-start.20 = (f32[256,1024]{1,0:T(8,128)}, f32[256,1024]{1,0:T(8,128)S(1)}, u32[]{:S(2)}, u32[]{:S(2)}) collective-permute-start(f32[256,1024]{1,0:T(8,128)} %get-tuple-element.61), channel_id=1, source_target_pairs={{0,1},{1,0},{2,3},{3,2},{4,5},{5,4},{6,7},{7,6},{8,9},{9,8},{10,11... | collective-permute-start | bytes 3145736 | tf_op jit(solution)/shard_map/ppermute | solution.py:420
  132.5 14.1 %all-to-all-start.5 = ((f32[16,72,128]{2,1,0:T(8,128)}), f32[16,72,128]{2,1,0:T(8,128)S(1)}, u32[]{:S(2)}, u32[]{:S(2)}) async-start(f32[16,72,128]{2,1,0:T(8,128)} %shard_map.90), calls=%async_computation.5 | async-start | bytes 1179648 | tf_op jit(solution)/shard_map/all_to_all | solution.py:441
  146.6 13.0 %all-to-all-start.6 = ((bf16[16,16,1024]{2,1,0:T(8,128)(2,1)}), bf16[16,16,1024]{2,1,0:T(8,128)(2,1)S(1)}, u32[]{:S(2)}, u32[]{:S(2)}) async-start(bf16[16,16,1024]{2,1,0:T(8,128)(2,1)} %bitcast.18), calls=%async_computation.6 | async-start | bytes 1048576 | tf_op jit(solution)/shard_map/all_to_all | solution.py:444
  159.6 7.4 %collective-permute-start.21 = (bf16[8,3,128,128]{3,2,1,0:T(8,128)(2,1)}, bf16[8,3,128,128]{3,2,1,0:T(8,128)(2,1)S(1)}, u32[]{:S(2)}, u32[]{:S(2)}) collective-permute-start(bf16[8,3,128,128]{3,2,1,0:T(8,128)(2,1)} %get-tuple-element.67), channel_id=1, source_target_pairs={{0,1},{1,0},{2,3},{3,2},{4,5},{5,4},{6,7},{7,6},{8,9},{9,8},{10,11... | collective-permute-start | bytes 2359304 | tf_op jit(solution)/shard_map/ppermute | solution.py:460
  164.1 1.4 collective-permute-start.22
  (6 other events, 18.3 us)

commit v4 on v3

--- a/solution.py
+++ b/solution.py
@@ -59,7 +59,7 @@
         ref[2 * head + half, HALF:ROWS] = tail
 
 
-def call(body, grid, ins, outs, scratch=()):
+def call(body, grid, ins, outs, scratch=(), aliases=()):
     run = pl.pallas_call(
         body,
         grid_spec=pltpu.PrefetchScalarGridSpec(
@@ -70,6 +70,7 @@
             scratch_shapes=list(scratch),
         ),
         out_shape=[pltpu.HBM(spec[2], spec[3]) for spec in outs],
+        input_output_aliases=dict(aliases),
         compiler_params=PARAMS,
     )
 
@@ -123,21 +124,27 @@
     send_ref[...] = jnp.where(place[0] == 0, high, low)
 
 
-def attn_grad_body(count, place, *refs):
+def attn_grad_body(count, ahead_of, place, *refs):
     *og_refs, w_ref, out_ref, tokens, arrived = refs
-    copies, start = [], 0
+    copies = []
     for position, ref in enumerate(og_refs):
-        here = tokens.at[pl.ds(start, ref.shape[0])]
+        here = tokens.at[pl.ds(position * BLK, BLK)]
         copies.append(pltpu.make_async_copy(ref, here, arrived.at[position]))
         copies[-1].start()
-        start += ref.shape[0]
-    batch = count // 2
-    for first, waits in ((0, copies[:batch]), (batch, copies[batch:])):
-        for copy in waits:
+    batch = (len(og_refs) + 1) // 2
+    for first in range(0, len(og_refs), batch):
+        last = min(first + batch, len(og_refs))
+        for copy in copies[first:last]:
             copy.wait()
-        part = dot(tokens[first * BLK : (first + batch) * BLK], w_ref[...], NT).astype(BF)
-        for more in range(batch):
-            out_ref[lax.rem(place[3] + first + more, count)] = part[more * BLK : (more + 1) * BLK]
+        part = dot(tokens[first * BLK : last * BLK], w_ref[...], NT).astype(BF)
+        for position in range(first, last):
+            start = (position - first) * BLK
+            out_ref[lax.rem(place[3] + ahead_of[position], count)] = part[start : start + BLK]
+
+
+def last_grad_body(place, low_ref, high_ref, w_ref, _, out_ref):
+    rows = jnp.concatenate([low_ref[...], high_ref[...]], axis=0)
+    out_ref[0] = dot(rows, w_ref[...], NT).astype(BF)
 
 
 def forward_body(
@@ -391,13 +398,33 @@
     att_mine = lax.all_to_all(attended, "z", 0, 0, tiled=True)
     att_other = swap(att_mine)
 
+    ahead_of = [*range(nz // 2), *range(nz // 2 + 1, nz)]
+    early = [part for part in og_all if part.shape[0] == tok]
+    grads_shape = (nz, tok, 2 * DH)
     attn_grad = call(
-        functools.partial(attn_grad_body, nz),
+        functools.partial(attn_grad_body, nz, ahead_of),
         (1,),
-        [(None, None, pl.ANY)] * len(og_all) + [whole(2 * DH, model)],
-        [(*whole(nz, tok, 2 * DH), (nz, tok, 2 * DH), BF)],
-        [pltpu.VMEM((nz * tok, model), BF), pltpu.SemaphoreType.DMA((len(og_all),))],
-    )(place, *og_all, rows)[0]
+        [(None, None, pl.ANY)] * len(early) + [whole(2 * DH, model)],
+        [(*whole(*grads_shape), grads_shape, BF)],
+        [
+            pltpu.VMEM((len(early) * tok, model), BF),
+            pltpu.SemaphoreType.DMA((len(early),)),
+        ],
+    )(place, *early, rows)[0]
+    attn_grad = call(
+        last_grad_body,
+        (1,),
+        [whole(tok // 2, model)] * 2 + [whole(2 * DH, model), (None, None, pl.ANY)],
+        [
+            (
+                (1, tok, 2 * DH),
+                lambda j, p: (lax.rem(p[3] + nz // 2, nz), 0, 0),
+                grads_shape,
+                BF,
+            )
+        ],
+        aliases={4: 0},
+    )(place, *kept_out(low, high), rows, *kept_out(attn_grad))[0]
     attn_grad, att_mine = lax.optimization_barrier((attn_grad, att_mine))
     grad_mine = lax.all_to_all(attn_grad, "z", 0, 0, tiled=True)
 
@@ -472,9 +499,9 @@
     )
     grads = call(
         merge_body,
-        grid,
-        [grad_out[:2]] * 2,
-        [(*head_spec, (tok, width), BF)] * 3,
+        (1,),
+        [whole(pairs, 3, tok, DH)] * 2,
+        [(*whole(tok, width), (tok, width), BF)] * 3,
     )(place, *kept_out(keep), back)
     return (*(grad.reshape(1, tok, width) for grad in grads), weight_grad)
 

time: 172 us -> 169 us (0.983)
  waiting for transfers between devices: 44.6 us -> 37.1 us
  starting transfers between devices: 62.5 us -> 65.1 us
    ppermute x14, waiting for transfers between devices: 10.7 us -> 5.64 us  [from_ahead(): lax.ppermute(piece, axis, [((i + ahead) % size, i) for i in range(size)])]
    all_to_all x1, waiting for transfers between devices: 9.18 us -> 6.64 us  [on_device(): grad_mine = lax.all_to_all(attn_grad, 'z', 0, 0, tiled=True)]
    ppermute x1, starting transfers between devices: 0.49 us -> 2.42 us  [on_device(): grad_other = swap(grad_mine)]
    pallas_call x2 -> x3, Pallas kernels: 9.52 us -> 11 us  [the longest x1 5.05 us: on_device(): call(functools.partial(attn_grad_body, nz, ahead_of), (1,), [(None, None,...]
  transfers between devices with their start and end apart: 29 -> 29, of which waited for: 10 -> 10; matrix products, arithmetic and copies ran while one was open for 3% -> 3% of each run, Pallas kernels for 23% -> 24%
where the time goes in v4:
time: 169 us; the launch traced here: 168 us
  starting transfers between devices  65.1 us (39%)
  Pallas kernels  44.1 us (26%)
  waiting for transfers between devices  37.1 us (22%)
  blocking collectives  15.3 us (9%)
  local copies, waits for them, and re-layouts  2.64 us (2%)
  other arithmetic  2.58 us (2%)
    ppermute x14, starting transfers between devices, from_ahead(): lax.ppermute(piece, axis, [((i + ahead) % size, i) for i in range(size)])  22.6 us
    all_to_all x1, blocking collectives, on_device(): parts = lax.all_to_all(grad_sum, plane, 0, 0, tiled=True)  15.3 us
    all_to_all x1, waiting for transfers between devices, on_device(): later = lax.all_to_all(later, plane, 0, 0, tiled=True)  9.54 us
    pallas_call x1, Pallas kernels, on_device(): call(backward_body, grid, [pair_spec] * 3 + [state_spec, state_spec, pair...  7.62 us
    all_to_all x1, waiting for transfers between devices, on_device(): grad_mine = lax.all_to_all(attn_grad, 'z', 0, 0, tiled=True)  6.64 us
    pallas_call x1, Pallas kernels, on_device(): call(functools.partial(weight_body, steps, nz), (2 * steps,), [att_spec]...  6.23 us
    ppermute x1, starting transfers between devices, on_device(): rows_other = swap(rows_mine)  5.79 us
    ppermute x14, waiting for transfers between devices, from_ahead(): lax.ppermute(piece, axis, [((i + ahead) % size, i) for i in range(size)])  5.64 us
  transfers between devices with their start and end apart: 29, of which 10 were waited for; matrix products, arithmetic and copies ran while one was open for 3% of the time, Pallas kernels for 24%

profile of v4, /device:TPU:1, one launch (start us, length us, event | category | flops | bytes accessed | tf_op | source)
XLA Modules:
  0.0 167.6 jit_solution(15905679164869557772)
XLA Ops:
  0.6 3.3 %collective-permute-start.1 = (bf16[128,2048]{1,0:T(8,128)(2,1)}, bf16[128,2048]{1,0:T(8,128)(2,1)S(1)}, u32[]{:S(2)}, u32[]{:S(2)}) collective-permute-start(bf16[128,2048]{1,0:T(8,128)(2,1)} %bitcast.36), channel_id=1, source_target_pairs={{0,1},{1,0},{2,3},{3,2},{4,5},{5,4},{6,7},{7,6},{8,9},{9,8},{10,11... | collective-permute-start | bytes 1572872 | tf_op jit(solution)/shard_map/ppermute | solution.py:331
  4.1 3.8 %collective-permute-start.3 = (bf16[128,2048]{1,0:T(8,128)(2,1)}, bf16[128,2048]{1,0:T(8,128)(2,1)S(1)}, u32[]{:S(2)}, u32[]{:S(2)}) collective-permute-start(bf16[128,2048]{1,0:T(8,128)(2,1)} %bitcast.32), channel_id=1, source_target_pairs={{32,0},{64,32},{96,64},{128,96},{160,128},{192,160},{224,192},{0,2... | collective-permute-start | bytes 1572872 | tf_op jit(solution)/shard_map/ppermute | solution.py:329
  8.0 4.5 %shard_map.84 = (bf16[8,2,128,128]{3,2,1,0:T(8,128)(2,1)}, bf16[8,2,128,128]{3,2,1,0:T(8,128)(2,1)}, f32[16,72,128]{2,1,0:T(8,128)}, f32[16,72,128]{2,1,0:T(8,128)}) custom-call(s32[4]{0:T(128)S(1)} %pad_add_fusion.place, bf16[128,2048]{1,0:T(8,128)(2,1)} %bitcast.37, bf16[128,2048]{1,0:T(8,128)(2,1)} %bitcast.39, ...), custom_call_target="tpu_custom_call" | custom-call | tf_op jit(solution)/shard_map/pallas_call | solution.py:354
  12.5 2.8 %collective-permute-start.11 = (bf16[8,2048]{1,0:T(8,128)(2,1)S(1)}, bf16[8,2048]{1,0:T(8,128)(2,1)S(1)}, u32[]{:S(2)}, u32[]{:S(2)}) collective-permute-start(bf16[8,2048]{1,0:T(8,128)(2,1)S(1)} %copy-done.8), channel_id=1, source_target_pairs={{2,0},{4,2},{6,4},{0,6},{3,1},{5,3},{7,5},{1,7},{10,8},{12,10},{14... | collective-permute-start | bytes 98312 | tf_op jit(solution)/shard_map/ppermute | solution.py:329
  16.3 4.3 %all-to-all-start = ((f32[16,72,128]{2,1,0:T(8,128)}), f32[16,72,128]{2,1,0:T(8,128)S(1)}, u32[]{:S(2)}, u32[]{:S(2)}) async-start(f32[16,72,128]{2,1,0:T(8,128)} %get-tuple-element.41), calls=%async_computation | async-start | bytes 1179648 | tf_op jit(solution)/shard_map/all_to_all | solution.py:375
  20.6 2.9 %collective-permute-start.12 = (bf16[8,2048]{1,0:T(8,128)(2,1)S(1)}, bf16[8,2048]{1,0:T(8,128)(2,1)S(1)}, u32[]{:S(2)}, u32[]{:S(2)}) collective-permute-start(bf16[8,2048]{1,0:T(8,128)(2,1)S(1)} %copy-done.8), channel_id=1, source_target_pairs={{4,0},{6,2},{0,4},{2,6},{5,1},{7,3},{1,5},{3,7},{12,8},{14,10},{8,... | collective-permute-start | bytes 98312 | tf_op jit(solution)/shard_map/ppermute | solution.py:329
  23.8 3.0 %collective-permute-start.4 = (bf16[128,2048]{1,0:T(8,128)(2,1)S(1)}, bf16[128,2048]{1,0:T(8,128)(2,1)}, u32[]{:S(2)}, u32[]{:S(2)}) collective-permute-start(bf16[128,2048]{1,0:T(8,128)(2,1)S(1)} %collective-permute-done.3.refs_1_), channel_id=1, source_target_pairs={{32,0},{64,32},{96,64},{128,96},{160,128},{192,160},{224,192},{0,2... | collective-permute-start | bytes 1572872 | tf_op jit(solution)/shard_map/ppermute | solution.py:329
  26.8 4.6 %all-to-all-done.in_ref = f32[16,72,128]{2,1,0:T(8,128)S(1)} async-done(((f32[16,72,128]{2,1,0:T(8,128)}), f32[16,72,128]{2,1,0:T(8,128)S(1)}, u32[]{:S(2)}, u32[]{:S(2)}) %all-to-all-start) | async-done | bytes 589856 | tf_op jit(solution)/shard_map/all_to_all | solution.py:375
  32.8 5.0 %all-to-all-start.1 = ((f32[16,72,128]{2,1,0:T(8,128)}), f32[16,72,128]{2,1,0:T(8,128)S(1)}, u32[]{:S(2)}, u32[]{:S(2)}) async-start(f32[16,72,128]{2,1,0:T(8,128)} %shard_map.85), calls=%async_computation.1 | async-start | bytes 1179648 | tf_op jit(solution)/shard_map/all_to_all | solution.py:382
  37.8 2.7 %collective-permute-start.14 = (bf16[4,8,2048]{2,1,0:T(8,128)(2,1)S(1)}, bf16[4,8,2048]{2,1,0:T(8,128)(2,1)S(1)}, u32[]{:S(2)}, u32[]{:S(2)}) collective-permute-start(bf16[4,8,2048]{2,1,0:T(8,128)(2,1)S(1)} %bitcast_dynamic-update-slice_fusion.3), channel_id=1, source_target_pairs={{8,0},{16,8},{24,16},{0,24},{9,1},{17,9},{25,17},{1,25},{10,2},{18... | collective-permute-start | bytes 393224 | tf_op jit(solution)/shard_map/ppermute | solution.py:329
  41.6 3.0 %collective-permute-start.5 = (bf16[128,2048]{1,0:T(8,128)(2,1)}, bf16[128,2048]{1,0:T(8,128)(2,1)S(1)}, u32[]{:S(2)}, u32[]{:S(2)}) collective-permute-start(bf16[128,2048]{1,0:T(8,128)(2,1)} %collective-permute-done.4.refs_2_), channel_id=1, source_target_pairs={{32,0},{64,32},{96,64},{128,96},{160,128},{192,160},{224,192},{0,2... | collective-permute-start | bytes 1572872 | tf_op jit(solution)/shard_map/ppermute | solution.py:329
  44.6 3.8 %all-to-all-done.1.in_ref = f32[16,72,128]{2,1,0:T(8,128)S(1)} async-done(((f32[16,72,128]{2,1,0:T(8,128)}), f32[16,72,128]{2,1,0:T(8,128)S(1)}, u32[]{:S(2)}, u32[]{:S(2)}) %all-to-all-start.1) | async-done | bytes 589856 | tf_op jit(solution)/shard_map/all_to_all | solution.py:382
  48.4 5.6 %shard_map.86 = (bf16[8,2,128,128]{3,2,1,0:T(8,128)(2,1)}, f32[16,72,128]{2,1,0:T(8,128)}, bf16[8,256,128]{2,1,0:T(8,128)(2,1)}, f32[8,2,128,128]{3,2,1,0:T(8,128)}, f32[8,2,128,128]{3,2,1,0:T(8,128)}) custom-call(s32[4]{0:T(128)S(1)} %pad_add_fusion.place, bf16[128,2048]{1,0:T(8,128)(2,1)} %bitcast.41, bf16[128,2048]{1,0:T(8,128)(2,1)S(1)} %collective-permute-done.q_other, ...), custom_call_target="tpu_custom_call" | custom-call | tf_op jit(solution)/shard_map/pallas_call | solution.py:383
  54.1 4.6 %all-to-all-start.2 = ((bf16[8,256,128]{2,1,0:T(8,128)(2,1)}), bf16[8,256,128]{2,1,0:T(8,128)(2,1)S(1)}, u32[]{:S(2)}, u32[]{:S(2)}) async-start(bf16[8,256,128]{2,1,0:T(8,128)(2,1)} %get-tuple-element.48), calls=%async_computation.2 | async-start | bytes 1048576 | tf_op jit(solution)/shard_map/all_to_all | solution.py:398
  59.7 5.8 %collective-permute-start.17 = (bf16[16,8,2048]{2,1,0:T(8,128)(2,1)S(1)}, bf16[16,8,2048]{2,1,0:T(8,128)(2,1)S(1)}, u32[]{:S(2)}, u32[]{:S(2)}) collective-permute-start(bf16[16,8,2048]{2,1,0:T(8,128)(2,1)S(1)} %bitcast.30), channel_id=1, source_target_pairs={{0,1},{1,0},{2,3},{3,2},{4,5},{5,4},{6,7},{7,6},{8,9},{9,8},{10,11... | collective-permute-start | bytes 1572872 | tf_op jit(solution)/shard_map/ppermute | solution.py:392
  65.5 3.0 %collective-permute-start.6 = (bf16[64,2048]{1,0:T(8,128)(2,1)S(1)}, bf16[64,2048]{1,0:T(8,128)(2,1)S(1)}, u32[]{:S(2)}, u32[]{:S(2)}) collective-permute-start(bf16[64,2048]{1,0:T(8,128)(2,1)S(1)} %slice.8), channel_id=1, source_target_pairs={{32,0},{64,32},{96,64},{128,96},{160,128},{192,160},{224,192},{0,2... | collective-permute-start | bytes 786440 | tf_op jit(solution)/shard_map/ppermute | solution.py:329
  69.5 5.1 %shard_map.87._ = bf16[8,128,256]{2,1,0:T(8,128)(2,1)} custom-call(s32[4]{0:T(128)S(1)} %pad_add_fusion.place, bf16[128,2048]{1,0:T(8,128)(2,1)} %bitcast.34, bf16[128,2048]{1,0:T(8,128)(2,1)} %copy-done.2, bf16[128,2048]{1,0:T(8,128)(2,1)} %collective-permute-done.4.refs_2_, bf16[128,2048]{1,0:T(8,128)(2,1)} %copy-done, bf16[128,2048]{1,0:T(8,128)(2,1)} %copy-done.1, ...), custom_call_target="tpu_custom_call" | custom-call | tf_op jit(solution)/shard_map/pallas_call | solution.py:404
  74.6 2.4 %collective-permute-done.6.low_ref.refs_4_ = bf16[64,2048]{1,0:T(8,128)(2,1)S(1)} collective-permute-done((bf16[64,2048]{1,0:T(8,128)(2,1)S(1)}, bf16[64,2048]{1,0:T(8,128)(2,1)S(1)}, u32[]{:S(2)}, u32[]{:S(2)}) %collective-permute-start.6) | collective-permute-done | bytes 262176 | tf_op jit(solution)/shard_map/ppermute | solution.py:329
  77.0 3.2 %collective-permute-done.10.high_ref.refs_5_ = bf16[64,2048]{1,0:T(8,128)(2,1)S(1)} collective-permute-done((bf16[64,2048]{1,0:T(8,128)(2,1)}, bf16[64,2048]{1,0:T(8,128)(2,1)S(1)}, u32[]{:S(2)}, u32[]{:S(2)}) %collective-permute-start.10) | collective-permute-done | bytes 262176 | tf_op jit(solution)/shard_map/ppermute | solution.py:329
  80.9 2.7 %shard_map.88 = bf16[8,128,256]{2,1,0:T(8,128)(2,1)} custom-call(s32[4]{0:T(128)S(1)} %pad_add_fusion.place, bf16[64,2048]{1,0:T(8,128)(2,1)} %copy-done.5, bf16[64,2048]{1,0:T(8,128)(2,1)} %copy-done.6, bf16[256,2048]{1,0:T(8,128)(2,1)S(1)} %bitcast.29, bf16[8,128,256]{2,1,0:T(8,128)(2,1)} %shard_map.87._), custom_call_target="tpu_custom_call", output_to_operand_aliasing={{}: (4, {})} | custom-call | tf_op jit(solution)/shard_map/pallas_call | solution.py:414
  83.6 3.8 %all-to-all-start.3 = ((bf16[8,128,256]{2,1,0:T(8,128)(2,1)}), bf16[8,128,256]{2,1,0:T(8,128)(2,1)S(1)}, u32[]{:S(2)}, u32[]{:S(2)}) async-start(bf16[8,128,256]{2,1,0:T(8,128)(2,1)} %shard_map.88), calls=%async_computation.3 | async-start | bytes 1048576 | tf_op jit(solution)/shard_map/all_to_all | solution.py:429
  90.6 6.2 %shard_map.89 = (f32[256,1024]{1,0:T(8,128)}, f32[256,1024]{1,0:T(8,128)}) custom-call(s32[4]{0:T(128)S(1)} %pad_add_fusion.place, bf16[8,256,128]{2,1,0:T(8,128)(2,1)S(1)} %all-to-all-done.2.mine_ref, bf16[8,256,128]{2,1,0:T(8,128)(2,1)S(1)} %collective-permute-done.18.other_ref, bf16[128,2048]{1,0:T(8,128)(2,1)} %bitcast.35, bf16[128,2048]{1,0:T(8,128)(2,1)} %copy-done.2, ...), custom_call_target="tpu_custom_call" | custom-call | tf_op jit(solution)/shard_map/pallas_call | solution.py:435
  96.8 6.6 %all-to-all-done.3.grad_ref = bf16[8,128,256]{2,1,0:T(8,128)(2,1)S(1)} async-done(((bf16[8,128,256]{2,1,0:T(8,128)(2,1)}), bf16[8,128,256]{2,1,0:T(8,128)(2,1)S(1)}, u32[]{:S(2)}, u32[]{:S(2)}) %all-to-all-start.3) | async-done | bytes 524320 | tf_op jit(solution)/shard_map/all_to_all | solution.py:429
  103.5 2.4 %collective-permute-start.19 = (bf16[8,128,256]{2,1,0:T(8,128)(2,1)S(1)}, bf16[8,128,256]{2,1,0:T(8,128)(2,1)S(1)}, u32[]{:S(2)}, u32[]{:S(2)}) collective-permute-start(bf16[8,128,256]{2,1,0:T(8,128)(2,1)S(1)} %all-to-all-done.3.grad_ref), channel_id=1, source_target_pairs={{0,1},{1,0},{2,3},{3,2},{4,5},{5,4},{6,7},{7,6},{8,9},{9,8},{10,11... | collective-permute-start | bytes 1572872 | tf_op jit(solution)/shard_map/ppermute | solution.py:446
  108.1 5.0 %shard_map.90 = (f32[8,2,128,128]{3,2,1,0:T(8,128)}, f32[8,2,128,128]{3,2,1,0:T(8,128)}, f32[16,72,128]{2,1,0:T(8,128)}, f32[16,72,128]{2,1,0:T(8,128)}) custom-call(s32[4]{0:T(128)S(1)} %pad_add_fusion.place, bf16[8,2,128,128]{3,2,1,0:T(8,128)(2,1)} %get-tuple-element.43.queries, f32[8,2,128,128]{3,2,1,0:T(8,128)} %get-tuple-element.45.o_ref, ...), custom_call_target="tpu_custom_call" | custom-call | tf_op jit(solution)/shard_map/pallas_call | solution.py:450
  113.2 15.3 %all_to_all.35.in_ref = f32[16,72,128]{2,1,0:T(8,128)S(1)} all-to-all(f32[16,72,128]{2,1,0:T(8,128)} %get-tuple-element.59), channel_id=1, replica_groups=mesh['z'=8,'x'=4,'y'=4,'c'=2] {'x','y'}, dimensions={0} | all-to-all | bytes 1179648 | tf_op jit(solution)/shard_map/all_to_all | solution.py:461
  129.8 3.6 %all-to-all-start.5 = ((f32[16,72,128]{2,1,0:T(8,128)}), f32[16,72,128]{2,1,0:T(8,128)S(1)}, u32[]{:S(2)}, u32[]{:S(2)}) async-start(f32[16,72,128]{2,1,0:T(8,128)} %shard_map.91), calls=%async_computation.5 | async-start | bytes 1179648 | tf_op jit(solution)/shard_map/all_to_all | solution.py:468
  134.4 9.5 %all-to-all-done.5.later_ref = f32[16,72,128]{2,1,0:T(8,128)S(1)} async-done(((f32[16,72,128]{2,1,0:T(8,128)}), f32[16,72,128]{2,1,0:T(8,128)S(1)}, u32[]{:S(2)}, u32[]{:S(2)}) %all-to-all-start.5) | async-done | bytes 589856 | tf_op jit(solution)/shard_map/all_to_all | solution.py:468
  143.9 3.7 %all-to-all-start.6 = ((bf16[16,16,1024]{2,1,0:T(8,128)(2,1)}), bf16[16,16,1024]{2,1,0:T(8,128)(2,1)S(1)}, u32[]{:S(2)}, u32[]{:S(2)}) async-start(bf16[16,16,1024]{2,1,0:T(8,128)(2,1)} %bitcast.18), calls=%async_computation.6 | async-start | bytes 1048576 | tf_op jit(solution)/shard_map/all_to_all | solution.py:471
  147.7 7.6 %shard_map.92 = (bf16[8,3,128,128]{3,2,1,0:T(8,128)(2,1)}, bf16[8,3,128,128]{3,2,1,0:T(8,128)(2,1)}) custom-call(s32[4]{0:T(128)S(1)} %pad_add_fusion.place, bf16[8,2,128,128]{3,2,1,0:T(8,128)(2,1)} %get-tuple-element.43.queries, bf16[8,2,128,128]{3,2,1,0:T(8,128)(2,1)} %get-tuple-element.39.keys, bf16[8,2,128,128]{3,2,1,0:T(8,128)(2,1)} %get-tuple-element.40.values, ...), custom_call_target="tpu_custom_call" | custom-call | tf_op jit(solution)/shard_map/pallas_call | solution.py:473
  156.9 3.3 %collective-permute-start.21 = (bf16[8,3,128,128]{3,2,1,0:T(8,128)(2,1)}, bf16[8,3,128,128]{3,2,1,0:T(8,128)(2,1)S(1)}, u32[]{:S(2)}, u32[]{:S(2)}) collective-permute-start(bf16[8,3,128,128]{3,2,1,0:T(8,128)(2,1)} %get-tuple-element.67), channel_id=1, source_target_pairs={{0,1},{1,0},{2,3},{3,2},{4,5},{5,4},{6,7},{7,6},{8,9},{9,8},{10,11... | collective-permute-start | bytes 2359304 | tf_op jit(solution)/shard_map/ppermute | solution.py:487
  164.3 3.2 %shard_map.93 = (bf16[128,2048]{1,0:T(8,128)(2,1)}, bf16[128,2048]{1,0:T(8,128)(2,1)}, bf16[128,2048]{1,0:T(8,128)(2,1)}) custom-call(s32[4]{0:T(128)S(1)} %pad_add_fusion.place, bf16[8,3,128,128]{3,2,1,0:T(8,128)(2,1)} %get-tuple-element.64.keep_ref, bf16[8,3,128,128]{3,2,1,0:T(8,128)(2,1)S(1)} %collective-permute-done.21.back_ref), custom_call_target="tpu_custom_call" | custom-call | tf_op jit(solution)/shard_map/pallas_call | solution.py:500
  (70 shorter events, 20.3 us)
Async XLA Ops:
  0.6 7.4 %collective-permute-start.1 = (bf16[128,2048]{1,0:T(8,128)(2,1)}, bf16[128,2048]{1,0:T(8,128)(2,1)S(1)}, u32[]{:S(2)}, u32[]{:S(2)}) collective-permute-start(bf16[128,2048]{1,0:T(8,128)(2,1)} %bitcast.36), channel_id=1, source_target_pairs={{0,1},{1,0},{2,3},{3,2},{4,5},{5,4},{6,7},{7,6},{8,9},{9,8},{10,11... | collective-permute-start | bytes 1572872 | tf_op jit(solution)/shard_map/ppermute | solution.py:331
  4.0 4.0 %collective-permute-start.2 = (bf16[128,2048]{1,0:T(8,128)(2,1)}, bf16[128,2048]{1,0:T(8,128)(2,1)S(1)}, u32[]{:S(2)}, u32[]{:S(2)}) collective-permute-start(bf16[128,2048]{1,0:T(8,128)(2,1)} %bitcast.38), channel_id=1, source_target_pairs={{0,1},{1,0},{2,3},{3,2},{4,5},{5,4},{6,7},{7,6},{8,9},{9,8},{10,11... | collective-permute-start | bytes 1572872 | tf_op jit(solution)/shard_map/ppermute | solution.py:331
  4.1 19.4 %collective-permute-start.3 = (bf16[128,2048]{1,0:T(8,128)(2,1)}, bf16[128,2048]{1,0:T(8,128)(2,1)S(1)}, u32[]{:S(2)}, u32[]{:S(2)}) collective-permute-start(bf16[128,2048]{1,0:T(8,128)(2,1)} %bitcast.32), channel_id=1, source_target_pairs={{32,0},{64,32},{96,64},{128,96},{160,128},{192,160},{224,192},{0,2... | collective-permute-start | bytes 1572872 | tf_op jit(solution)/shard_map/ppermute | solution.py:329
  7.9 15.9 %collective-permute-start.7 = (bf16[128,2048]{1,0:T(8,128)(2,1)}, bf16[128,2048]{1,0:T(8,128)(2,1)S(1)}, u32[]{:S(2)}, u32[]{:S(2)}) collective-permute-start(bf16[128,2048]{1,0:T(8,128)(2,1)} %bitcast.33), channel_id=1, source_target_pairs={{224,0},{0,32},{32,64},{64,96},{96,128},{128,160},{160,192},{192,2... | collective-permute-start | bytes 1572872 | tf_op jit(solution)/shard_map/ppermute | solution.py:329
  8.0 7.4 %copy-start.7 = (bf16[1,128,2048]{2,1,0:T(8,128)(2,1)S(1)}, bf16[1,128,2048]{2,1,0:T(8,128)(2,1)}, u32[]{:S(2)}) copy-start(bf16[1,128,2048]{2,1,0:T(8,128)(2,1)} %param.5) | copy-start | bytes 1572868
  12.5 14.2 %collective-permute-start.11 = (bf16[8,2048]{1,0:T(8,128)(2,1)S(1)}, bf16[8,2048]{1,0:T(8,128)(2,1)S(1)}, u32[]{:S(2)}, u32[]{:S(2)}) collective-permute-start(bf16[8,2048]{1,0:T(8,128)(2,1)S(1)} %copy-done.8), channel_id=1, source_target_pairs={{2,0},{4,2},{6,4},{0,6},{3,1},{5,3},{7,5},{1,7},{10,8},{12,10},{14... | collective-permute-start | bytes 98312 | tf_op jit(solution)/shard_map/ppermute | solution.py:329
  15.3 25.7 %collective-permute-start = (bf16[128,2048]{1,0:T(8,128)(2,1)S(1)}, bf16[128,2048]{1,0:T(8,128)(2,1)S(1)}, u32[]{:S(2)}, u32[]{:S(2)}) collective-permute-start(bf16[128,2048]{1,0:T(8,128)(2,1)S(1)} %bitcast.42), channel_id=1, source_target_pairs={{0,1},{1,0},{2,3},{3,2},{4,5},{5,4},{6,7},{7,6},{8,9},{9,8},{10,11... | collective-permute-start | bytes 1572872 | tf_op jit(solution)/shard_map/ppermute | solution.py:331
  16.3 15.1 %all-to-all-start = ((f32[16,72,128]{2,1,0:T(8,128)}), f32[16,72,128]{2,1,0:T(8,128)S(1)}, u32[]{:S(2)}, u32[]{:S(2)}) async-start(f32[16,72,128]{2,1,0:T(8,128)} %get-tuple-element.41), calls=%async_computation | async-start | bytes 1179648 | tf_op jit(solution)/shard_map/all_to_all | solution.py:375
  20.6 6.2 %collective-permute-start.12 = (bf16[8,2048]{1,0:T(8,128)(2,1)S(1)}, bf16[8,2048]{1,0:T(8,128)(2,1)S(1)}, u32[]{:S(2)}, u32[]{:S(2)}) collective-permute-start(bf16[8,2048]{1,0:T(8,128)(2,1)S(1)} %copy-done.8), channel_id=1, source_target_pairs={{4,0},{6,2},{0,4},{2,6},{5,1},{7,3},{1,5},{3,7},{12,8},{14,10},{8,... | collective-permute-start | bytes 98312 | tf_op jit(solution)/shard_map/ppermute | solution.py:329
  23.5 9.3 %copy-start.2 = (bf16[128,2048]{1,0:T(8,128)(2,1)}, bf16[128,2048]{1,0:T(8,128)(2,1)S(1)}, u32[]{:S(2)}) copy-start(bf16[128,2048]{1,0:T(8,128)(2,1)S(1)} %collective-permute-done.3.refs_1_) | copy-start | bytes 1572868
  23.5 14.3 %collective-permute-start.13 = (bf16[8,2048]{1,0:T(8,128)(2,1)S(1)}, bf16[8,2048]{1,0:T(8,128)(2,1)S(1)}, u32[]{:S(2)}, u32[]{:S(2)}) collective-permute-start(bf16[8,2048]{1,0:T(8,128)(2,1)S(1)} %copy-done.8), channel_id=1, source_target_pairs={{6,0},{0,2},{2,4},{4,6},{7,1},{1,3},{3,5},{5,7},{14,8},{8,10},{10,... | collective-permute-start | bytes 98312 | tf_op jit(solution)/shard_map/ppermute | solution.py:329
  23.8 9.0 %copy-start.3 = (bf16[128,2048]{1,0:T(8,128)(2,1)}, bf16[128,2048]{1,0:T(8,128)(2,1)S(1)}, u32[]{:S(2)}) copy-start(bf16[128,2048]{1,0:T(8,128)(2,1)S(1)} %collective-permute-done.7.refs_6_.refs_8_) | copy-start | bytes 1572868
  23.8 17.9 %collective-permute-start.4 = (bf16[128,2048]{1,0:T(8,128)(2,1)S(1)}, bf16[128,2048]{1,0:T(8,128)(2,1)}, u32[]{:S(2)}, u32[]{:S(2)}) collective-permute-start(bf16[128,2048]{1,0:T(8,128)(2,1)S(1)} %collective-permute-done.3.refs_1_), channel_id=1, source_target_pairs={{32,0},{64,32},{96,64},{128,96},{160,128},{192,160},{224,192},{0,2... | collective-permute-start | bytes 1572872 | tf_op jit(solution)/shard_map/ppermute | solution.py:329
  26.7 17.9 %collective-permute-start.8 = (bf16[128,2048]{1,0:T(8,128)(2,1)S(1)}, bf16[128,2048]{1,0:T(8,128)(2,1)}, u32[]{:S(2)}, u32[]{:S(2)}) collective-permute-start(bf16[128,2048]{1,0:T(8,128)(2,1)S(1)} %collective-permute-done.7.refs_6_.refs_8_), channel_id=1, source_target_pairs={{224,0},{0,32},{32,64},{64,96},{96,128},{128,160},{160,192},{192,2... | collective-permute-start | bytes 1572872 | tf_op jit(solution)/shard_map/ppermute | solution.py:329
  32.8 15.6 %all-to-all-start.1 = ((f32[16,72,128]{2,1,0:T(8,128)}), f32[16,72,128]{2,1,0:T(8,128)S(1)}, u32[]{:S(2)}, u32[]{:S(2)}) async-start(f32[16,72,128]{2,1,0:T(8,128)} %shard_map.85), calls=%async_computation.1 | async-start | bytes 1179648 | tf_op jit(solution)/shard_map/all_to_all | solution.py:382
  37.8 20.9 %collective-permute-start.14 = (bf16[4,8,2048]{2,1,0:T(8,128)(2,1)S(1)}, bf16[4,8,2048]{2,1,0:T(8,128)(2,1)S(1)}, u32[]{:S(2)}, u32[]{:S(2)}) collective-permute-start(bf16[4,8,2048]{2,1,0:T(8,128)(2,1)S(1)} %bitcast_dynamic-update-slice_fusion.3), channel_id=1, source_target_pairs={{8,0},{16,8},{24,16},{0,24},{9,1},{17,9},{25,17},{1,25},{10,2},{18... | collective-permute-start | bytes 393224 | tf_op jit(solution)/shard_map/ppermute | solution.py:329
  40.5 18.2 %collective-permute-start.15 = (bf16[4,8,2048]{2,1,0:T(8,128)(2,1)S(1)}, bf16[4,8,2048]{2,1,0:T(8,128)(2,1)}, u32[]{:S(2)}, u32[]{:S(2)}) collective-permute-start(bf16[4,8,2048]{2,1,0:T(8,128)(2,1)S(1)} %bitcast_dynamic-update-slice_fusion.3), channel_id=1, source_target_pairs={{16,0},{24,8},{0,16},{8,24},{17,1},{25,9},{1,17},{9,25},{18,2},{26... | collective-permute-start | bytes 393224 | tf_op jit(solution)/shard_map/ppermute | solution.py:329
  41.1 17.6 %collective-permute-start.16 = (bf16[4,8,2048]{2,1,0:T(8,128)(2,1)S(1)}, bf16[4,8,2048]{2,1,0:T(8,128)(2,1)S(1)}, u32[]{:S(2)}, u32[]{:S(2)}) collective-permute-start(bf16[4,8,2048]{2,1,0:T(8,128)(2,1)S(1)} %bitcast_dynamic-update-slice_fusion.3), channel_id=1, source_target_pairs={{24,0},{0,8},{8,16},{16,24},{25,1},{1,9},{9,17},{17,25},{26,2},{2,... | collective-permute-start | bytes 393224 | tf_op jit(solution)/shard_map/ppermute | solution.py:329
  41.6 23.9 %collective-permute-start.5 = (bf16[128,2048]{1,0:T(8,128)(2,1)}, bf16[128,2048]{1,0:T(8,128)(2,1)S(1)}, u32[]{:S(2)}, u32[]{:S(2)}) collective-permute-start(bf16[128,2048]{1,0:T(8,128)(2,1)} %collective-permute-done.4.refs_2_), channel_id=1, source_target_pairs={{32,0},{64,32},{96,64},{128,96},{160,128},{192,160},{224,192},{0,2... | collective-permute-start | bytes 1572872 | tf_op jit(solution)/shard_map/ppermute | solution.py:329
  44.6 24.0 %collective-permute-start.9 = (bf16[128,2048]{1,0:T(8,128)(2,1)}, bf16[128,2048]{1,0:T(8,128)(2,1)S(1)}, u32[]{:S(2)}, u32[]{:S(2)}) collective-permute-start(bf16[128,2048]{1,0:T(8,128)(2,1)} %collective-permute-done.8.refs_5_.refs_7_), channel_id=1, source_target_pairs={{224,0},{0,32},{32,64},{64,96},{96,128},{128,160},{160,192},{192,2... | collective-permute-start | bytes 1572872 | tf_op jit(solution)/shard_map/ppermute | solution.py:329
  54.1 29.5 %all-to-all-start.2 = ((bf16[8,256,128]{2,1,0:T(8,128)(2,1)}), bf16[8,256,128]{2,1,0:T(8,128)(2,1)S(1)}, u32[]{:S(2)}, u32[]{:S(2)}) async-start(bf16[8,256,128]{2,1,0:T(8,128)(2,1)} %get-tuple-element.48), calls=%async_computation.2 | async-start | bytes 1048576 | tf_op jit(solution)/shard_map/all_to_all | solution.py:398
  59.7 9.7 %collective-permute-start.17 = (bf16[16,8,2048]{2,1,0:T(8,128)(2,1)S(1)}, bf16[16,8,2048]{2,1,0:T(8,128)(2,1)S(1)}, u32[]{:S(2)}, u32[]{:S(2)}) collective-permute-start(bf16[16,8,2048]{2,1,0:T(8,128)(2,1)S(1)} %bitcast.30), channel_id=1, source_target_pairs={{0,1},{1,0},{2,3},{3,2},{4,5},{5,4},{6,7},{7,6},{8,9},{9,8},{10,11... | collective-permute-start | bytes 1572872 | tf_op jit(solution)/shard_map/ppermute | solution.py:392
  65.5 11.5 %collective-permute-start.6 = (bf16[64,2048]{1,0:T(8,128)(2,1)S(1)}, bf16[64,2048]{1,0:T(8,128)(2,1)S(1)}, u32[]{:S(2)}, u32[]{:S(2)}) collective-permute-start(bf16[64,2048]{1,0:T(8,128)(2,1)S(1)} %slice.8), channel_id=1, source_target_pairs={{32,0},{64,32},{96,64},{128,96},{160,128},{192,160},{224,192},{0,2... | collective-permute-start | bytes 786440 | tf_op jit(solution)/shard_map/ppermute | solution.py:329
  69.4 10.8 %collective-permute-start.10 = (bf16[64,2048]{1,0:T(8,128)(2,1)}, bf16[64,2048]{1,0:T(8,128)(2,1)S(1)}, u32[]{:S(2)}, u32[]{:S(2)}) collective-permute-start(bf16[64,2048]{1,0:T(8,128)(2,1)} %slice.9), channel_id=1, source_target_pairs={{224,0},{0,32},{32,64},{64,96},{96,128},{128,160},{160,192},{192,2... | collective-permute-start | bytes 786440 | tf_op jit(solution)/shard_map/ppermute | solution.py:329
  83.6 19.8 %all-to-all-start.3 = ((bf16[8,128,256]{2,1,0:T(8,128)(2,1)}), bf16[8,128,256]{2,1,0:T(8,128)(2,1)S(1)}, u32[]{:S(2)}, u32[]{:S(2)}) async-start(bf16[8,128,256]{2,1,0:T(8,128)(2,1)} %shard_map.88), calls=%async_computation.3 | async-start | bytes 1048576 | tf_op jit(solution)/shard_map/all_to_all | solution.py:429
  87.4 3.2 %collective-permute-start.18 = (bf16[8,256,128]{2,1,0:T(8,128)(2,1)S(1)}, bf16[8,256,128]{2,1,0:T(8,128)(2,1)S(1)}, u32[]{:S(2)}, u32[]{:S(2)}) collective-permute-start(bf16[8,256,128]{2,1,0:T(8,128)(2,1)S(1)} %all-to-all-done.2.mine_ref), channel_id=1, source_target_pairs={{0,1},{1,0},{2,3},{3,2},{4,5},{5,4},{6,7},{7,6},{8,9},{9,8},{10,11... | collective-permute-start | bytes 1572872 | tf_op jit(solution)/shard_map/ppermute | solution.py:399
  103.5 4.7 %collective-permute-start.19 = (bf16[8,128,256]{2,1,0:T(8,128)(2,1)S(1)}, bf16[8,128,256]{2,1,0:T(8,128)(2,1)S(1)}, u32[]{:S(2)}, u32[]{:S(2)}) collective-permute-start(bf16[8,128,256]{2,1,0:T(8,128)(2,1)S(1)} %all-to-all-done.3.grad_ref), channel_id=1, source_target_pairs={{0,1},{1,0},{2,3},{3,2},{4,5},{5,4},{6,7},{7,6},{8,9},{9,8},{10,11... | collective-permute-start | bytes 1572872 | tf_op jit(solution)/shard_map/ppermute | solution.py:446
  105.9 27.5 %collective-permute-start.20 = (f32[256,1024]{1,0:T(8,128)}, f32[256,1024]{1,0:T(8,128)S(1)}, u32[]{:S(2)}, u32[]{:S(2)}) collective-permute-start(f32[256,1024]{1,0:T(8,128)} %get-tuple-element.61), channel_id=1, source_target_pairs={{0,1},{1,0},{2,3},{3,2},{4,5},{5,4},{6,7},{7,6},{8,9},{9,8},{10,11... | collective-permute-start | bytes 3145736 | tf_op jit(solution)/shard_map/ppermute | solution.py:447
  129.8 14.1 %all-to-all-start.5 = ((f32[16,72,128]{2,1,0:T(8,128)}), f32[16,72,128]{2,1,0:T(8,128)S(1)}, u32[]{:S(2)}, u32[]{:S(2)}) async-start(f32[16,72,128]{2,1,0:T(8,128)} %shard_map.91), calls=%async_computation.5 | async-start | bytes 1179648 | tf_op jit(solution)/shard_map/all_to_all | solution.py:468
  143.9 13.0 %all-to-all-start.6 = ((bf16[16,16,1024]{2,1,0:T(8,128)(2,1)}), bf16[16,16,1024]{2,1,0:T(8,128)(2,1)S(1)}, u32[]{:S(2)}, u32[]{:S(2)}) async-start(bf16[16,16,1024]{2,1,0:T(8,128)(2,1)} %bitcast.18), calls=%async_computation.6 | async-start | bytes 1048576 | tf_op jit(solution)/shard_map/all_to_all | solution.py:471
  156.9 7.4 %collective-permute-start.21 = (bf16[8,3,128,128]{3,2,1,0:T(8,128)(2,1)}, bf16[8,3,128,128]{3,2,1,0:T(8,128)(2,1)S(1)}, u32[]{:S(2)}, u32[]{:S(2)}) collective-permute-start(bf16[8,3,128,128]{3,2,1,0:T(8,128)(2,1)} %get-tuple-element.67), channel_id=1, source_target_pairs={{0,1},{1,0},{2,3},{3,2},{4,5},{5,4},{6,7},{7,6},{8,9},{9,8},{10,11... | collective-permute-start | bytes 2359304 | tf_op jit(solution)/shard_map/ppermute | solution.py:487
  161.4 1.4 collective-permute-start.22
  (6 other events, 18.3 us)

commit v5 on v4

--- a/solution.py
+++ b/solution.py
@@ -339,7 +339,7 @@
     low, high = both_ways(og_3[: tok // 2], og_5[tok // 2 :])
     og_all = kept_out(og, og_1, og_2, og_3, low, high, og_5, og_6, og_7)
 
-    heads = 2
+    heads = 4
     grid = (pairs // heads,)
     lead = lambda j, p: (j, 0, 0)
     lead4 = lambda j, p: (j, 0, 0, 0)

time: 169 us -> 166 us (0.982)
  Pallas kernels: 44.1 us -> 40.9 us
  transfers between devices with their start and end apart: 29 -> 29, of which waited for: 10 -> 10; matrix products, arithmetic and copies ran while one was open for 3% -> 3% of each run, Pallas kernels for 24% -> 23%
where the time goes in v5:
time: 166 us; the launch traced here: 165 us
  starting transfers between devices  64.8 us (39%)
  Pallas kernels  40.9 us (25%)
  waiting for transfers between devices  37.6 us (23%)
  blocking collectives  15.3 us (9%)
  local copies, waits for them, and re-layouts  2.64 us (2%)
  other arithmetic  2.58 us (2%)
    ppermute x14, starting transfers between devices, from_ahead(): lax.ppermute(piece, axis, [((i + ahead) % size, i) for i in range(size)])  22.5 us
    all_to_all x1, blocking collectives, on_device(): parts = lax.all_to_all(grad_sum, plane, 0, 0, tiled=True)  15.3 us
    all_to_all x1, waiting for transfers between devices, on_device(): later = lax.all_to_all(later, plane, 0, 0, tiled=True)  9.54 us
    pallas_call x1, Pallas kernels, on_device(): call(backward_body, grid, [pair_spec] * 3 + [state_spec, state_spec, pair...  7.39 us
    all_to_all x1, waiting for transfers between devices, on_device(): grad_mine = lax.all_to_all(attn_grad, 'z', 0, 0, tiled=True)  6.6 us
    pallas_call x1, Pallas kernels, on_device(): call(functools.partial(weight_body, steps, nz), (2 * steps,), [att_spec]...  6.23 us
    ppermute x14, waiting for transfers between devices, from_ahead(): lax.ppermute(piece, axis, [((i + ahead) % size, i) for i in range(size)])  5.95 us
    ppermute x1, starting transfers between devices, on_device(): rows_other = swap(rows_mine)  5.61 us
  transfers between devices with their start and end apart: 29, of which 10 were waited for; matrix products, arithmetic and copies ran while one was open for 3% of the time, Pallas kernels for 23%

profile of v5, /device:TPU:1, one launch (start us, length us, event | category | flops | bytes accessed | tf_op | source)
XLA Modules:
  0.0 164.6 jit_solution(16493704204663419387)
XLA Ops:
  0.6 3.3 %collective-permute-start.1 = (bf16[128,2048]{1,0:T(8,128)(2,1)}, bf16[128,2048]{1,0:T(8,128)(2,1)S(1)}, u32[]{:S(2)}, u32[]{:S(2)}) collective-permute-start(bf16[128,2048]{1,0:T(8,128)(2,1)} %bitcast.36), channel_id=1, source_target_pairs={{0,1},{1,0},{2,3},{3,2},{4,5},{5,4},{6,7},{7,6},{8,9},{9,8},{10,11... | collective-permute-start | bytes 1572872 | tf_op jit(solution)/shard_map/ppermute | solution.py:331
  4.1 3.8 %collective-permute-start.3 = (bf16[128,2048]{1,0:T(8,128)(2,1)}, bf16[128,2048]{1,0:T(8,128)(2,1)S(1)}, u32[]{:S(2)}, u32[]{:S(2)}) collective-permute-start(bf16[128,2048]{1,0:T(8,128)(2,1)} %bitcast.32), channel_id=1, source_target_pairs={{32,0},{64,32},{96,64},{128,96},{160,128},{192,160},{224,192},{0,2... | collective-permute-start | bytes 1572872 | tf_op jit(solution)/shard_map/ppermute | solution.py:329
  8.0 3.4 %shard_map.84 = (bf16[8,2,128,128]{3,2,1,0:T(8,128)(2,1)}, bf16[8,2,128,128]{3,2,1,0:T(8,128)(2,1)}, f32[16,72,128]{2,1,0:T(8,128)}, f32[16,72,128]{2,1,0:T(8,128)}) custom-call(s32[4]{0:T(128)S(1)} %pad_add_fusion.place, bf16[128,2048]{1,0:T(8,128)(2,1)} %bitcast.37, bf16[128,2048]{1,0:T(8,128)(2,1)} %bitcast.39, ...), custom_call_target="tpu_custom_call" | custom-call | tf_op jit(solution)/shard_map/pallas_call | solution.py:354
  11.4 2.8 %collective-permute-start.11 = (bf16[8,2048]{1,0:T(8,128)(2,1)S(1)}, bf16[8,2048]{1,0:T(8,128)(2,1)S(1)}, u32[]{:S(2)}, u32[]{:S(2)}) collective-permute-start(bf16[8,2048]{1,0:T(8,128)(2,1)S(1)} %copy-done.8), channel_id=1, source_target_pairs={{2,0},{4,2},{6,4},{0,6},{3,1},{5,3},{7,5},{1,7},{10,8},{12,10},{14... | collective-permute-start | bytes 98312 | tf_op jit(solution)/shard_map/ppermute | solution.py:329
  15.1 4.3 %all-to-all-start = ((f32[16,72,128]{2,1,0:T(8,128)}), f32[16,72,128]{2,1,0:T(8,128)S(1)}, u32[]{:S(2)}, u32[]{:S(2)}) async-start(f32[16,72,128]{2,1,0:T(8,128)} %get-tuple-element.41), calls=%async_computation | async-start | bytes 1179648 | tf_op jit(solution)/shard_map/all_to_all | solution.py:375
  19.5 2.9 %collective-permute-start.12 = (bf16[8,2048]{1,0:T(8,128)(2,1)S(1)}, bf16[8,2048]{1,0:T(8,128)(2,1)S(1)}, u32[]{:S(2)}, u32[]{:S(2)}) collective-permute-start(bf16[8,2048]{1,0:T(8,128)(2,1)S(1)} %copy-done.8), channel_id=1, source_target_pairs={{4,0},{6,2},{0,4},{2,6},{5,1},{7,3},{1,5},{3,7},{12,8},{14,10},{8,... | collective-permute-start | bytes 98312 | tf_op jit(solution)/shard_map/ppermute | solution.py:329
  22.6 2.9 %collective-permute-start.4 = (bf16[128,2048]{1,0:T(8,128)(2,1)S(1)}, bf16[128,2048]{1,0:T(8,128)(2,1)}, u32[]{:S(2)}, u32[]{:S(2)}) collective-permute-start(bf16[128,2048]{1,0:T(8,128)(2,1)S(1)} %collective-permute-done.3.refs_1_), channel_id=1, source_target_pairs={{32,0},{64,32},{96,64},{128,96},{160,128},{192,160},{224,192},{0,2... | collective-permute-start | bytes 1572872 | tf_op jit(solution)/shard_map/ppermute | solution.py:329
  25.6 4.6 %all-to-all-done.in_ref = f32[16,72,128]{2,1,0:T(8,128)S(1)} async-done(((f32[16,72,128]{2,1,0:T(8,128)}), f32[16,72,128]{2,1,0:T(8,128)S(1)}, u32[]{:S(2)}, u32[]{:S(2)}) %all-to-all-start) | async-done | bytes 589856 | tf_op jit(solution)/shard_map/all_to_all | solution.py:375
  31.7 5.0 %all-to-all-start.1 = ((f32[16,72,128]{2,1,0:T(8,128)}), f32[16,72,128]{2,1,0:T(8,128)S(1)}, u32[]{:S(2)}, u32[]{:S(2)}) async-start(f32[16,72,128]{2,1,0:T(8,128)} %shard_map.85), calls=%async_computation.1 | async-start | bytes 1179648 | tf_op jit(solution)/shard_map/all_to_all | solution.py:382
  36.7 2.7 %collective-permute-start.14 = (bf16[4,8,2048]{2,1,0:T(8,128)(2,1)S(1)}, bf16[4,8,2048]{2,1,0:T(8,128)(2,1)S(1)}, u32[]{:S(2)}, u32[]{:S(2)}) collective-permute-start(bf16[4,8,2048]{2,1,0:T(8,128)(2,1)S(1)} %bitcast_dynamic-update-slice_fusion.3), channel_id=1, source_target_pairs={{8,0},{16,8},{24,16},{0,24},{9,1},{17,9},{25,17},{1,25},{10,2},{18... | collective-permute-start | bytes 393224 | tf_op jit(solution)/shard_map/ppermute | solution.py:329
  40.5 2.9 %collective-permute-start.5 = (bf16[128,2048]{1,0:T(8,128)(2,1)}, bf16[128,2048]{1,0:T(8,128)(2,1)S(1)}, u32[]{:S(2)}, u32[]{:S(2)}) collective-permute-start(bf16[128,2048]{1,0:T(8,128)(2,1)} %collective-permute-done.4.refs_2_), channel_id=1, source_target_pairs={{32,0},{64,32},{96,64},{128,96},{160,128},{192,160},{224,192},{0,2... | collective-permute-start | bytes 1572872 | tf_op jit(solution)/shard_map/ppermute | solution.py:329
  43.4 3.9 %all-to-all-done.1.in_ref = f32[16,72,128]{2,1,0:T(8,128)S(1)} async-done(((f32[16,72,128]{2,1,0:T(8,128)}), f32[16,72,128]{2,1,0:T(8,128)S(1)}, u32[]{:S(2)}, u32[]{:S(2)}) %all-to-all-start.1) | async-done | bytes 589856 | tf_op jit(solution)/shard_map/all_to_all | solution.py:382
  47.3 5.0 %shard_map.86 = (bf16[8,2,128,128]{3,2,1,0:T(8,128)(2,1)}, f32[16,72,128]{2,1,0:T(8,128)}, bf16[8,256,128]{2,1,0:T(8,128)(2,1)}, f32[8,2,128,128]{3,2,1,0:T(8,128)}, f32[8,2,128,128]{3,2,1,0:T(8,128)}) custom-call(s32[4]{0:T(128)S(1)} %pad_add_fusion.place, bf16[128,2048]{1,0:T(8,128)(2,1)} %bitcast.41, bf16[128,2048]{1,0:T(8,128)(2,1)S(1)} %collective-permute-done.q_other, ...), custom_call_target="tpu_custom_call" | custom-call | tf_op jit(solution)/shard_map/pallas_call | solution.py:383
  52.2 4.6 %all-to-all-start.2 = ((bf16[8,256,128]{2,1,0:T(8,128)(2,1)}), bf16[8,256,128]{2,1,0:T(8,128)(2,1)S(1)}, u32[]{:S(2)}, u32[]{:S(2)}) async-start(bf16[8,256,128]{2,1,0:T(8,128)(2,1)} %get-tuple-element.48), calls=%async_computation.2 | async-start | bytes 1048576 | tf_op jit(solution)/shard_map/all_to_all | solution.py:398
  57.9 5.6 %collective-permute-start.17 = (bf16[16,8,2048]{2,1,0:T(8,128)(2,1)S(1)}, bf16[16,8,2048]{2,1,0:T(8,128)(2,1)S(1)}, u32[]{:S(2)}, u32[]{:S(2)}) collective-permute-start(bf16[16,8,2048]{2,1,0:T(8,128)(2,1)S(1)} %bitcast.30), channel_id=1, source_target_pairs={{0,1},{1,0},{2,3},{3,2},{4,5},{5,4},{6,7},{7,6},{8,9},{9,8},{10,11... | collective-permute-start | bytes 1572872 | tf_op jit(solution)/shard_map/ppermute | solution.py:392
  63.5 3.0 %collective-permute-start.6 = (bf16[64,2048]{1,0:T(8,128)(2,1)S(1)}, bf16[64,2048]{1,0:T(8,128)(2,1)S(1)}, u32[]{:S(2)}, u32[]{:S(2)}) collective-permute-start(bf16[64,2048]{1,0:T(8,128)(2,1)S(1)} %slice.8), channel_id=1, source_target_pairs={{32,0},{64,32},{96,64},{128,96},{160,128},{192,160},{224,192},{0,2... | collective-permute-start | bytes 786440 | tf_op jit(solution)/shard_map/ppermute | solution.py:329
  67.5 5.1 %shard_map.87._ = bf16[8,128,256]{2,1,0:T(8,128)(2,1)} custom-call(s32[4]{0:T(128)S(1)} %pad_add_fusion.place, bf16[128,2048]{1,0:T(8,128)(2,1)} %bitcast.34, bf16[128,2048]{1,0:T(8,128)(2,1)} %copy-done.2, bf16[128,2048]{1,0:T(8,128)(2,1)} %collective-permute-done.4.refs_2_, bf16[128,2048]{1,0:T(8,128)(2,1)} %copy-done, bf16[128,2048]{1,0:T(8,128)(2,1)} %copy-done.1, ...), custom_call_target="tpu_custom_call" | custom-call | tf_op jit(solution)/shard_map/pallas_call | solution.py:404
  72.6 2.6 %collective-permute-done.6.low_ref.refs_4_ = bf16[64,2048]{1,0:T(8,128)(2,1)S(1)} collective-permute-done((bf16[64,2048]{1,0:T(8,128)(2,1)S(1)}, bf16[64,2048]{1,0:T(8,128)(2,1)S(1)}, u32[]{:S(2)}, u32[]{:S(2)}) %collective-permute-start.6) | collective-permute-done | bytes 262176 | tf_op jit(solution)/shard_map/ppermute | solution.py:329
  75.2 3.3 %collective-permute-done.10.high_ref.refs_5_ = bf16[64,2048]{1,0:T(8,128)(2,1)S(1)} collective-permute-done((bf16[64,2048]{1,0:T(8,128)(2,1)}, bf16[64,2048]{1,0:T(8,128)(2,1)S(1)}, u32[]{:S(2)}, u32[]{:S(2)}) %collective-permute-start.10) | collective-permute-done | bytes 262176 | tf_op jit(solution)/shard_map/ppermute | solution.py:329
  79.2 2.7 %shard_map.88 = bf16[8,128,256]{2,1,0:T(8,128)(2,1)} custom-call(s32[4]{0:T(128)S(1)} %pad_add_fusion.place, bf16[64,2048]{1,0:T(8,128)(2,1)} %copy-done.5, bf16[64,2048]{1,0:T(8,128)(2,1)} %copy-done.6, bf16[256,2048]{1,0:T(8,128)(2,1)S(1)} %bitcast.29, bf16[8,128,256]{2,1,0:T(8,128)(2,1)} %shard_map.87._), custom_call_target="tpu_custom_call", output_to_operand_aliasing={{}: (4, {})} | custom-call | tf_op jit(solution)/shard_map/pallas_call | solution.py:414
  81.9 3.7 %all-to-all-start.3 = ((bf16[8,128,256]{2,1,0:T(8,128)(2,1)}), bf16[8,128,256]{2,1,0:T(8,128)(2,1)S(1)}, u32[]{:S(2)}, u32[]{:S(2)}) async-start(bf16[8,128,256]{2,1,0:T(8,128)(2,1)} %shard_map.88), calls=%async_computation.3 | async-start | bytes 1048576 | tf_op jit(solution)/shard_map/all_to_all | solution.py:429
  88.7 6.2 %shard_map.89 = (f32[256,1024]{1,0:T(8,128)}, f32[256,1024]{1,0:T(8,128)}) custom-call(s32[4]{0:T(128)S(1)} %pad_add_fusion.place, bf16[8,256,128]{2,1,0:T(8,128)(2,1)S(1)} %all-to-all-done.2.mine_ref, bf16[8,256,128]{2,1,0:T(8,128)(2,1)S(1)} %collective-permute-done.18.other_ref, bf16[128,2048]{1,0:T(8,128)(2,1)} %bitcast.35, bf16[128,2048]{1,0:T(8,128)(2,1)} %copy-done.2, ...), custom_call_target="tpu_custom_call" | custom-call | tf_op jit(solution)/shard_map/pallas_call | solution.py:435
  95.0 6.6 %all-to-all-done.3.grad_ref = bf16[8,128,256]{2,1,0:T(8,128)(2,1)S(1)} async-done(((bf16[8,128,256]{2,1,0:T(8,128)(2,1)}), bf16[8,128,256]{2,1,0:T(8,128)(2,1)S(1)}, u32[]{:S(2)}, u32[]{:S(2)}) %all-to-all-start.3) | async-done | bytes 524320 | tf_op jit(solution)/shard_map/all_to_all | solution.py:429
  101.6 2.4 %collective-permute-start.19 = (bf16[8,128,256]{2,1,0:T(8,128)(2,1)S(1)}, bf16[8,128,256]{2,1,0:T(8,128)(2,1)S(1)}, u32[]{:S(2)}, u32[]{:S(2)}) collective-permute-start(bf16[8,128,256]{2,1,0:T(8,128)(2,1)S(1)} %all-to-all-done.3.grad_ref), channel_id=1, source_target_pairs={{0,1},{1,0},{2,3},{3,2},{4,5},{5,4},{6,7},{7,6},{8,9},{9,8},{10,11... | collective-permute-start | bytes 1572872 | tf_op jit(solution)/shard_map/ppermute | solution.py:446
  106.3 4.0 %shard_map.90 = (f32[8,2,128,128]{3,2,1,0:T(8,128)}, f32[8,2,128,128]{3,2,1,0:T(8,128)}, f32[16,72,128]{2,1,0:T(8,128)}, f32[16,72,128]{2,1,0:T(8,128)}) custom-call(s32[4]{0:T(128)S(1)} %pad_add_fusion.place, bf16[8,2,128,128]{3,2,1,0:T(8,128)(2,1)} %get-tuple-element.43.queries, f32[8,2,128,128]{3,2,1,0:T(8,128)} %get-tuple-element.45.o_ref, ...), custom_call_target="tpu_custom_call" | custom-call | tf_op jit(solution)/shard_map/pallas_call | solution.py:450
  110.2 15.3 %all_to_all.35.in_ref = f32[16,72,128]{2,1,0:T(8,128)S(1)} all-to-all(f32[16,72,128]{2,1,0:T(8,128)} %get-tuple-element.59), channel_id=1, replica_groups=mesh['z'=8,'x'=4,'y'=4,'c'=2] {'x','y'}, dimensions={0} | all-to-all | bytes 1179648 | tf_op jit(solution)/shard_map/all_to_all | solution.py:461
  126.9 3.6 %all-to-all-start.5 = ((f32[16,72,128]{2,1,0:T(8,128)}), f32[16,72,128]{2,1,0:T(8,128)S(1)}, u32[]{:S(2)}, u32[]{:S(2)}) async-start(f32[16,72,128]{2,1,0:T(8,128)} %shard_map.91), calls=%async_computation.5 | async-start | bytes 1179648 | tf_op jit(solution)/shard_map/all_to_all | solution.py:468
  131.5 9.5 %all-to-all-done.5.later_ref = f32[16,72,128]{2,1,0:T(8,128)S(1)} async-done(((f32[16,72,128]{2,1,0:T(8,128)}), f32[16,72,128]{2,1,0:T(8,128)S(1)}, u32[]{:S(2)}, u32[]{:S(2)}) %all-to-all-start.5) | async-done | bytes 589856 | tf_op jit(solution)/shard_map/all_to_all | solution.py:468
  141.0 3.7 %all-to-all-start.6 = ((bf16[16,16,1024]{2,1,0:T(8,128)(2,1)}), bf16[16,16,1024]{2,1,0:T(8,128)(2,1)S(1)}, u32[]{:S(2)}, u32[]{:S(2)}) async-start(bf16[16,16,1024]{2,1,0:T(8,128)(2,1)} %bitcast.18), calls=%async_computation.6 | async-start | bytes 1048576 | tf_op jit(solution)/shard_map/all_to_all | solution.py:471
  144.8 7.4 %shard_map.92 = (bf16[8,3,128,128]{3,2,1,0:T(8,128)(2,1)}, bf16[8,3,128,128]{3,2,1,0:T(8,128)(2,1)}) custom-call(s32[4]{0:T(128)S(1)} %pad_add_fusion.place, bf16[8,2,128,128]{3,2,1,0:T(8,128)(2,1)} %get-tuple-element.43.queries, bf16[8,2,128,128]{3,2,1,0:T(8,128)(2,1)} %get-tuple-element.39.keys, bf16[8,2,128,128]{3,2,1,0:T(8,128)(2,1)} %get-tuple-element.40.values, ...), custom_call_target="tpu_custom_call" | custom-call | tf_op jit(solution)/shard_map/pallas_call | solution.py:473
  154.0 3.3 %collective-permute-start.21 = (bf16[8,3,128,128]{3,2,1,0:T(8,128)(2,1)}, bf16[8,3,128,128]{3,2,1,0:T(8,128)(2,1)S(1)}, u32[]{:S(2)}, u32[]{:S(2)}) collective-permute-start(bf16[8,3,128,128]{3,2,1,0:T(8,128)(2,1)} %get-tuple-element.67), channel_id=1, source_target_pairs={{0,1},{1,0},{2,3},{3,2},{4,5},{5,4},{6,7},{7,6},{8,9},{9,8},{10,11... | collective-permute-start | bytes 2359304 | tf_op jit(solution)/shard_map/ppermute | solution.py:487
  161.4 3.2 %shard_map.93 = (bf16[128,2048]{1,0:T(8,128)(2,1)}, bf16[128,2048]{1,0:T(8,128)(2,1)}, bf16[128,2048]{1,0:T(8,128)(2,1)}) custom-call(s32[4]{0:T(128)S(1)} %pad_add_fusion.place, bf16[8,3,128,128]{3,2,1,0:T(8,128)(2,1)} %get-tuple-element.64.keep_ref, bf16[8,3,128,128]{3,2,1,0:T(8,128)(2,1)S(1)} %collective-permute-done.21.back_ref), custom_call_target="tpu_custom_call" | custom-call | tf_op jit(solution)/shard_map/pallas_call | solution.py:500
  (70 shorter events, 20.5 us)
Async XLA Ops:
  0.6 7.4 %collective-permute-start.1 = (bf16[128,2048]{1,0:T(8,128)(2,1)}, bf16[128,2048]{1,0:T(8,128)(2,1)S(1)}, u32[]{:S(2)}, u32[]{:S(2)}) collective-permute-start(bf16[128,2048]{1,0:T(8,128)(2,1)} %bitcast.36), channel_id=1, source_target_pairs={{0,1},{1,0},{2,3},{3,2},{4,5},{5,4},{6,7},{7,6},{8,9},{9,8},{10,11... | collective-permute-start | bytes 1572872 | tf_op jit(solution)/shard_map/ppermute | solution.py:331
  4.0 4.0 %collective-permute-start.2 = (bf16[128,2048]{1,0:T(8,128)(2,1)}, bf16[128,2048]{1,0:T(8,128)(2,1)S(1)}, u32[]{:S(2)}, u32[]{:S(2)}) collective-permute-start(bf16[128,2048]{1,0:T(8,128)(2,1)} %bitcast.38), channel_id=1, source_target_pairs={{0,1},{1,0},{2,3},{3,2},{4,5},{5,4},{6,7},{7,6},{8,9},{9,8},{10,11... | collective-permute-start | bytes 1572872 | tf_op jit(solution)/shard_map/ppermute | solution.py:331
  4.1 18.3 %collective-permute-start.3 = (bf16[128,2048]{1,0:T(8,128)(2,1)}, bf16[128,2048]{1,0:T(8,128)(2,1)S(1)}, u32[]{:S(2)}, u32[]{:S(2)}) collective-permute-start(bf16[128,2048]{1,0:T(8,128)(2,1)} %bitcast.32), channel_id=1, source_target_pairs={{32,0},{64,32},{96,64},{128,96},{160,128},{192,160},{224,192},{0,2... | collective-permute-start | bytes 1572872 | tf_op jit(solution)/shard_map/ppermute | solution.py:329
  7.9 14.7 %collective-permute-start.7 = (bf16[128,2048]{1,0:T(8,128)(2,1)}, bf16[128,2048]{1,0:T(8,128)(2,1)S(1)}, u32[]{:S(2)}, u32[]{:S(2)}) collective-permute-start(bf16[128,2048]{1,0:T(8,128)(2,1)} %bitcast.33), channel_id=1, source_target_pairs={{224,0},{0,32},{32,64},{64,96},{96,128},{128,160},{160,192},{192,2... | collective-permute-start | bytes 1572872 | tf_op jit(solution)/shard_map/ppermute | solution.py:329
  8.0 6.2 %copy-start.7 = (bf16[1,128,2048]{2,1,0:T(8,128)(2,1)S(1)}, bf16[1,128,2048]{2,1,0:T(8,128)(2,1)}, u32[]{:S(2)}) copy-start(bf16[1,128,2048]{2,1,0:T(8,128)(2,1)} %param.5) | copy-start | bytes 1572868
  11.4 14.2 %collective-permute-start.11 = (bf16[8,2048]{1,0:T(8,128)(2,1)S(1)}, bf16[8,2048]{1,0:T(8,128)(2,1)S(1)}, u32[]{:S(2)}, u32[]{:S(2)}) collective-permute-start(bf16[8,2048]{1,0:T(8,128)(2,1)S(1)} %copy-done.8), channel_id=1, source_target_pairs={{2,0},{4,2},{6,4},{0,6},{3,1},{5,3},{7,5},{1,7},{10,8},{12,10},{14... | collective-permute-start | bytes 98312 | tf_op jit(solution)/shard_map/ppermute | solution.py:329
  14.2 25.7 %collective-permute-start = (bf16[128,2048]{1,0:T(8,128)(2,1)S(1)}, bf16[128,2048]{1,0:T(8,128)(2,1)S(1)}, u32[]{:S(2)}, u32[]{:S(2)}) collective-permute-start(bf16[128,2048]{1,0:T(8,128)(2,1)S(1)} %bitcast.42), channel_id=1, source_target_pairs={{0,1},{1,0},{2,3},{3,2},{4,5},{5,4},{6,7},{7,6},{8,9},{9,8},{10,11... | collective-permute-start | bytes 1572872 | tf_op jit(solution)/shard_map/ppermute | solution.py:331
  15.1 15.1 %all-to-all-start = ((f32[16,72,128]{2,1,0:T(8,128)}), f32[16,72,128]{2,1,0:T(8,128)S(1)}, u32[]{:S(2)}, u32[]{:S(2)}) async-start(f32[16,72,128]{2,1,0:T(8,128)} %get-tuple-element.41), calls=%async_computation | async-start | bytes 1179648 | tf_op jit(solution)/shard_map/all_to_all | solution.py:375
  19.5 6.2 %collective-permute-start.12 = (bf16[8,2048]{1,0:T(8,128)(2,1)S(1)}, bf16[8,2048]{1,0:T(8,128)(2,1)S(1)}, u32[]{:S(2)}, u32[]{:S(2)}) collective-permute-start(bf16[8,2048]{1,0:T(8,128)(2,1)S(1)} %copy-done.8), channel_id=1, source_target_pairs={{4,0},{6,2},{0,4},{2,6},{5,1},{7,3},{1,5},{3,7},{12,8},{14,10},{8,... | collective-permute-start | bytes 98312 | tf_op jit(solution)/shard_map/ppermute | solution.py:329
  22.3 9.3 %copy-start.2 = (bf16[128,2048]{1,0:T(8,128)(2,1)}, bf16[128,2048]{1,0:T(8,128)(2,1)S(1)}, u32[]{:S(2)}) copy-start(bf16[128,2048]{1,0:T(8,128)(2,1)S(1)} %collective-permute-done.3.refs_1_) | copy-start | bytes 1572868
  22.3 14.3 %collective-permute-start.13 = (bf16[8,2048]{1,0:T(8,128)(2,1)S(1)}, bf16[8,2048]{1,0:T(8,128)(2,1)S(1)}, u32[]{:S(2)}, u32[]{:S(2)}) collective-permute-start(bf16[8,2048]{1,0:T(8,128)(2,1)S(1)} %copy-done.8), channel_id=1, source_target_pairs={{6,0},{0,2},{2,4},{4,6},{7,1},{1,3},{3,5},{5,7},{14,8},{8,10},{10,... | collective-permute-start | bytes 98312 | tf_op jit(solution)/shard_map/ppermute | solution.py:329
  22.6 9.0 %copy-start.3 = (bf16[128,2048]{1,0:T(8,128)(2,1)}, bf16[128,2048]{1,0:T(8,128)(2,1)S(1)}, u32[]{:S(2)}) copy-start(bf16[128,2048]{1,0:T(8,128)(2,1)S(1)} %collective-permute-done.7.refs_6_.refs_8_) | copy-start | bytes 1572868
  22.6 17.9 %collective-permute-start.4 = (bf16[128,2048]{1,0:T(8,128)(2,1)S(1)}, bf16[128,2048]{1,0:T(8,128)(2,1)}, u32[]{:S(2)}, u32[]{:S(2)}) collective-permute-start(bf16[128,2048]{1,0:T(8,128)(2,1)S(1)} %collective-permute-done.3.refs_1_), channel_id=1, source_target_pairs={{32,0},{64,32},{96,64},{128,96},{160,128},{192,160},{224,192},{0,2... | collective-permute-start | bytes 1572872 | tf_op jit(solution)/shard_map/ppermute | solution.py:329
  25.6 17.9 %collective-permute-start.8 = (bf16[128,2048]{1,0:T(8,128)(2,1)S(1)}, bf16[128,2048]{1,0:T(8,128)(2,1)}, u32[]{:S(2)}, u32[]{:S(2)}) collective-permute-start(bf16[128,2048]{1,0:T(8,128)(2,1)S(1)} %collective-permute-done.7.refs_6_.refs_8_), channel_id=1, source_target_pairs={{224,0},{0,32},{32,64},{64,96},{96,128},{128,160},{160,192},{192,2... | collective-permute-start | bytes 1572872 | tf_op jit(solution)/shard_map/ppermute | solution.py:329
  31.7 15.6 %all-to-all-start.1 = ((f32[16,72,128]{2,1,0:T(8,128)}), f32[16,72,128]{2,1,0:T(8,128)S(1)}, u32[]{:S(2)}, u32[]{:S(2)}) async-start(f32[16,72,128]{2,1,0:T(8,128)} %shard_map.85), calls=%async_computation.1 | async-start | bytes 1179648 | tf_op jit(solution)/shard_map/all_to_all | solution.py:382
  36.7 20.2 %collective-permute-start.14 = (bf16[4,8,2048]{2,1,0:T(8,128)(2,1)S(1)}, bf16[4,8,2048]{2,1,0:T(8,128)(2,1)S(1)}, u32[]{:S(2)}, u32[]{:S(2)}) collective-permute-start(bf16[4,8,2048]{2,1,0:T(8,128)(2,1)S(1)} %bitcast_dynamic-update-slice_fusion.3), channel_id=1, source_target_pairs={{8,0},{16,8},{24,16},{0,24},{9,1},{17,9},{25,17},{1,25},{10,2},{18... | collective-permute-start | bytes 393224 | tf_op jit(solution)/shard_map/ppermute | solution.py:329
  39.3 17.5 %collective-permute-start.15 = (bf16[4,8,2048]{2,1,0:T(8,128)(2,1)S(1)}, bf16[4,8,2048]{2,1,0:T(8,128)(2,1)}, u32[]{:S(2)}, u32[]{:S(2)}) collective-permute-start(bf16[4,8,2048]{2,1,0:T(8,128)(2,1)S(1)} %bitcast_dynamic-update-slice_fusion.3), channel_id=1, source_target_pairs={{16,0},{24,8},{0,16},{8,24},{17,1},{25,9},{1,17},{9,25},{18,2},{26... | collective-permute-start | bytes 393224 | tf_op jit(solution)/shard_map/ppermute | solution.py:329
  39.9 16.9 %collective-permute-start.16 = (bf16[4,8,2048]{2,1,0:T(8,128)(2,1)S(1)}, bf16[4,8,2048]{2,1,0:T(8,128)(2,1)S(1)}, u32[]{:S(2)}, u32[]{:S(2)}) collective-permute-start(bf16[4,8,2048]{2,1,0:T(8,128)(2,1)S(1)} %bitcast_dynamic-update-slice_fusion.3), channel_id=1, source_target_pairs={{24,0},{0,8},{8,16},{16,24},{25,1},{1,9},{9,17},{17,25},{26,2},{2,... | collective-permute-start | bytes 393224 | tf_op jit(solution)/shard_map/ppermute | solution.py:329
  40.5 23.0 %collective-permute-start.5 = (bf16[128,2048]{1,0:T(8,128)(2,1)}, bf16[128,2048]{1,0:T(8,128)(2,1)S(1)}, u32[]{:S(2)}, u32[]{:S(2)}) collective-permute-start(bf16[128,2048]{1,0:T(8,128)(2,1)} %collective-permute-done.4.refs_2_), channel_id=1, source_target_pairs={{32,0},{64,32},{96,64},{128,96},{160,128},{192,160},{224,192},{0,2... | collective-permute-start | bytes 1572872 | tf_op jit(solution)/shard_map/ppermute | solution.py:329
  43.4 23.1 %collective-permute-start.9 = (bf16[128,2048]{1,0:T(8,128)(2,1)}, bf16[128,2048]{1,0:T(8,128)(2,1)S(1)}, u32[]{:S(2)}, u32[]{:S(2)}) collective-permute-start(bf16[128,2048]{1,0:T(8,128)(2,1)} %collective-permute-done.8.refs_5_.refs_7_), channel_id=1, source_target_pairs={{224,0},{0,32},{32,64},{64,96},{96,128},{128,160},{160,192},{192,2... | collective-permute-start | bytes 1572872 | tf_op jit(solution)/shard_map/ppermute | solution.py:329
  52.2 29.7 %all-to-all-start.2 = ((bf16[8,256,128]{2,1,0:T(8,128)(2,1)}), bf16[8,256,128]{2,1,0:T(8,128)(2,1)S(1)}, u32[]{:S(2)}, u32[]{:S(2)}) async-start(bf16[8,256,128]{2,1,0:T(8,128)(2,1)} %get-tuple-element.48), calls=%async_computation.2 | async-start | bytes 1048576 | tf_op jit(solution)/shard_map/all_to_all | solution.py:398
  57.9 9.5 %collective-permute-start.17 = (bf16[16,8,2048]{2,1,0:T(8,128)(2,1)S(1)}, bf16[16,8,2048]{2,1,0:T(8,128)(2,1)S(1)}, u32[]{:S(2)}, u32[]{:S(2)}) collective-permute-start(bf16[16,8,2048]{2,1,0:T(8,128)(2,1)S(1)} %bitcast.30), channel_id=1, source_target_pairs={{0,1},{1,0},{2,3},{3,2},{4,5},{5,4},{6,7},{7,6},{8,9},{9,8},{10,11... | collective-permute-start | bytes 1572872 | tf_op jit(solution)/shard_map/ppermute | solution.py:392
  63.5 11.7 %collective-permute-start.6 = (bf16[64,2048]{1,0:T(8,128)(2,1)S(1)}, bf16[64,2048]{1,0:T(8,128)(2,1)S(1)}, u32[]{:S(2)}, u32[]{:S(2)}) collective-permute-start(bf16[64,2048]{1,0:T(8,128)(2,1)S(1)} %slice.8), channel_id=1, source_target_pairs={{32,0},{64,32},{96,64},{128,96},{160,128},{192,160},{224,192},{0,2... | collective-permute-start | bytes 786440 | tf_op jit(solution)/shard_map/ppermute | solution.py:329
  67.3 11.2 %collective-permute-start.10 = (bf16[64,2048]{1,0:T(8,128)(2,1)}, bf16[64,2048]{1,0:T(8,128)(2,1)S(1)}, u32[]{:S(2)}, u32[]{:S(2)}) collective-permute-start(bf16[64,2048]{1,0:T(8,128)(2,1)} %slice.9), channel_id=1, source_target_pairs={{224,0},{0,32},{32,64},{64,96},{96,128},{128,160},{160,192},{192,2... | collective-permute-start | bytes 786440 | tf_op jit(solution)/shard_map/ppermute | solution.py:329
  81.9 19.7 %all-to-all-start.3 = ((bf16[8,128,256]{2,1,0:T(8,128)(2,1)}), bf16[8,128,256]{2,1,0:T(8,128)(2,1)S(1)}, u32[]{:S(2)}, u32[]{:S(2)}) async-start(bf16[8,128,256]{2,1,0:T(8,128)(2,1)} %shard_map.88), calls=%async_computation.3 | async-start | bytes 1048576 | tf_op jit(solution)/shard_map/all_to_all | solution.py:429
  85.6 3.2 %collective-permute-start.18 = (bf16[8,256,128]{2,1,0:T(8,128)(2,1)S(1)}, bf16[8,256,128]{2,1,0:T(8,128)(2,1)S(1)}, u32[]{:S(2)}, u32[]{:S(2)}) collective-permute-start(bf16[8,256,128]{2,1,0:T(8,128)(2,1)S(1)} %all-to-all-done.2.mine_ref), channel_id=1, source_target_pairs={{0,1},{1,0},{2,3},{3,2},{4,5},{5,4},{6,7},{7,6},{8,9},{9,8},{10,11... | collective-permute-start | bytes 1572872 | tf_op jit(solution)/shard_map/ppermute | solution.py:399
  101.6 4.7 %collective-permute-start.19 = (bf16[8,128,256]{2,1,0:T(8,128)(2,1)S(1)}, bf16[8,128,256]{2,1,0:T(8,128)(2,1)S(1)}, u32[]{:S(2)}, u32[]{:S(2)}) collective-permute-start(bf16[8,128,256]{2,1,0:T(8,128)(2,1)S(1)} %all-to-all-done.3.grad_ref), channel_id=1, source_target_pairs={{0,1},{1,0},{2,3},{3,2},{4,5},{5,4},{6,7},{7,6},{8,9},{9,8},{10,11... | collective-permute-start | bytes 1572872 | tf_op jit(solution)/shard_map/ppermute | solution.py:446
  104.0 26.5 %collective-permute-start.20 = (f32[256,1024]{1,0:T(8,128)}, f32[256,1024]{1,0:T(8,128)S(1)}, u32[]{:S(2)}, u32[]{:S(2)}) collective-permute-start(f32[256,1024]{1,0:T(8,128)} %get-tuple-element.61), channel_id=1, source_target_pairs={{0,1},{1,0},{2,3},{3,2},{4,5},{5,4},{6,7},{7,6},{8,9},{9,8},{10,11... | collective-permute-start | bytes 3145736 | tf_op jit(solution)/shard_map/ppermute | solution.py:447
  126.9 14.1 %all-to-all-start.5 = ((f32[16,72,128]{2,1,0:T(8,128)}), f32[16,72,128]{2,1,0:T(8,128)S(1)}, u32[]{:S(2)}, u32[]{:S(2)}) async-start(f32[16,72,128]{2,1,0:T(8,128)} %shard_map.91), calls=%async_computation.5 | async-start | bytes 1179648 | tf_op jit(solution)/shard_map/all_to_all | solution.py:468
  141.0 13.0 %all-to-all-start.6 = ((bf16[16,16,1024]{2,1,0:T(8,128)(2,1)}), bf16[16,16,1024]{2,1,0:T(8,128)(2,1)S(1)}, u32[]{:S(2)}, u32[]{:S(2)}) async-start(bf16[16,16,1024]{2,1,0:T(8,128)(2,1)} %bitcast.18), calls=%async_computation.6 | async-start | bytes 1048576 | tf_op jit(solution)/shard_map/all_to_all | solution.py:471
  154.0 7.4 %collective-permute-start.21 = (bf16[8,3,128,128]{3,2,1,0:T(8,128)(2,1)}, bf16[8,3,128,128]{3,2,1,0:T(8,128)(2,1)S(1)}, u32[]{:S(2)}, u32[]{:S(2)}) collective-permute-start(bf16[8,3,128,128]{3,2,1,0:T(8,128)(2,1)} %get-tuple-element.67), channel_id=1, source_target_pairs={{0,1},{1,0},{2,3},{3,2},{4,5},{5,4},{6,7},{7,6},{8,9},{9,8},{10,11... | collective-permute-start | bytes 2359304 | tf_op jit(solution)/shard_map/ppermute | solution.py:487
  158.5 1.4 collective-permute-start.22
  (6 other events, 17.2 us)

commit v6 on v5

--- a/solution.py
+++ b/solution.py
@@ -278,7 +278,10 @@
     send_ref[...] = held[1 - me]
 
 
-def merge_body(place, keep_ref, back_ref, q_ref, k_ref, v_ref):
+def merge_body(place, keep_ref, back_ref, kept_ref, got_ref, q_ref, k_ref, v_ref, w_ref):
+    half = kept_ref.shape[1]
+    w_ref[:, pl.ds(pl.multiple_of(place[0] * half, DH), half)] = kept_ref[...]
+    w_ref[:, pl.ds(pl.multiple_of((1 - place[0]) * half, DH), half)] = got_ref[...]
     for head in range(keep_ref.shape[0]):
         mine = pl.ds(pl.multiple_of((2 * head + place[0]) * DH, DH), DH)
         other = pl.ds(pl.multiple_of((2 * head + 1 - place[0]) * DH, DH), DH)
@@ -492,17 +495,13 @@
         [(*whole(8, half), (8, half), F32)] * 2,
     )(place, shares)
     weight_got = swap(weight_moved)
-    weight_grad = jnp.where(
-        me == 0,
-        jnp.concatenate([weight_kept, weight_got], axis=1),
-        jnp.concatenate([weight_got, weight_kept], axis=1),
-    )
-    grads = call(
+    *grads, weight_grad = call(
         merge_body,
         (1,),
-        [whole(pairs, 3, tok, DH)] * 2,
-        [(*whole(tok, width), (tok, width), BF)] * 3,
-    )(place, *kept_out(keep), back)
+        [whole(pairs, 3, tok, DH)] * 2 + [whole(8, half)] * 2,
+        [(*whole(tok, width), (tok, width), BF)] * 3
+        + [(*whole(8, model), (8, model), F32)],
+    )(place, *kept_out(keep), back, weight_kept, weight_got)
     return (*(grad.reshape(1, tok, width) for grad in grads), weight_grad)
 
 

time: 166 us -> 165 us (level)
  transfers between devices with their start and end apart: 29 -> 29, of which waited for: 10 -> 10; matrix products, arithmetic and copies ran while one was open for 3% -> 2% of each run, Pallas kernels for 23% -> 23%
where the time goes in v6:
time: 165 us; the launch traced here: 164 us
  starting transfers between devices  64.7 us (39%)
  Pallas kernels  40.9 us (25%)
  waiting for transfers between devices  37.6 us (23%)
  blocking collectives  15.3 us (9%)
  local copies, waits for them, and re-layouts  3.42 us (2%)
    ppermute x14, starting transfers between devices, from_ahead(): lax.ppermute(piece, axis, [((i + ahead) % size, i) for i in range(size)])  22.5 us
    all_to_all x1, blocking collectives, on_device(): parts = lax.all_to_all(grad_sum, plane, 0, 0, tiled=True)  15.3 us
    all_to_all x1, waiting for transfers between devices, on_device(): later = lax.all_to_all(later, plane, 0, 0, tiled=True)  9.56 us
    pallas_call x1, Pallas kernels, on_device(): call(backward_body, grid, [pair_spec] * 3 + [state_spec, state_spec, pair...  7.4 us
    all_to_all x1, waiting for transfers between devices, on_device(): grad_mine = lax.all_to_all(attn_grad, 'z', 0, 0, tiled=True)  6.6 us
    pallas_call x1, Pallas kernels, on_device(): call(functools.partial(weight_body, steps, nz), (2 * steps,), [att_spec]...  6.26 us
    ppermute x14, waiting for transfers between devices, from_ahead(): lax.ppermute(piece, axis, [((i + ahead) % size, i) for i in range(size)])  5.94 us
    ppermute x1, starting transfers between devices, on_device(): rows_other = swap(rows_mine)  5.61 us
  transfers between devices with their start and end apart: 29, of which 10 were waited for; matrix products, arithmetic and copies ran while one was open for 2% of the time, Pallas kernels for 23%

profile of v6, /device:TPU:1, one launch (start us, length us, event | category | flops | bytes accessed | tf_op | source)
XLA Modules:
  0.0 163.9 jit_solution(12489454264224308494)
XLA Ops:
  0.6 3.3 %collective-permute-start.1 = (bf16[128,2048]{1,0:T(8,128)(2,1)}, bf16[128,2048]{1,0:T(8,128)(2,1)S(1)}, u32[]{:S(2)}, u32[]{:S(2)}) collective-permute-start(bf16[128,2048]{1,0:T(8,128)(2,1)} %bitcast.36), channel_id=1, source_target_pairs={{0,1},{1,0},{2,3},{3,2},{4,5},{5,4},{6,7},{7,6},{8,9},{9,8},{10,11... | collective-permute-start | bytes 1572872 | tf_op jit(solution)/shard_map/ppermute | solution.py:334
  4.1 3.8 %collective-permute-start.3 = (bf16[128,2048]{1,0:T(8,128)(2,1)}, bf16[128,2048]{1,0:T(8,128)(2,1)S(1)}, u32[]{:S(2)}, u32[]{:S(2)}) collective-permute-start(bf16[128,2048]{1,0:T(8,128)(2,1)} %bitcast.32), channel_id=1, source_target_pairs={{32,0},{64,32},{96,64},{128,96},{160,128},{192,160},{224,192},{0,2... | collective-permute-start | bytes 1572872 | tf_op jit(solution)/shard_map/ppermute | solution.py:332
  8.0 3.3 %shard_map.84 = (bf16[8,2,128,128]{3,2,1,0:T(8,128)(2,1)}, bf16[8,2,128,128]{3,2,1,0:T(8,128)(2,1)}, f32[16,72,128]{2,1,0:T(8,128)}, f32[16,72,128]{2,1,0:T(8,128)}) custom-call(s32[4]{0:T(128)S(1)} %pad_add_fusion.place, bf16[128,2048]{1,0:T(8,128)(2,1)} %bitcast.37, bf16[128,2048]{1,0:T(8,128)(2,1)} %bitcast.39, ...), custom_call_target="tpu_custom_call" | custom-call | tf_op jit(solution)/shard_map/pallas_call | solution.py:357
  11.4 2.8 %collective-permute-start.11 = (bf16[8,2048]{1,0:T(8,128)(2,1)S(1)}, bf16[8,2048]{1,0:T(8,128)(2,1)S(1)}, u32[]{:S(2)}, u32[]{:S(2)}) collective-permute-start(bf16[8,2048]{1,0:T(8,128)(2,1)S(1)} %copy-done.9), channel_id=1, source_target_pairs={{2,0},{4,2},{6,4},{0,6},{3,1},{5,3},{7,5},{1,7},{10,8},{12,10},{14... | collective-permute-start | bytes 98312 | tf_op jit(solution)/shard_map/ppermute | solution.py:332
  15.1 4.3 %all-to-all-start = ((f32[16,72,128]{2,1,0:T(8,128)}), f32[16,72,128]{2,1,0:T(8,128)S(1)}, u32[]{:S(2)}, u32[]{:S(2)}) async-start(f32[16,72,128]{2,1,0:T(8,128)} %get-tuple-element.42), calls=%async_computation | async-start | bytes 1179648 | tf_op jit(solution)/shard_map/all_to_all | solution.py:378
  19.5 2.9 %collective-permute-start.12 = (bf16[8,2048]{1,0:T(8,128)(2,1)S(1)}, bf16[8,2048]{1,0:T(8,128)(2,1)S(1)}, u32[]{:S(2)}, u32[]{:S(2)}) collective-permute-start(bf16[8,2048]{1,0:T(8,128)(2,1)S(1)} %copy-done.9), channel_id=1, source_target_pairs={{4,0},{6,2},{0,4},{2,6},{5,1},{7,3},{1,5},{3,7},{12,8},{14,10},{8,... | collective-permute-start | bytes 98312 | tf_op jit(solution)/shard_map/ppermute | solution.py:332
  22.6 2.9 %collective-permute-start.4 = (bf16[128,2048]{1,0:T(8,128)(2,1)S(1)}, bf16[128,2048]{1,0:T(8,128)(2,1)}, u32[]{:S(2)}, u32[]{:S(2)}) collective-permute-start(bf16[128,2048]{1,0:T(8,128)(2,1)S(1)} %collective-permute-done.3.refs_1_), channel_id=1, source_target_pairs={{32,0},{64,32},{96,64},{128,96},{160,128},{192,160},{224,192},{0,2... | collective-permute-start | bytes 1572872 | tf_op jit(solution)/shard_map/ppermute | solution.py:332
  25.6 4.6 %all-to-all-done.in_ref = f32[16,72,128]{2,1,0:T(8,128)S(1)} async-done(((f32[16,72,128]{2,1,0:T(8,128)}), f32[16,72,128]{2,1,0:T(8,128)S(1)}, u32[]{:S(2)}, u32[]{:S(2)}) %all-to-all-start) | async-done | bytes 589856 | tf_op jit(solution)/shard_map/all_to_all | solution.py:378
  31.6 5.0 %all-to-all-start.1 = ((f32[16,72,128]{2,1,0:T(8,128)}), f32[16,72,128]{2,1,0:T(8,128)S(1)}, u32[]{:S(2)}, u32[]{:S(2)}) async-start(f32[16,72,128]{2,1,0:T(8,128)} %shard_map.85), calls=%async_computation.1 | async-start | bytes 1179648 | tf_op jit(solution)/shard_map/all_to_all | solution.py:385
  36.6 2.7 %collective-permute-start.14 = (bf16[4,8,2048]{2,1,0:T(8,128)(2,1)S(1)}, bf16[4,8,2048]{2,1,0:T(8,128)(2,1)S(1)}, u32[]{:S(2)}, u32[]{:S(2)}) collective-permute-start(bf16[4,8,2048]{2,1,0:T(8,128)(2,1)S(1)} %bitcast_dynamic-update-slice_fusion.3), channel_id=1, source_target_pairs={{8,0},{16,8},{24,16},{0,24},{9,1},{17,9},{25,17},{1,25},{10,2},{18... | collective-permute-start | bytes 393224 | tf_op jit(solution)/shard_map/ppermute | solution.py:332
  40.5 2.9 %collective-permute-start.5 = (bf16[128,2048]{1,0:T(8,128)(2,1)}, bf16[128,2048]{1,0:T(8,128)(2,1)S(1)}, u32[]{:S(2)}, u32[]{:S(2)}) collective-permute-start(bf16[128,2048]{1,0:T(8,128)(2,1)} %collective-permute-done.4.refs_2_), channel_id=1, source_target_pairs={{32,0},{64,32},{96,64},{128,96},{160,128},{192,160},{224,192},{0,2... | collective-permute-start | bytes 1572872 | tf_op jit(solution)/shard_map/ppermute | solution.py:332
  43.4 3.9 %all-to-all-done.1.in_ref = f32[16,72,128]{2,1,0:T(8,128)S(1)} async-done(((f32[16,72,128]{2,1,0:T(8,128)}), f32[16,72,128]{2,1,0:T(8,128)S(1)}, u32[]{:S(2)}, u32[]{:S(2)}) %all-to-all-start.1) | async-done | bytes 589856 | tf_op jit(solution)/shard_map/all_to_all | solution.py:385
  47.3 4.9 %shard_map.86 = (bf16[8,2,128,128]{3,2,1,0:T(8,128)(2,1)}, f32[16,72,128]{2,1,0:T(8,128)}, bf16[8,256,128]{2,1,0:T(8,128)(2,1)}, f32[8,2,128,128]{3,2,1,0:T(8,128)}, f32[8,2,128,128]{3,2,1,0:T(8,128)}) custom-call(s32[4]{0:T(128)S(1)} %pad_add_fusion.place, bf16[128,2048]{1,0:T(8,128)(2,1)} %bitcast.41, bf16[128,2048]{1,0:T(8,128)(2,1)S(1)} %collective-permute-done.q_other, ...), custom_call_target="tpu_custom_call" | custom-call | tf_op jit(solution)/shard_map/pallas_call | solution.py:386
  52.2 4.6 %all-to-all-start.2 = ((bf16[8,256,128]{2,1,0:T(8,128)(2,1)}), bf16[8,256,128]{2,1,0:T(8,128)(2,1)S(1)}, u32[]{:S(2)}, u32[]{:S(2)}) async-start(bf16[8,256,128]{2,1,0:T(8,128)(2,1)} %get-tuple-element.49), calls=%async_computation.2 | async-start | bytes 1048576 | tf_op jit(solution)/shard_map/all_to_all | solution.py:401
  57.8 5.6 %collective-permute-start.17 = (bf16[16,8,2048]{2,1,0:T(8,128)(2,1)S(1)}, bf16[16,8,2048]{2,1,0:T(8,128)(2,1)S(1)}, u32[]{:S(2)}, u32[]{:S(2)}) collective-permute-start(bf16[16,8,2048]{2,1,0:T(8,128)(2,1)S(1)} %bitcast.30), channel_id=1, source_target_pairs={{0,1},{1,0},{2,3},{3,2},{4,5},{5,4},{6,7},{7,6},{8,9},{9,8},{10,11... | collective-permute-start | bytes 1572872 | tf_op jit(solution)/shard_map/ppermute | solution.py:395
  63.5 3.0 %collective-permute-start.6 = (bf16[64,2048]{1,0:T(8,128)(2,1)S(1)}, bf16[64,2048]{1,0:T(8,128)(2,1)S(1)}, u32[]{:S(2)}, u32[]{:S(2)}) collective-permute-start(bf16[64,2048]{1,0:T(8,128)(2,1)S(1)} %slice.8), channel_id=1, source_target_pairs={{32,0},{64,32},{96,64},{128,96},{160,128},{192,160},{224,192},{0,2... | collective-permute-start | bytes 786440 | tf_op jit(solution)/shard_map/ppermute | solution.py:332
  67.5 5.1 %shard_map.87._ = bf16[8,128,256]{2,1,0:T(8,128)(2,1)} custom-call(s32[4]{0:T(128)S(1)} %pad_add_fusion.place, bf16[128,2048]{1,0:T(8,128)(2,1)} %bitcast.34, bf16[128,2048]{1,0:T(8,128)(2,1)} %copy-done.3, bf16[128,2048]{1,0:T(8,128)(2,1)} %collective-permute-done.4.refs_2_, bf16[128,2048]{1,0:T(8,128)(2,1)} %copy-done.1, bf16[128,2048]{1,0:T(8,128)(2,1)} %copy-done.2, ...), custom_call_target="tpu_custom_call" | custom-call | tf_op jit(solution)/shard_map/pallas_call | solution.py:407
  72.6 2.6 %collective-permute-done.6.low_ref.refs_4_ = bf16[64,2048]{1,0:T(8,128)(2,1)S(1)} collective-permute-done((bf16[64,2048]{1,0:T(8,128)(2,1)S(1)}, bf16[64,2048]{1,0:T(8,128)(2,1)S(1)}, u32[]{:S(2)}, u32[]{:S(2)}) %collective-permute-start.6) | collective-permute-done | bytes 262176 | tf_op jit(solution)/shard_map/ppermute | solution.py:332
  75.2 3.3 %collective-permute-done.10.high_ref.refs_5_ = bf16[64,2048]{1,0:T(8,128)(2,1)S(1)} collective-permute-done((bf16[64,2048]{1,0:T(8,128)(2,1)}, bf16[64,2048]{1,0:T(8,128)(2,1)S(1)}, u32[]{:S(2)}, u32[]{:S(2)}) %collective-permute-start.10) | collective-permute-done | bytes 262176 | tf_op jit(solution)/shard_map/ppermute | solution.py:332
  79.2 2.7 %shard_map.88 = bf16[8,128,256]{2,1,0:T(8,128)(2,1)} custom-call(s32[4]{0:T(128)S(1)} %pad_add_fusion.place, bf16[64,2048]{1,0:T(8,128)(2,1)} %copy-done.6, bf16[64,2048]{1,0:T(8,128)(2,1)} %copy-done.7, bf16[256,2048]{1,0:T(8,128)(2,1)S(1)} %bitcast.29, bf16[8,128,256]{2,1,0:T(8,128)(2,1)} %shard_map.87._), custom_call_target="tpu_custom_call", output_to_operand_aliasing={{}: (4, {})} | custom-call | tf_op jit(solution)/shard_map/pallas_call | solution.py:417
  81.9 3.7 %all-to-all-start.3 = ((bf16[8,128,256]{2,1,0:T(8,128)(2,1)}), bf16[8,128,256]{2,1,0:T(8,128)(2,1)S(1)}, u32[]{:S(2)}, u32[]{:S(2)}) async-start(bf16[8,128,256]{2,1,0:T(8,128)(2,1)} %shard_map.88), calls=%async_computation.3 | async-start | bytes 1048576 | tf_op jit(solution)/shard_map/all_to_all | solution.py:432
  88.7 6.3 %shard_map.89 = (f32[256,1024]{1,0:T(8,128)}, f32[256,1024]{1,0:T(8,128)}) custom-call(s32[4]{0:T(128)S(1)} %pad_add_fusion.place, bf16[8,256,128]{2,1,0:T(8,128)(2,1)S(1)} %all-to-all-done.2.mine_ref, bf16[8,256,128]{2,1,0:T(8,128)(2,1)S(1)} %collective-permute-done.18.other_ref, bf16[128,2048]{1,0:T(8,128)(2,1)} %bitcast.35, bf16[128,2048]{1,0:T(8,128)(2,1)} %copy-done.3, ...), custom_call_target="tpu_custom_call" | custom-call | tf_op jit(solution)/shard_map/pallas_call | solution.py:438
  95.0 6.6 %all-to-all-done.3.grad_ref = bf16[8,128,256]{2,1,0:T(8,128)(2,1)S(1)} async-done(((bf16[8,128,256]{2,1,0:T(8,128)(2,1)}), bf16[8,128,256]{2,1,0:T(8,128)(2,1)S(1)}, u32[]{:S(2)}, u32[]{:S(2)}) %all-to-all-start.3) | async-done | bytes 524320 | tf_op jit(solution)/shard_map/all_to_all | solution.py:432
  101.5 2.4 %collective-permute-start.19 = (bf16[8,128,256]{2,1,0:T(8,128)(2,1)S(1)}, bf16[8,128,256]{2,1,0:T(8,128)(2,1)S(1)}, u32[]{:S(2)}, u32[]{:S(2)}) collective-permute-start(bf16[8,128,256]{2,1,0:T(8,128)(2,1)S(1)} %all-to-all-done.3.grad_ref), channel_id=1, source_target_pairs={{0,1},{1,0},{2,3},{3,2},{4,5},{5,4},{6,7},{7,6},{8,9},{9,8},{10,11... | collective-permute-start | bytes 1572872 | tf_op jit(solution)/shard_map/ppermute | solution.py:449
  106.2 4.0 %shard_map.90 = (f32[8,2,128,128]{3,2,1,0:T(8,128)}, f32[8,2,128,128]{3,2,1,0:T(8,128)}, f32[16,72,128]{2,1,0:T(8,128)}, f32[16,72,128]{2,1,0:T(8,128)}) custom-call(s32[4]{0:T(128)S(1)} %pad_add_fusion.place, bf16[8,2,128,128]{3,2,1,0:T(8,128)(2,1)} %get-tuple-element.44.queries, f32[8,2,128,128]{3,2,1,0:T(8,128)} %get-tuple-element.46.o_ref, ...), custom_call_target="tpu_custom_call" | custom-call | tf_op jit(solution)/shard_map/pallas_call | solution.py:453
  110.2 15.3 %all_to_all.35.in_ref = f32[16,72,128]{2,1,0:T(8,128)S(1)} all-to-all(f32[16,72,128]{2,1,0:T(8,128)} %get-tuple-element.60), channel_id=1, replica_groups=mesh['z'=8,'x'=4,'y'=4,'c'=2] {'x','y'}, dimensions={0} | all-to-all | bytes 1179648 | tf_op jit(solution)/shard_map/all_to_all | solution.py:464
  126.9 3.6 %all-to-all-start.5 = ((f32[16,72,128]{2,1,0:T(8,128)}), f32[16,72,128]{2,1,0:T(8,128)S(1)}, u32[]{:S(2)}, u32[]{:S(2)}) async-start(f32[16,72,128]{2,1,0:T(8,128)} %shard_map.91), calls=%async_computation.5 | async-start | bytes 1179648 | tf_op jit(solution)/shard_map/all_to_all | solution.py:471
  131.4 9.6 %all-to-all-done.5.later_ref = f32[16,72,128]{2,1,0:T(8,128)S(1)} async-done(((f32[16,72,128]{2,1,0:T(8,128)}), f32[16,72,128]{2,1,0:T(8,128)S(1)}, u32[]{:S(2)}, u32[]{:S(2)}) %all-to-all-start.5) | async-done | bytes 589856 | tf_op jit(solution)/shard_map/all_to_all | solution.py:471
  141.0 3.7 %all-to-all-start.6 = ((bf16[16,16,1024]{2,1,0:T(8,128)(2,1)}), bf16[16,16,1024]{2,1,0:T(8,128)(2,1)S(1)}, u32[]{:S(2)}, u32[]{:S(2)}) async-start(bf16[16,16,1024]{2,1,0:T(8,128)(2,1)} %bitcast.18), calls=%async_computation.6 | async-start | bytes 1048576 | tf_op jit(solution)/shard_map/all_to_all | solution.py:474
  144.7 7.4 %shard_map.92 = (bf16[8,3,128,128]{3,2,1,0:T(8,128)(2,1)}, bf16[8,3,128,128]{3,2,1,0:T(8,128)(2,1)}) custom-call(s32[4]{0:T(128)S(1)} %pad_add_fusion.place, bf16[8,2,128,128]{3,2,1,0:T(8,128)(2,1)} %get-tuple-element.44.queries, bf16[8,2,128,128]{3,2,1,0:T(8,128)(2,1)} %get-tuple-element.40.keys, bf16[8,2,128,128]{3,2,1,0:T(8,128)(2,1)} %get-tuple-element.41.values, ...), custom_call_target="tpu_custom_call" | custom-call | tf_op jit(solution)/shard_map/pallas_call | solution.py:476
  153.9 3.3 %collective-permute-start.21 = (bf16[8,3,128,128]{3,2,1,0:T(8,128)(2,1)}, bf16[8,3,128,128]{3,2,1,0:T(8,128)(2,1)S(1)}, u32[]{:S(2)}, u32[]{:S(2)}) collective-permute-start(bf16[8,3,128,128]{3,2,1,0:T(8,128)(2,1)} %get-tuple-element.68), channel_id=1, source_target_pairs={{0,1},{1,0},{2,3},{3,2},{4,5},{5,4},{6,7},{7,6},{8,9},{9,8},{10,11... | collective-permute-start | bytes 2359304 | tf_op jit(solution)/shard_map/ppermute | solution.py:490
  160.7 3.3 %shard_map.94 = (bf16[128,2048]{1,0:T(8,128)(2,1)}, bf16[128,2048]{1,0:T(8,128)(2,1)}, bf16[128,2048]{1,0:T(8,128)(2,1)}, f32[8,2048]{1,0:T(8,128)}) custom-call(s32[4]{0:T(128)S(1)} %pad_add_fusion.place, bf16[8,3,128,128]{3,2,1,0:T(8,128)(2,1)} %get-tuple-element.65.keep_ref, bf16[8,3,128,128]{3,2,1,0:T(8,128)(2,1)S(1)} %collective-permute-done.21.back_ref, ...), custom_call_target="tpu_custom_call" | custom-call | tf_op jit(solution)/shard_map/pallas_call | solution.py:498
  (71 shorter events, 19.8 us)
Async XLA Ops:
  0.6 7.4 %collective-permute-start.1 = (bf16[128,2048]{1,0:T(8,128)(2,1)}, bf16[128,2048]{1,0:T(8,128)(2,1)S(1)}, u32[]{:S(2)}, u32[]{:S(2)}) collective-permute-start(bf16[128,2048]{1,0:T(8,128)(2,1)} %bitcast.36), channel_id=1, source_target_pairs={{0,1},{1,0},{2,3},{3,2},{4,5},{5,4},{6,7},{7,6},{8,9},{9,8},{10,11... | collective-permute-start | bytes 1572872 | tf_op jit(solution)/shard_map/ppermute | solution.py:334
  4.0 4.0 %collective-permute-start.2 = (bf16[128,2048]{1,0:T(8,128)(2,1)}, bf16[128,2048]{1,0:T(8,128)(2,1)S(1)}, u32[]{:S(2)}, u32[]{:S(2)}) collective-permute-start(bf16[128,2048]{1,0:T(8,128)(2,1)} %bitcast.38), channel_id=1, source_target_pairs={{0,1},{1,0},{2,3},{3,2},{4,5},{5,4},{6,7},{7,6},{8,9},{9,8},{10,11... | collective-permute-start | bytes 1572872 | tf_op jit(solution)/shard_map/ppermute | solution.py:334
  4.1 18.3 %collective-permute-start.3 = (bf16[128,2048]{1,0:T(8,128)(2,1)}, bf16[128,2048]{1,0:T(8,128)(2,1)S(1)}, u32[]{:S(2)}, u32[]{:S(2)}) collective-permute-start(bf16[128,2048]{1,0:T(8,128)(2,1)} %bitcast.32), channel_id=1, source_target_pairs={{32,0},{64,32},{96,64},{128,96},{160,128},{192,160},{224,192},{0,2... | collective-permute-start | bytes 1572872 | tf_op jit(solution)/shard_map/ppermute | solution.py:332
  7.9 14.7 %collective-permute-start.7 = (bf16[128,2048]{1,0:T(8,128)(2,1)}, bf16[128,2048]{1,0:T(8,128)(2,1)S(1)}, u32[]{:S(2)}, u32[]{:S(2)}) collective-permute-start(bf16[128,2048]{1,0:T(8,128)(2,1)} %bitcast.33), channel_id=1, source_target_pairs={{224,0},{0,32},{32,64},{64,96},{96,128},{128,160},{160,192},{192,2... | collective-permute-start | bytes 1572872 | tf_op jit(solution)/shard_map/ppermute | solution.py:332
  8.0 6.2 %copy-start.8 = (bf16[1,128,2048]{2,1,0:T(8,128)(2,1)S(1)}, bf16[1,128,2048]{2,1,0:T(8,128)(2,1)}, u32[]{:S(2)}) copy-start(bf16[1,128,2048]{2,1,0:T(8,128)(2,1)} %param.5) | copy-start | bytes 1572868
  11.4 14.2 %collective-permute-start.11 = (bf16[8,2048]{1,0:T(8,128)(2,1)S(1)}, bf16[8,2048]{1,0:T(8,128)(2,1)S(1)}, u32[]{:S(2)}, u32[]{:S(2)}) collective-permute-start(bf16[8,2048]{1,0:T(8,128)(2,1)S(1)} %copy-done.9), channel_id=1, source_target_pairs={{2,0},{4,2},{6,4},{0,6},{3,1},{5,3},{7,5},{1,7},{10,8},{12,10},{14... | collective-permute-start | bytes 98312 | tf_op jit(solution)/shard_map/ppermute | solution.py:332
  14.2 25.7 %collective-permute-start = (bf16[128,2048]{1,0:T(8,128)(2,1)S(1)}, bf16[128,2048]{1,0:T(8,128)(2,1)S(1)}, u32[]{:S(2)}, u32[]{:S(2)}) collective-permute-start(bf16[128,2048]{1,0:T(8,128)(2,1)S(1)} %bitcast.42), channel_id=1, source_target_pairs={{0,1},{1,0},{2,3},{3,2},{4,5},{5,4},{6,7},{7,6},{8,9},{9,8},{10,11... | collective-permute-start | bytes 1572872 | tf_op jit(solution)/shard_map/ppermute | solution.py:334
  15.1 15.1 %all-to-all-start = ((f32[16,72,128]{2,1,0:T(8,128)}), f32[16,72,128]{2,1,0:T(8,128)S(1)}, u32[]{:S(2)}, u32[]{:S(2)}) async-start(f32[16,72,128]{2,1,0:T(8,128)} %get-tuple-element.42), calls=%async_computation | async-start | bytes 1179648 | tf_op jit(solution)/shard_map/all_to_all | solution.py:378
  19.5 6.2 %collective-permute-start.12 = (bf16[8,2048]{1,0:T(8,128)(2,1)S(1)}, bf16[8,2048]{1,0:T(8,128)(2,1)S(1)}, u32[]{:S(2)}, u32[]{:S(2)}) collective-permute-start(bf16[8,2048]{1,0:T(8,128)(2,1)S(1)} %copy-done.9), channel_id=1, source_target_pairs={{4,0},{6,2},{0,4},{2,6},{5,1},{7,3},{1,5},{3,7},{12,8},{14,10},{8,... | collective-permute-start | bytes 98312 | tf_op jit(solution)/shard_map/ppermute | solution.py:332
  22.3 9.3 %copy-start.3 = (bf16[128,2048]{1,0:T(8,128)(2,1)}, bf16[128,2048]{1,0:T(8,128)(2,1)S(1)}, u32[]{:S(2)}) copy-start(bf16[128,2048]{1,0:T(8,128)(2,1)S(1)} %collective-permute-done.3.refs_1_) | copy-start | bytes 1572868
  22.3 14.3 %collective-permute-start.13 = (bf16[8,2048]{1,0:T(8,128)(2,1)S(1)}, bf16[8,2048]{1,0:T(8,128)(2,1)S(1)}, u32[]{:S(2)}, u32[]{:S(2)}) collective-permute-start(bf16[8,2048]{1,0:T(8,128)(2,1)S(1)} %copy-done.9), channel_id=1, source_target_pairs={{6,0},{0,2},{2,4},{4,6},{7,1},{1,3},{3,5},{5,7},{14,8},{8,10},{10,... | collective-permute-start | bytes 98312 | tf_op jit(solution)/shard_map/ppermute | solution.py:332
  22.6 9.0 %copy-start.4 = (bf16[128,2048]{1,0:T(8,128)(2,1)}, bf16[128,2048]{1,0:T(8,128)(2,1)S(1)}, u32[]{:S(2)}) copy-start(bf16[128,2048]{1,0:T(8,128)(2,1)S(1)} %collective-permute-done.7.refs_6_.refs_8_) | copy-start | bytes 1572868
  22.6 17.8 %collective-permute-start.4 = (bf16[128,2048]{1,0:T(8,128)(2,1)S(1)}, bf16[128,2048]{1,0:T(8,128)(2,1)}, u32[]{:S(2)}, u32[]{:S(2)}) collective-permute-start(bf16[128,2048]{1,0:T(8,128)(2,1)S(1)} %collective-permute-done.3.refs_1_), channel_id=1, source_target_pairs={{32,0},{64,32},{96,64},{128,96},{160,128},{192,160},{224,192},{0,2... | collective-permute-start | bytes 1572872 | tf_op jit(solution)/shard_map/ppermute | solution.py:332
  25.6 17.8 %collective-permute-start.8 = (bf16[128,2048]{1,0:T(8,128)(2,1)S(1)}, bf16[128,2048]{1,0:T(8,128)(2,1)}, u32[]{:S(2)}, u32[]{:S(2)}) collective-permute-start(bf16[128,2048]{1,0:T(8,128)(2,1)S(1)} %collective-permute-done.7.refs_6_.refs_8_), channel_id=1, source_target_pairs={{224,0},{0,32},{32,64},{64,96},{96,128},{128,160},{160,192},{192,2... | collective-permute-start | bytes 1572872 | tf_op jit(solution)/shard_map/ppermute | solution.py:332
  31.6 15.6 %all-to-all-start.1 = ((f32[16,72,128]{2,1,0:T(8,128)}), f32[16,72,128]{2,1,0:T(8,128)S(1)}, u32[]{:S(2)}, u32[]{:S(2)}) async-start(f32[16,72,128]{2,1,0:T(8,128)} %shard_map.85), calls=%async_computation.1 | async-start | bytes 1179648 | tf_op jit(solution)/shard_map/all_to_all | solution.py:385
  36.6 20.1 %collective-permute-start.14 = (bf16[4,8,2048]{2,1,0:T(8,128)(2,1)S(1)}, bf16[4,8,2048]{2,1,0:T(8,128)(2,1)S(1)}, u32[]{:S(2)}, u32[]{:S(2)}) collective-permute-start(bf16[4,8,2048]{2,1,0:T(8,128)(2,1)S(1)} %bitcast_dynamic-update-slice_fusion.3), channel_id=1, source_target_pairs={{8,0},{16,8},{24,16},{0,24},{9,1},{17,9},{25,17},{1,25},{10,2},{18... | collective-permute-start | bytes 393224 | tf_op jit(solution)/shard_map/ppermute | solution.py:332
  39.3 17.5 %collective-permute-start.15 = (bf16[4,8,2048]{2,1,0:T(8,128)(2,1)S(1)}, bf16[4,8,2048]{2,1,0:T(8,128)(2,1)}, u32[]{:S(2)}, u32[]{:S(2)}) collective-permute-start(bf16[4,8,2048]{2,1,0:T(8,128)(2,1)S(1)} %bitcast_dynamic-update-slice_fusion.3), channel_id=1, source_target_pairs={{16,0},{24,8},{0,16},{8,24},{17,1},{25,9},{1,17},{9,25},{18,2},{26... | collective-permute-start | bytes 393224 | tf_op jit(solution)/shard_map/ppermute | solution.py:332
  39.9 16.9 %collective-permute-start.16 = (bf16[4,8,2048]{2,1,0:T(8,128)(2,1)S(1)}, bf16[4,8,2048]{2,1,0:T(8,128)(2,1)S(1)}, u32[]{:S(2)}, u32[]{:S(2)}) collective-permute-start(bf16[4,8,2048]{2,1,0:T(8,128)(2,1)S(1)} %bitcast_dynamic-update-slice_fusion.3), channel_id=1, source_target_pairs={{24,0},{0,8},{8,16},{16,24},{25,1},{1,9},{9,17},{17,25},{26,2},{2,... | collective-permute-start | bytes 393224 | tf_op jit(solution)/shard_map/ppermute | solution.py:332
  40.5 23.0 %collective-permute-start.5 = (bf16[128,2048]{1,0:T(8,128)(2,1)}, bf16[128,2048]{1,0:T(8,128)(2,1)S(1)}, u32[]{:S(2)}, u32[]{:S(2)}) collective-permute-start(bf16[128,2048]{1,0:T(8,128)(2,1)} %collective-permute-done.4.refs_2_), channel_id=1, source_target_pairs={{32,0},{64,32},{96,64},{128,96},{160,128},{192,160},{224,192},{0,2... | collective-permute-start | bytes 1572872 | tf_op jit(solution)/shard_map/ppermute | solution.py:332
  43.4 23.1 %collective-permute-start.9 = (bf16[128,2048]{1,0:T(8,128)(2,1)}, bf16[128,2048]{1,0:T(8,128)(2,1)S(1)}, u32[]{:S(2)}, u32[]{:S(2)}) collective-permute-start(bf16[128,2048]{1,0:T(8,128)(2,1)} %collective-permute-done.8.refs_5_.refs_7_), channel_id=1, source_target_pairs={{224,0},{0,32},{32,64},{64,96},{96,128},{128,160},{160,192},{192,2... | collective-permute-start | bytes 1572872 | tf_op jit(solution)/shard_map/ppermute | solution.py:332
  52.2 29.7 %all-to-all-start.2 = ((bf16[8,256,128]{2,1,0:T(8,128)(2,1)}), bf16[8,256,128]{2,1,0:T(8,128)(2,1)S(1)}, u32[]{:S(2)}, u32[]{:S(2)}) async-start(bf16[8,256,128]{2,1,0:T(8,128)(2,1)} %get-tuple-element.49), calls=%async_computation.2 | async-start | bytes 1048576 | tf_op jit(solution)/shard_map/all_to_all | solution.py:401
  57.8 9.5 %collective-permute-start.17 = (bf16[16,8,2048]{2,1,0:T(8,128)(2,1)S(1)}, bf16[16,8,2048]{2,1,0:T(8,128)(2,1)S(1)}, u32[]{:S(2)}, u32[]{:S(2)}) collective-permute-start(bf16[16,8,2048]{2,1,0:T(8,128)(2,1)S(1)} %bitcast.30), channel_id=1, source_target_pairs={{0,1},{1,0},{2,3},{3,2},{4,5},{5,4},{6,7},{7,6},{8,9},{9,8},{10,11... | collective-permute-start | bytes 1572872 | tf_op jit(solution)/shard_map/ppermute | solution.py:395
  63.5 11.7 %collective-permute-start.6 = (bf16[64,2048]{1,0:T(8,128)(2,1)S(1)}, bf16[64,2048]{1,0:T(8,128)(2,1)S(1)}, u32[]{:S(2)}, u32[]{:S(2)}) collective-permute-start(bf16[64,2048]{1,0:T(8,128)(2,1)S(1)} %slice.8), channel_id=1, source_target_pairs={{32,0},{64,32},{96,64},{128,96},{160,128},{192,160},{224,192},{0,2... | collective-permute-start | bytes 786440 | tf_op jit(solution)/shard_map/ppermute | solution.py:332
  67.3 11.2 %collective-permute-start.10 = (bf16[64,2048]{1,0:T(8,128)(2,1)}, bf16[64,2048]{1,0:T(8,128)(2,1)S(1)}, u32[]{:S(2)}, u32[]{:S(2)}) collective-permute-start(bf16[64,2048]{1,0:T(8,128)(2,1)} %slice.9), channel_id=1, source_target_pairs={{224,0},{0,32},{32,64},{64,96},{96,128},{128,160},{160,192},{192,2... | collective-permute-start | bytes 786440 | tf_op jit(solution)/shard_map/ppermute | solution.py:332
  81.9 19.7 %all-to-all-start.3 = ((bf16[8,128,256]{2,1,0:T(8,128)(2,1)}), bf16[8,128,256]{2,1,0:T(8,128)(2,1)S(1)}, u32[]{:S(2)}, u32[]{:S(2)}) async-start(bf16[8,128,256]{2,1,0:T(8,128)(2,1)} %shard_map.88), calls=%async_computation.3 | async-start | bytes 1048576 | tf_op jit(solution)/shard_map/all_to_all | solution.py:432
  85.5 3.2 %collective-permute-start.18 = (bf16[8,256,128]{2,1,0:T(8,128)(2,1)S(1)}, bf16[8,256,128]{2,1,0:T(8,128)(2,1)S(1)}, u32[]{:S(2)}, u32[]{:S(2)}) collective-permute-start(bf16[8,256,128]{2,1,0:T(8,128)(2,1)S(1)} %all-to-all-done.2.mine_ref), channel_id=1, source_target_pairs={{0,1},{1,0},{2,3},{3,2},{4,5},{5,4},{6,7},{7,6},{8,9},{9,8},{10,11... | collective-permute-start | bytes 1572872 | tf_op jit(solution)/shard_map/ppermute | solution.py:402
  101.5 4.7 %collective-permute-start.19 = (bf16[8,128,256]{2,1,0:T(8,128)(2,1)S(1)}, bf16[8,128,256]{2,1,0:T(8,128)(2,1)S(1)}, u32[]{:S(2)}, u32[]{:S(2)}) collective-permute-start(bf16[8,128,256]{2,1,0:T(8,128)(2,1)S(1)} %all-to-all-done.3.grad_ref), channel_id=1, source_target_pairs={{0,1},{1,0},{2,3},{3,2},{4,5},{5,4},{6,7},{7,6},{8,9},{9,8},{10,11... | collective-permute-start | bytes 1572872 | tf_op jit(solution)/shard_map/ppermute | solution.py:449
  104.0 26.5 %collective-permute-start.20 = (f32[256,1024]{1,0:T(8,128)}, f32[256,1024]{1,0:T(8,128)S(1)}, u32[]{:S(2)}, u32[]{:S(2)}) collective-permute-start(f32[256,1024]{1,0:T(8,128)} %get-tuple-element.62), channel_id=1, source_target_pairs={{0,1},{1,0},{2,3},{3,2},{4,5},{5,4},{6,7},{7,6},{8,9},{9,8},{10,11... | collective-permute-start | bytes 3145736 | tf_op jit(solution)/shard_map/ppermute | solution.py:450
  126.9 14.1 %all-to-all-start.5 = ((f32[16,72,128]{2,1,0:T(8,128)}), f32[16,72,128]{2,1,0:T(8,128)S(1)}, u32[]{:S(2)}, u32[]{:S(2)}) async-start(f32[16,72,128]{2,1,0:T(8,128)} %shard_map.91), calls=%async_computation.5 | async-start | bytes 1179648 | tf_op jit(solution)/shard_map/all_to_all | solution.py:471
  141.0 13.0 %all-to-all-start.6 = ((bf16[16,16,1024]{2,1,0:T(8,128)(2,1)}), bf16[16,16,1024]{2,1,0:T(8,128)(2,1)S(1)}, u32[]{:S(2)}, u32[]{:S(2)}) async-start(bf16[16,16,1024]{2,1,0:T(8,128)(2,1)} %bitcast.18), calls=%async_computation.6 | async-start | bytes 1048576 | tf_op jit(solution)/shard_map/all_to_all | solution.py:474
  153.9 5.9 %collective-permute-start.21 = (bf16[8,3,128,128]{3,2,1,0:T(8,128)(2,1)}, bf16[8,3,128,128]{3,2,1,0:T(8,128)(2,1)S(1)}, u32[]{:S(2)}, u32[]{:S(2)}) collective-permute-start(bf16[8,3,128,128]{3,2,1,0:T(8,128)(2,1)} %get-tuple-element.68), channel_id=1, source_target_pairs={{0,1},{1,0},{2,3},{3,2},{4,5},{5,4},{6,7},{7,6},{8,9},{9,8},{10,11... | collective-permute-start | bytes 2359304 | tf_op jit(solution)/shard_map/ppermute | solution.py:490
  158.5 1.4 collective-permute-start.22
  (7 other events, 18.0 us)
